TPU v7x, 32 devices: a whole 2x2x4 slice. The times are simulated.
32 devices in a mesh: seq: 16 (over z, y, x), head: 2 (over core).
Axes of the slice: x: 2, y: 2, z: 4, core: 2. Of those that a mesh axis runs over, the one named last changes fastest.
Arguments:
- ssm_input: bfloat16 [8192, 3072], P('seq', 'head'), may hold values from -125 to 125
- input_map: bfloat16 [8192, 1024], P('seq', 'head'), may hold values from -0.4375 to 0.4375
- output_map: bfloat16 [8192, 1024], P('seq', 'head'), may hold values from -0.4375 to 0.4375
- decay_forward: bfloat16 [48, 8192], P('head', 'seq'), may hold values from -2 to 0
- decay_reverse: bfloat16 [48, 8192], P('head', 'seq'), may hold values from -2 to 0
- skip_gain: float32 [48], P('head'), may hold values from 0.2 to 1
- norm_gain: float32 [3072], P('head'), may hold values from 0.5 to 1.5
- scan_order: int32 [256], P('seq'), may hold values from 0 to 255, as said below
- raster_order: int32 [256], P('seq'), may hold values from 0 to 255, as said below
- grad_normed: bfloat16 [8192, 3072], P('seq', 'head'), may hold values from -6 to 6
Outputs:
- normed_output: bfloat16 [8192, 3072], P('seq', 'head')
- grad_input: bfloat16 [8192, 3072], P('seq', 'head')
Inputs may be any that keep to these rules, and one draw needn't show every extreme that they name: scan_order is a permutation of the units; the units held by any index of seq, as positions 16 * e to 16 * e + 15, come one from every index of seq. raster_order is the inverse of scan_order.
All inputs are finite; a program needn't handle non-finite values.
Results may differ from a plain program's by a relative error of at most 0.011.
Values may be sent and summed in bfloat16 or wider, within the bound.
A program may use at most 128 MiB of HBM per device.

v0:
```python
import jax
import jax.numpy as jnp
from jax import lax
from jax.sharding import PartitionSpec as P

HEAD_DIM = 64
STATE = 128
SPAN = 256
FEATURES = 3072


EPSILON = 1e-05


def passed_along(block, axis, distance):
    devices = range(lax.axis_size(axis))
    route = [(i - distance, i) for i in devices if i - distance in devices]
    return lax.ppermute(block, axis, route)


def combine(earlier, latter):
    return (earlier[0] + latter[0], jnp.exp(latter[0])[..., None, None] * earlier[1] + latter[1])


def carried(device_sum, reverse):
    direction = -1 if reverse else 1
    shifted = passed_along((device_sum[0], device_sum[1]), "seq", direction)
    for bit_index in range(lax.axis_size("seq").bit_length() - 1):
        arrived = passed_along((shifted[0], shifted[1]), "seq", direction * (1 << bit_index))
        shifted = combine(arrived, shifted)
    return shifted


def scan_block(values, key_rows, query_rows, log_decay, reverse):
    tok_rows = values.shape[0]
    head_count = log_decay.shape[0]
    head_width = values.shape[1] // head_count
    group_count = key_rows.shape[1] // STATE
    per_group = head_count // group_count
    span_count = tok_rows // SPAN
    value_blocks = values.reshape(span_count, SPAN, group_count, per_group, head_width)
    key_blocks = key_rows.reshape(span_count, SPAN, group_count, STATE)
    query_blocks = query_rows.reshape(span_count, SPAN, group_count, STATE)
    cumulative = jnp.cumsum(
        log_decay.astype(jnp.float32).reshape(group_count, per_group, span_count, SPAN), axis=3
    )
    scores = jnp.einsum(
        "cign,cjgn->gcij", query_blocks, key_blocks, preferred_element_type=jnp.float32
    )
    spread = cumulative[..., :, None] - cumulative[..., None, :]
    row_ids = lax.broadcasted_iota(jnp.int32, (SPAN, SPAN), 0)
    col_ids = lax.broadcasted_iota(jnp.int32, (SPAN, SPAN), 1)
    span_end = cumulative[..., -1]
    if reverse:
        allowed = col_ids >= row_ids
        damping = jnp.exp(jnp.minimum(-spread, 0.0))
        key_weight = jnp.exp(cumulative)
        query_weight = jnp.exp(span_end[..., None] - cumulative)
    else:
        allowed = col_ids <= row_ids
        damping = jnp.exp(jnp.minimum(spread, 0.0))
        key_weight = jnp.exp(span_end[..., None] - cumulative)
        query_weight = jnp.exp(cumulative)
    weights = jnp.where(allowed, scores[:, None] * damping, 0.0).astype(jnp.bfloat16)
    inner_part = jnp.einsum(
        "ghcij,cjghp->cighp", weights, value_blocks, preferred_element_type=jnp.float32
    )
    scaled_keys = (jnp.transpose(key_blocks, (2, 0, 1, 3))[:, None] * key_weight[..., None]).astype(
        jnp.bfloat16
    )
    span_states = jnp.einsum(
        "ghcjn,cjghp->ghcnp", scaled_keys, value_blocks, preferred_element_type=jnp.float32
    )
    visit_order = list(range(span_count))
    if reverse:
        visit_order = visit_order[::-1]
    running = (jnp.zeros_like(span_end[..., 0]), jnp.zeros_like(span_states[:, :, 0]))
    preceding = [running] * span_count
    for position in visit_order:
        preceding[position] = running
        running = combine(running, (span_end[..., position], span_states[:, :, position]))
    incoming = carried(running, reverse)
    entering = jnp.stack(
        [piece[1] + jnp.exp(piece[0])[..., None, None] * incoming[1] for piece in preceding], axis=2
    )
    entering = entering.astype(jnp.bfloat16)
    outer_part = jnp.einsum(
        "cign,ghcnp->cighp", query_blocks, entering, preferred_element_type=jnp.float32
    )
    outer_part = outer_part * jnp.transpose(query_weight, (2, 3, 0, 1))[..., None]
    return (inner_part + outer_part).reshape(tok_rows, head_count * head_width)


def reorder(array, send_index, recv_index):
    outgoing = jnp.take(array, send_index, axis=0)
    arrived = lax.all_to_all(outgoing, "seq", split_axis=0, concat_axis=0, tiled=True)
    return jnp.take(arrived, recv_index, axis=0)


def shards(
    ssm_input,
    input_map,
    output_map,
    decay_forward,
    decay_reverse,
    skip_gain,
    norm_gain,
    scan_order,
    raster_order,
    grad_normed,
):
    unit_count = scan_order.shape[0]
    tok_rows = ssm_input.shape[0]
    unit_rows = tok_rows // unit_count
    head_width = ssm_input.shape[1]
    state_width = input_map.shape[1]
    raster_dest = raster_order // unit_count
    scan_source = scan_order // unit_count
    send_scan = jnp.argsort(raster_dest, stable=True)
    send_raster = jnp.argsort(scan_source, stable=True)

    def to_scan(array):
        return reorder(array.reshape(unit_count, unit_rows, -1), send_scan, scan_source).reshape(
            tok_rows, -1
        )

    def to_raster(array):
        return reorder(array.reshape(unit_count, unit_rows, -1), send_raster, raster_dest).reshape(
            tok_rows, -1
        )

    joined = jnp.concatenate([ssm_input, input_map, output_map], axis=1)
    joined_scan = to_scan(joined)
    values_scan = joined_scan[:, :head_width]
    in_map_scan = joined_scan[:, head_width : head_width + state_width]
    out_map_scan = joined_scan[:, head_width + state_width :]
    y_forward = scan_block(ssm_input, input_map, output_map, decay_forward, False).astype(
        jnp.bfloat16
    )
    y_reverse = to_raster(
        scan_block(values_scan, in_map_scan, out_map_scan, decay_reverse, True).astype(jnp.bfloat16)
    )
    skip_cols = jnp.repeat(skip_gain, HEAD_DIM)
    combined = (
        y_forward.astype(jnp.float32)
        + y_reverse.astype(jnp.float32)
        + skip_cols * ssm_input.astype(jnp.float32)
    )
    squares = lax.psum(jnp.sum(combined * combined, axis=1), "head")
    inv_rms = lax.rsqrt(squares / FEATURES + EPSILON)
    normed_output = (combined * inv_rms[:, None] * norm_gain).astype(jnp.bfloat16)
    scaled_grad = norm_gain * grad_normed.astype(jnp.float32)
    inner_sum = lax.psum(jnp.sum(combined * scaled_grad, axis=1), "head")
    grad_combined = (
        inv_rms[:, None] * scaled_grad - combined * (inv_rms**3 * inner_sum / FEATURES)[:, None]
    )
    grad_combined = grad_combined.astype(jnp.bfloat16)
    grad_forward = scan_block(grad_combined, output_map, input_map, decay_forward, True).astype(
        jnp.bfloat16
    )
    grad_scan = scan_block(
        to_scan(grad_combined), out_map_scan, in_map_scan, decay_reverse, False
    ).astype(jnp.bfloat16)
    grad_reverse = to_raster(grad_scan)
    grad_input = (
        grad_forward.astype(jnp.float32)
        + grad_reverse.astype(jnp.float32)
        + skip_cols * grad_combined.astype(jnp.float32)
    )
    return (normed_output, grad_input.astype(jnp.bfloat16))


def solution(mesh):
    return jax.shard_map(
        shards,
        mesh=mesh,
        in_specs=(
            P("seq", "head"),
            P("seq", "head"),
            P("seq", "head"),
            P("head", "seq"),
            P("head", "seq"),
            P("head"),
            P("head"),
            P("seq"),
            P("seq"),
            P("seq", "head"),
        ),
        out_specs=(P("seq", "head"), P("seq", "head")),
        check_vma=False,
    )
```

profile of v0, /device:TPU:12, one launch (start us, length us, event | category | flops | bytes accessed | tf_op | source)
XLA Modules:
  0.0 733.5 jit_solution(14580029138867898096)
XLA Ops:
  7.3 3.5 broadcast_select_fusion.1
  10.8 7.3 all-to-all-start
  18.2 14.5 %reduce-window.16 = f32[4,6,2,2,128]{4,3,2,1,0:T(2,128)S(1)} reduce-window(f32[4,6,2,2,128]{4,3,2,1,0:T(2,128)S(1)} %reshape.254, f32[]{:T(128)} %constant.51.clone.1), window={size=1x1x1x1x128 pad=0_0x0_0x0_0x0_0x127_0}, to_apply=%region_3.5 | reduce-window | flops 1560576 | bytes 98308 | tf_op jit(solution)/shard_map/reduce-window.2
  34.0 3.4 collective-permute-start.9
  38.2 14.5 %reduce-window.14 = f32[4,6,2,2,128]{4,3,2,1,0:T(2,128)S(1)} reduce-window(f32[4,6,2,2,128]{4,3,2,1,0:T(2,128)S(1)} %reshape.252, f32[]{:T(128)} %constant.51.clone.1), window={size=1x1x1x1x128 pad=0_0x0_0x0_0x0_0x127_0}, to_apply=%region_0.1 | reduce-window | flops 1560576 | bytes 98308 | tf_op jit(solution)/shard_map/reduce-window
  54.1 23.1 %all-to-all-done = bf16[16,32,2560]{2,1,0:T(8,128)(2,1)S(1)} async-done(((bf16[16,32,2560]{2,1,0:T(8,128)(2,1)}), bf16[16,32,2560]{2,1,0:T(8,128)(2,1)S(1)}, u32[]{:S(2)}, u32[]{:S(2)}) %all-to-all-start) | async-done | bytes 2621472 | tf_op jit(solution)/shard_map/all_to_all | solution.py:96
  88.8 5.9 fusion.47
  104.4 12.0 %collective-permute-done.13 = f32[4,6,128,64]{2,3,1,0:T(8,128)S(1)} collective-permute-done((f32[4,6,128,64]{2,3,1,0:T(8,128)}, f32[4,6,128,64]{2,3,1,0:T(8,128)S(1)}, u32[]{:S(2)}, u32[]{:S(2)}) %collective-permute-start.13) | collective-permute-done | bytes 786464 | tf_op jit(solution)/shard_map/ppermute | solution.py:18
  116.4 3.1 collective-permute-start.14
  119.5 4.2 fusion.46
  127.8 4.1 collective-permute-start.4
  131.9 22.5 %collective-permute-done.10 = f32[4,6]{1,0:T(4,128)S(1)} collective-permute-done((f32[4,6]{1,0:T(4,128)}, f32[4,6]{1,0:T(4,128)S(1)}, u32[]{:S(2)}, u32[]{:S(2)}) %collective-permute-start.10) | collective-permute-done | bytes 128 | tf_op jit(solution)/shard_map/ppermute | solution.py:18
  161.6 6.3 collective-permute-start.5
  170.5 19.7 %collective-permute-done.15 = f32[4,6,128,64]{2,3,1,0:T(8,128)} collective-permute-done((f32[4,6,128,64]{2,3,1,0:T(8,128)S(1)}, f32[4,6,128,64]{2,3,1,0:T(8,128)}, u32[]{:S(2)}, u32[]{:S(2)}) %collective-permute-start.15) | collective-permute-done | bytes 786464 | tf_op jit(solution)/shard_map/ppermute | solution.py:18
  194.6 5.9 collective-permute-start.6
  202.5 4.8 collective-permute-start.2
  207.4 4.5 collective-permute-done.11
  215.5 16.9 %collective-permute-done.12 = f32[4,6]{1,0:T(4,128)S(1)} collective-permute-done((f32[4,6]{1,0:T(4,128)S(1)}, f32[4,6]{1,0:T(4,128)S(1)}, u32[]{:S(2)}, u32[]{:S(2)}) %collective-permute-start.12) | collective-permute-done | bytes 128 | tf_op jit(solution)/shard_map/ppermute | solution.py:18
  241.7 4.1 fusion.53
  245.8 6.7 copy.133
  252.6 5.6 convert_element_type.136
  260.0 2.8 broadcast_select_fusion.7
  262.7 13.2 %all-to-all-start.1 = ((bf16[16,32,1536]{2,1,0:T(8,128)(2,1)}), bf16[16,32,1536]{2,1,0:T(8,128)(2,1)}, u32[]{:S(2)}, u32[]{:S(2)}) async-start(bf16[16,32,1536]{2,1,0:T(8,128)(2,1)} %broadcast_select_fusion.7), calls=%async_computation.1 | async-start | bytes 3145728 | tf_op jit(solution)/shard_map/all_to_all | solution.py:96
  278.4 5.2 collective-permute-start.8
  286.4 3.0 fusion.120
  291.6 51.1 %collective-permute-done.3 = f32[4,6]{1,0:T(4,128)S(1)} collective-permute-done((f32[4,6]{1,0:T(4,128)S(1)}, f32[4,6]{1,0:T(4,128)S(1)}, u32[]{:S(2)}, u32[]{:S(2)}) %collective-permute-start.3) | collective-permute-done | bytes 128 | tf_op jit(solution)/shard_map/ppermute | solution.py:18
  346.7 3.2 fusion.72
  354.3 3.2 gather_fusion.3
  361.3 3.6 copy.134
  364.9 4.6 multiply_reduce_fusion
  372.0 3.9 subtract_convert_fusion
  378.5 2.8 broadcast_select_fusion.3
  381.4 8.3 %all-to-all-start.2 = ((bf16[16,32,1536]{2,1,0:T(8,128)(2,1)}), bf16[16,32,1536]{2,1,0:T(8,128)(2,1)}, u32[]{:S(2)}, u32[]{:S(2)}) async-start(bf16[16,32,1536]{2,1,0:T(8,128)(2,1)} %broadcast_select_fusion.3), calls=%async_computation.2 | async-start | bytes 3145728 | tf_op jit(solution)/shard_map/all_to_all | solution.py:96
  389.9 37.0 %all-to-all-done.2 = bf16[16,32,1536]{2,1,0:T(8,128)(2,1)} async-done(((bf16[16,32,1536]{2,1,0:T(8,128)(2,1)}), bf16[16,32,1536]{2,1,0:T(8,128)(2,1)}, u32[]{:S(2)}, u32[]{:S(2)}) %all-to-all-start.2) | async-done | bytes 1572896 | tf_op jit(solution)/shard_map/all_to_all | solution.py:96
  426.9 3.3 gather_fusion.5
  433.0 6.5 reshape_reshape.3
  439.5 5.3 copy.150
  444.8 4.1 fusion.56
  449.0 3.1 collective-permute-start.31
  452.1 3.4 collective-permute-start.27
  456.7 13.8 %collective-permute-done.27 = f32[4,6]{1,0:T(4,128)S(1)} collective-permute-done((f32[4,6]{1,0:T(4,128)}, f32[4,6]{1,0:T(4,128)S(1)}, u32[]{:S(2)}, u32[]{:S(2)}) %collective-permute-start.27) | collective-permute-done | bytes 128 | tf_op jit(solution)/shard_map/ppermute | solution.py:18
  472.6 4.8 collective-permute-start.32
  479.4 4.2 fusion.58
  485.8 10.3 %collective-permute-done.32 = f32[4,6,128,64]{2,3,1,0:T(8,128)} collective-permute-done((f32[4,6,128,64]{2,3,1,0:T(8,128)S(1)}, f32[4,6,128,64]{2,3,1,0:T(8,128)}, u32[]{:S(2)}, u32[]{:S(2)}) %collective-permute-start.32) | collective-permute-done | bytes 786464 | tf_op jit(solution)/shard_map/ppermute | solution.py:18
  497.3 14.1 %collective-permute-start.33 = (f32[4,6,128,64]{2,3,1,0:T(8,128)S(1)}, f32[4,6,128,64]{2,3,1,0:T(8,128)S(1)}, u32[]{:S(2)}, u32[]{:S(2)}) collective-permute-start(f32[4,6,128,64]{2,3,1,0:T(8,128)S(1)} %multiply_add_fusion.4), channel_id=1, source_target_pairs={{0,4},{2,6},{4,8},{6,10},{8,12},{10,14},{12,16},{14,18},{16,20},{1... | collective-permute-start | bytes 2359304 | tf_op jit(solution)/shard_map/ppermute | solution.py:18
  511.4 5.4 collective-permute-start.23
  516.8 10.7 %collective-permute-done.33 = f32[4,6,128,64]{2,3,1,0:T(8,128)S(1)} collective-permute-done((f32[4,6,128,64]{2,3,1,0:T(8,128)S(1)}, f32[4,6,128,64]{2,3,1,0:T(8,128)S(1)}, u32[]{:S(2)}, u32[]{:S(2)}) %collective-permute-start.33) | collective-permute-done | bytes 786464 | tf_op jit(solution)/shard_map/ppermute | solution.py:18
  529.8 21.5 %collective-permute-start.18 = (f32[4,6]{1,0:T(4,128)S(1)}, f32[4,6]{1,0:T(4,128)S(1)}, u32[]{:S(2)}, u32[]{:S(2)}) collective-permute-start(f32[4,6]{1,0:T(4,128)S(1)} %copy-done.47), channel_id=1, source_target_pairs={{2,0},{4,2},{6,4},{8,6},{10,8},{12,10},{14,12},{16,14},{18,16},{20... | collective-permute-start | bytes 296 | tf_op jit(solution)/shard_map/ppermute | solution.py:18
  552.7 4.9 collective-permute-start.19
  557.6 5.0 collective-permute-start.29
  566.9 4.8 collective-permute-start.24
  573.7 11.1 %collective-permute-done.24 = f32[4,6,128,64]{2,3,1,0:T(8,128)S(1)} collective-permute-done((f32[4,6,128,64]{2,3,1,0:T(8,128)S(1)}, f32[4,6,128,64]{2,3,1,0:T(8,128)S(1)}, u32[]{:S(2)}, u32[]{:S(2)}) %collective-permute-start.24) | collective-permute-done | bytes 786464 | tf_op jit(solution)/shard_map/ppermute | solution.py:18
  585.0 3.5 collective-permute-start.25
  588.5 12.0 %collective-permute-done.35 = f32[4,6,128,64]{2,3,1,0:T(8,128)S(1)} collective-permute-done((f32[4,6,128,64]{2,3,1,0:T(8,128)S(1)}, f32[4,6,128,64]{2,3,1,0:T(8,128)S(1)}, u32[]{:S(2)}, u32[]{:S(2)}) %collective-permute-start.35) | collective-permute-done | bytes 786464 | tf_op jit(solution)/shard_map/ppermute | solution.py:18
  602.3 4.3 fusion.49
  606.6 7.4 %copy.157 = bf16[2,256,4,6,64]{4,3,2,1,0:T(8,128)(2,1)} copy(bf16[2,256,4,6,64]{1,4,3,2,0:T(8,128)(2,1)} %fusion.49) | data formatting | bytes 3145728 | tf_op jit(solution)/shard_map/convert_element_type | solution.py:163
  614.0 6.4 convert_element_type.155
  620.5 3.3 gather_fusion.6
  626.6 7.3 all-to-all-start.3
  636.3 48.6 %collective-permute-done.20 = f32[4,6]{1,0:T(4,128)S(1)} collective-permute-done((f32[4,6]{1,0:T(4,128)S(1)}, f32[4,6]{1,0:T(4,128)S(1)}, u32[]{:S(2)}, u32[]{:S(2)}) %collective-permute-start.20) | collective-permute-done | bytes 128 | tf_op jit(solution)/shard_map/ppermute | solution.py:18
  696.6 11.7 %collective-permute-done.26 = f32[4,6,128,64]{2,3,1,0:T(8,128)S(1)} collective-permute-done((f32[4,6,128,64]{2,3,1,0:T(8,128)}, f32[4,6,128,64]{2,3,1,0:T(8,128)S(1)}, u32[]{:S(2)}, u32[]{:S(2)}) %collective-permute-start.26) | collective-permute-done | bytes 786464 | tf_op jit(solution)/shard_map/ppermute | solution.py:18
  712.0 3.5 fusion.75
  724.5 3.6 copy.158
  728.1 3.4 add_convert_fusion
  (297 shorter events, 145.0 us)
Async XLA Ops:
  10.8 27.4 %copy-start.39 = (bf16[24,512]{1,0:T(8,128)(2,1)S(1)}, bf16[24,512]{1,0:T(8,128)(2,1)}, u32[]{:S(2)}) copy-start(bf16[24,512]{1,0:T(8,128)(2,1)} %param.17) | copy-start | bytes 73732
  10.8 42.8 %copy-start.56 = (s32[16]{0:T(128)S(1)}, s32[16]{0:T(128)}, u32[]{:S(2)}) copy-start(s32[16]{0:T(128)} %param.21) | copy-start | bytes 196
  10.8 66.5 %all-to-all-start = ((bf16[16,32,2560]{2,1,0:T(8,128)(2,1)}), bf16[16,32,2560]{2,1,0:T(8,128)(2,1)S(1)}, u32[]{:S(2)}, u32[]{:S(2)}) async-start(bf16[16,32,2560]{2,1,0:T(8,128)(2,1)} %broadcast_select_fusion.1), calls=%async_computation | async-start | bytes 5242880 | tf_op jit(solution)/shard_map/all_to_all | solution.py:96
  34.0 91.9 %collective-permute-start.9 = (f32[4,6]{1,0:T(4,128)}, f32[4,6]{1,0:T(4,128)}, u32[]{:S(2)}, u32[]{:S(2)}) collective-permute-start(f32[4,6]{1,0:T(4,128)} %get-tuple-element.67), channel_id=1, source_target_pairs={{2,0},{4,2},{6,4},{8,6},{10,8},{12,10},{14,12},{16,14},{18,16},{20... | collective-permute-start | bytes 296 | tf_op jit(solution)/shard_map/ppermute | solution.py:18
  53.6 25.9 %copy-start.53 = (pred[16]{0:T(512)(128)(4,1)}, pred[16]{0:T(512)(128)(4,1)S(1)}, u32[]{:S(2)}) copy-start(pred[16]{0:T(512)(128)(4,1)S(1)} %get-tuple-element.31) | copy-start | bytes 52
  54.1 25.3 %copy-start.45 = (s32[1024]{0:T(1024)}, s32[1024]{0:T(1024)S(1)}, u32[]{:S(2)}) copy-start(s32[1024]{0:T(1024)S(1)} %pad_clamp_fusion.2) | copy-start | bytes 12292
  54.1 40.6 %copy-start.40 = (f32[4,6]{1,0:T(4,128)}, f32[4,6]{1,0:T(4,128)S(1)}, u32[]{:S(2)}) copy-start(f32[4,6]{1,0:T(4,128)S(1)} %get-tuple-element.62) | copy-start | bytes 292
  82.6 154.6 %copy-start.2 = (bf16[2,256,4,128]{3,2,1,0:T(4,128)(2,1)}, bf16[2,256,4,128]{3,2,1,0:T(4,128)(2,1)S(1)}, u32[]{:S(2)}) copy-start(bf16[2,256,4,128]{3,2,1,0:T(4,128)(2,1)S(1)} %reshape.247) | copy-start | bytes 1572868
  95.8 20.6 %collective-permute-start.13 = (f32[4,6,128,64]{2,3,1,0:T(8,128)}, f32[4,6,128,64]{2,3,1,0:T(8,128)S(1)}, u32[]{:S(2)}, u32[]{:S(2)}) collective-permute-start(f32[4,6,128,64]{2,3,1,0:T(8,128)} %fusion.88), channel_id=1, source_target_pairs={{2,0},{4,2},{6,4},{8,6},{10,8},{12,10},{14,12},{16,14},{18,16},{20... | collective-permute-start | bytes 2359304 | tf_op jit(solution)/shard_map/ppermute | solution.py:18
  104.4 54.0 %copy-start.46 = (f32[4,6]{1,0:T(4,128)}, f32[4,6]{1,0:T(4,128)S(1)}, u32[]{:S(2)}) copy-start(f32[4,6]{1,0:T(4,128)S(1)} %get-tuple-element.68) | copy-start | bytes 292
  116.4 9.5 %copy-start.23 = (f32[4,6,128,64]{2,3,1,0:T(8,128)}, f32[4,6,128,64]{2,3,1,0:T(8,128)S(1)}, u32[]{:S(2)}) copy-start(f32[4,6,128,64]{2,3,1,0:T(8,128)S(1)} %collective-permute-done.13) | copy-start | bytes 2359300
  116.4 38.7 %collective-permute-start.14 = (f32[4,6,128,64]{2,3,1,0:T(8,128)S(1)}, f32[4,6,128,64]{2,3,1,0:T(8,128)S(1)}, u32[]{:S(2)}, u32[]{:S(2)}) collective-permute-start(f32[4,6,128,64]{2,3,1,0:T(8,128)S(1)} %collective-permute-done.13), channel_id=1, source_target_pairs={{2,0},{4,2},{6,4},{8,6},{10,8},{12,10},{14,12},{16,14},{18,16},{20... | collective-permute-start | bytes 2359304 | tf_op jit(solution)/shard_map/ppermute | solution.py:18
  123.7 36.6 %copy-start.60 = (s32[16]{0:T(128)S(1)}, s32[16]{0:T(128)}, u32[]{:S(2)}) copy-start(s32[16]{0:T(128)} %copy-done.59) | copy-start | bytes 196
  125.9 28.5 %collective-permute-start.10 = (f32[4,6]{1,0:T(4,128)}, f32[4,6]{1,0:T(4,128)S(1)}, u32[]{:S(2)}, u32[]{:S(2)}) collective-permute-start(f32[4,6]{1,0:T(4,128)} %collective-permute-done.9), channel_id=1, source_target_pairs={{2,0},{4,2},{6,4},{8,6},{10,8},{12,10},{14,12},{16,14},{18,16},{20... | collective-permute-start | bytes 296 | tf_op jit(solution)/shard_map/ppermute | solution.py:18
  127.8 33.7 %collective-permute-start.4 = (f32[4,6,128,64]{2,3,1,0:T(8,128)}, f32[4,6,128,64]{2,3,1,0:T(8,128)}, u32[]{:S(2)}, u32[]{:S(2)}) collective-permute-start(f32[4,6,128,64]{2,3,1,0:T(8,128)} %fusion.90), channel_id=1, source_target_pairs={{0,2},{2,4},{4,6},{6,8},{8,10},{10,12},{12,14},{14,16},{16,18},{18... | collective-permute-start | bytes 2359304 | tf_op jit(solution)/shard_map/ppermute | solution.py:18
  156.4 33.7 %collective-permute-start.15 = (f32[4,6,128,64]{2,3,1,0:T(8,128)S(1)}, f32[4,6,128,64]{2,3,1,0:T(8,128)}, u32[]{:S(2)}, u32[]{:S(2)}) collective-permute-start(f32[4,6,128,64]{2,3,1,0:T(8,128)S(1)} %multiply_add_fusion.12), channel_id=1, source_target_pairs={{4,0},{6,2},{8,4},{10,6},{12,8},{14,10},{16,12},{18,14},{20,16},{2... | collective-permute-start | bytes 2359304 | tf_op jit(solution)/shard_map/ppermute | solution.py:18
  158.4 10.2 %collective-permute-start = (f32[4,6]{1,0:T(4,128)S(1)}, f32[4,6]{1,0:T(4,128)S(1)}, u32[]{:S(2)}, u32[]{:S(2)}) collective-permute-start(f32[4,6]{1,0:T(4,128)S(1)} %get-tuple-element.68), channel_id=1, source_target_pairs={{0,2},{2,4},{4,6},{6,8},{8,10},{10,12},{12,14},{14,16},{16,18},{18... | collective-permute-start | bytes 296 | tf_op jit(solution)/shard_map/ppermute | solution.py:18
  161.6 31.8 %collective-permute-start.5 = (f32[4,6,128,64]{2,3,1,0:T(8,128)}, f32[4,6,128,64]{2,3,1,0:T(8,128)S(1)}, u32[]{:S(2)}, u32[]{:S(2)}) collective-permute-start(f32[4,6,128,64]{2,3,1,0:T(8,128)} %collective-permute-done.4), channel_id=1, source_target_pairs={{0,2},{2,4},{4,6},{6,8},{8,10},{10,12},{12,14},{14,16},{16,18},{18... | collective-permute-start | bytes 2359304 | tf_op jit(solution)/shard_map/ppermute | solution.py:18
  167.9 92.1 %copy-start.49 = (pred[16]{0:T(512)(128)(4,1)}, pred[16]{0:T(512)(128)(4,1)S(1)}, u32[]{:S(2)}) copy-start(pred[16]{0:T(512)(128)(4,1)S(1)} %compare_and_fusion.1) | copy-start | bytes 52
  168.5 24.8 %collective-permute-start.1 = (f32[4,6]{1,0:T(4,128)S(1)}, f32[4,6]{1,0:T(4,128)S(1)}, u32[]{:S(2)}, u32[]{:S(2)}) collective-permute-start(f32[4,6]{1,0:T(4,128)S(1)} %collective-permute-done), channel_id=1, source_target_pairs={{0,2},{2,4},{4,6},{6,8},{8,10},{10,12},{12,14},{14,16},{16,18},{18... | collective-permute-start | bytes 296 | tf_op jit(solution)/shard_map/ppermute | solution.py:18
  191.4 22.6 %collective-permute-start.16 = (f32[4,6,128,64]{2,3,1,0:T(8,128)S(1)}, f32[4,6,128,64]{2,3,1,0:T(8,128)S(1)}, u32[]{:S(2)}, u32[]{:S(2)}) collective-permute-start(f32[4,6,128,64]{2,3,1,0:T(8,128)S(1)} %multiply_add_fusion.11), channel_id=1, source_target_pairs={{8,0},{10,2},{12,4},{14,6},{16,8},{18,10},{20,12},{22,14},{24,16},... | collective-permute-start | bytes 2359304 | tf_op jit(solution)/shard_map/ppermute | solution.py:18
  194.6 37.7 %collective-permute-start.6 = (f32[4,6,128,64]{2,3,1,0:T(8,128)S(1)}, f32[4,6,128,64]{2,3,1,0:T(8,128)S(1)}, u32[]{:S(2)}, u32[]{:S(2)}) collective-permute-start(f32[4,6,128,64]{2,3,1,0:T(8,128)S(1)} %multiply_add_fusion.16), channel_id=1, source_target_pairs={{0,4},{2,6},{4,8},{6,10},{8,12},{10,14},{12,16},{14,18},{16,20},{1... | collective-permute-start | bytes 2359304 | tf_op jit(solution)/shard_map/ppermute | solution.py:18
  200.6 57.5 %copy-start.42 = (s32[1024]{0:T(1024)}, s32[1024]{0:T(1024)S(1)}, u32[]{:S(2)}) copy-start(s32[1024]{0:T(1024)S(1)} %pad_clamp_fusion.1) | copy-start | bytes 12292
  200.6 11.3 %collective-permute-start.11 = (f32[4,6]{1,0:T(4,128)S(1)}, f32[4,6]{1,0:T(4,128)S(1)}, u32[]{:S(2)}, u32[]{:S(2)}) collective-permute-start(f32[4,6]{1,0:T(4,128)S(1)} %get-tuple-element.30), channel_id=1, source_target_pairs={{4,0},{6,2},{8,4},{10,6},{12,8},{14,10},{16,12},{18,14},{20,16},{2... | collective-permute-start | bytes 296 | tf_op jit(solution)/shard_map/ppermute | solution.py:18
  202.5 73.4 %collective-permute-start.2 = (f32[4,6]{1,0:T(4,128)S(1)}, f32[4,6]{1,0:T(4,128)S(1)}, u32[]{:S(2)}, u32[]{:S(2)}) collective-permute-start(f32[4,6]{1,0:T(4,128)S(1)} %get-tuple-element.36), channel_id=1, source_target_pairs={{0,4},{2,6},{4,8},{6,10},{8,12},{10,14},{12,16},{14,18},{16,20},{1... | collective-permute-start | bytes 296 | tf_op jit(solution)/shard_map/ppermute | solution.py:18
  211.9 20.4 %collective-permute-start.12 = (f32[4,6]{1,0:T(4,128)S(1)}, f32[4,6]{1,0:T(4,128)S(1)}, u32[]{:S(2)}, u32[]{:S(2)}) collective-permute-start(f32[4,6]{1,0:T(4,128)S(1)} %get-tuple-element.28), channel_id=1, source_target_pairs={{8,0},{10,2},{12,4},{14,6},{16,8},{18,10},{20,12},{22,14},{24,16},... | collective-permute-start | bytes 296 | tf_op jit(solution)/shard_map/ppermute | solution.py:18
  214.2 23.5 %collective-permute-start.17 = (f32[4,6,128,64]{2,3,1,0:T(8,128)S(1)}, f32[4,6,128,64]{2,3,1,0:T(8,128)}, u32[]{:S(2)}, u32[]{:S(2)}) collective-permute-start(f32[4,6,128,64]{2,3,1,0:T(8,128)S(1)} %multiply_add_fusion.10), channel_id=1, source_target_pairs={{16,0},{18,2},{20,4},{22,6},{24,8},{26,10},{28,12},{30,14},{17,1},... | collective-permute-start | bytes 2359304 | tf_op jit(solution)/shard_map/ppermute | solution.py:18
  233.5 42.5 %collective-permute-start.7 = (f32[4,6,128,64]{2,3,1,0:T(8,128)}, f32[4,6,128,64]{2,3,1,0:T(8,128)}, u32[]{:S(2)}, u32[]{:S(2)}) collective-permute-start(f32[4,6,128,64]{2,3,1,0:T(8,128)} %multiply_add_fusion.15), channel_id=1, source_target_pairs={{0,8},{2,10},{4,12},{6,14},{8,16},{10,18},{12,20},{14,22},{16,24},... | collective-permute-start | bytes 2359304 | tf_op jit(solution)/shard_map/ppermute | solution.py:18
  262.7 21.0 %copy-start.58 = (s32[16]{0:T(128)S(1)}, s32[16]{0:T(128)}, u32[]{:S(2)}) copy-start(s32[16]{0:T(128)} %copy-done.57) | copy-start | bytes 196
  262.7 21.0 %copy-start.15 = (bf16[512,512]{1,0:T(8,128)(2,1)S(1)}, bf16[512,512]{1,0:T(8,128)(2,1)}, u32[]{:S(2)}) copy-start(bf16[512,512]{1,0:T(8,128)(2,1)} %param.16) | copy-start | bytes 1572868
  262.7 91.5 %all-to-all-start.1 = ((bf16[16,32,1536]{2,1,0:T(8,128)(2,1)}), bf16[16,32,1536]{2,1,0:T(8,128)(2,1)}, u32[]{:S(2)}, u32[]{:S(2)}) async-start(bf16[16,32,1536]{2,1,0:T(8,128)(2,1)} %broadcast_select_fusion.7), calls=%async_computation.1 | async-start | bytes 3145728 | tf_op jit(solution)/shard_map/all_to_all | solution.py:96
  278.4 64.3 %collective-permute-start.8 = (f32[4,6,128,64]{2,3,1,0:T(8,128)}, f32[4,6,128,64]{2,3,1,0:T(8,128)}, u32[]{:S(2)}, u32[]{:S(2)}) collective-permute-start(f32[4,6,128,64]{2,3,1,0:T(8,128)} %multiply_add_fusion.14), channel_id=1, source_target_pairs={{0,16},{2,18},{4,20},{6,22},{8,24},{10,26},{12,28},{14,30},{1,17},... | collective-permute-start | bytes 2359304 | tf_op jit(solution)/shard_map/ppermute | solution.py:18
  286.4 67.9 %copy-start.43 = (s32[1024]{0:T(1024)}, s32[1024]{0:T(1024)S(1)}, u32[]{:S(2)}) copy-start(s32[1024]{0:T(1024)S(1)} %pad_clamp_fusion) | copy-start | bytes 12292
  286.4 58.9 %copy-start.27 = (pred[256,256]{1,0:T(8,128)(4,1)}, pred[256,256]{1,0:T(8,128)(4,1)S(1)}, u32[]{:S(2)}) copy-start(pred[256,256]{1,0:T(8,128)(4,1)S(1)} %iota_compare_fusion.1) | copy-start | bytes 196612
  289.4 53.4 %collective-permute-start.3 = (f32[4,6]{1,0:T(4,128)S(1)}, f32[4,6]{1,0:T(4,128)S(1)}, u32[]{:S(2)}, u32[]{:S(2)}) collective-permute-start(f32[4,6]{1,0:T(4,128)S(1)} %get-tuple-element.34), channel_id=1, source_target_pairs={{0,8},{2,10},{4,12},{6,14},{8,16},{10,18},{12,20},{14,22},{16,24},... | collective-permute-start | bytes 296 | tf_op jit(solution)/shard_map/ppermute | solution.py:18
  291.6 53.1 %copy-start.4 = (bf16[2,256,4,128]{3,2,1,0:T(4,128)(2,1)S(1)}, bf16[2,256,4,128]{3,2,1,0:T(4,128)(2,1)}, u32[]{:S(2)}) copy-start(bf16[2,256,4,128]{3,2,1,0:T(4,128)(2,1)} %reshape.238) | copy-start | bytes 1572868
  378.5 11.2 %copy-start.7 = (bf16[2,256,4,128]{3,2,1,0:T(4,128)(2,1)S(1)}, bf16[2,256,4,128]{3,2,1,0:T(4,128)(2,1)}, u32[]{:S(2)}) copy-start(bf16[2,256,4,128]{3,2,1,0:T(4,128)(2,1)} %copy-done.6) | copy-start | bytes 1572868
  381.4 45.5 %all-to-all-start.2 = ((bf16[16,32,1536]{2,1,0:T(8,128)(2,1)}), bf16[16,32,1536]{2,1,0:T(8,128)(2,1)}, u32[]{:S(2)}, u32[]{:S(2)}) async-start(bf16[16,32,1536]{2,1,0:T(8,128)(2,1)} %broadcast_select_fusion.3), calls=%async_computation.2 | async-start | bytes 3145728 | tf_op jit(solution)/shard_map/all_to_all | solution.py:96
  389.8 40.4 %copy-start.54 = (pred[16]{0:T(512)(128)(4,1)S(1)}, pred[16]{0:T(512)(128)(4,1)}, u32[]{:S(2)}) copy-start(pred[16]{0:T(512)(128)(4,1)} %copy-done.53) | copy-start | bytes 52
  444.8 10.8 %copy-start.24 = (f32[4,6,2,256]{3,1,0,2:T(8,128)S(1)}, f32[4,6,2,256]{3,1,0,2:T(8,128)}, u32[]{:S(2)}) copy-start(f32[4,6,2,256]{3,1,0,2:T(8,128)} %get-tuple-element.59) | copy-start | bytes 147460
  449.0 23.6 %collective-permute-start.31 = (f32[4,6,128,64]{2,3,1,0:T(8,128)S(1)}, f32[4,6,128,64]{2,3,1,0:T(8,128)S(1)}, u32[]{:S(2)}, u32[]{:S(2)}) collective-permute-start(f32[4,6,128,64]{2,3,1,0:T(8,128)S(1)} %fusion.84), channel_id=1, source_target_pairs={{0,2},{2,4},{4,6},{6,8},{8,10},{10,12},{12,14},{14,16},{16,18},{18... | collective-permute-start | bytes 2359304 | tf_op jit(solution)/shard_map/ppermute | solution.py:18
  452.1 18.4 %collective-permute-start.27 = (f32[4,6]{1,0:T(4,128)}, f32[4,6]{1,0:T(4,128)S(1)}, u32[]{:S(2)}, u32[]{:S(2)}) collective-permute-start(f32[4,6]{1,0:T(4,128)} %get-tuple-element.67), channel_id=1, source_target_pairs={{0,2},{2,4},{4,6},{6,8},{8,10},{10,12},{12,14},{14,16},{16,18},{18... | collective-permute-start | bytes 296 | tf_op jit(solution)/shard_map/ppermute | solution.py:18
  470.6 6.9 collective-permute-start.28
  472.6 23.4 %collective-permute-start.32 = (f32[4,6,128,64]{2,3,1,0:T(8,128)S(1)}, f32[4,6,128,64]{2,3,1,0:T(8,128)}, u32[]{:S(2)}, u32[]{:S(2)}) collective-permute-start(f32[4,6,128,64]{2,3,1,0:T(8,128)S(1)} %collective-permute-done.31), channel_id=1, source_target_pairs={{0,2},{2,4},{4,6},{6,8},{8,10},{10,12},{12,14},{14,16},{16,18},{18... | collective-permute-start | bytes 2359304 | tf_op jit(solution)/shard_map/ppermute | solution.py:18
  483.6 44.1 %copy-start.9 = (f32[4,6,2,128,64]{3,4,1,0,2:T(8,128)}, f32[4,6,2,128,64]{3,4,1,0,2:T(8,128)S(1)}, u32[]{:S(2)}) copy-start(f32[4,6,2,128,64]{3,4,1,0,2:T(8,128)S(1)} %fusion.58) | copy-start | bytes 4718596
  483.8 46.0 %copy-start.47 = (f32[4,6]{1,0:T(4,128)S(1)}, f32[4,6]{1,0:T(4,128)}, u32[]{:S(2)}) copy-start(f32[4,6]{1,0:T(4,128)} %copy-done.46) | copy-start | bytes 292
  483.8 27.6 %collective-permute-start.22 = (f32[4,6,128,64]{2,3,1,0:T(8,128)S(1)}, f32[4,6,128,64]{2,3,1,0:T(8,128)S(1)}, u32[]{:S(2)}, u32[]{:S(2)}) collective-permute-start(f32[4,6,128,64]{2,3,1,0:T(8,128)S(1)} %fusion.86), channel_id=1, source_target_pairs={{2,0},{4,2},{6,4},{8,6},{10,8},{12,10},{14,12},{16,14},{18,16},{20... | collective-permute-start | bytes 2359304 | tf_op jit(solution)/shard_map/ppermute | solution.py:18
  497.3 30.2 %collective-permute-start.33 = (f32[4,6,128,64]{2,3,1,0:T(8,128)S(1)}, f32[4,6,128,64]{2,3,1,0:T(8,128)S(1)}, u32[]{:S(2)}, u32[]{:S(2)}) collective-permute-start(f32[4,6,128,64]{2,3,1,0:T(8,128)S(1)} %multiply_add_fusion.4), channel_id=1, source_target_pairs={{0,4},{2,6},{4,8},{6,10},{8,12},{10,14},{12,16},{14,18},{16,20},{1... | collective-permute-start | bytes 2359304 | tf_op jit(solution)/shard_map/ppermute | solution.py:18
  511.4 55.3 %collective-permute-start.23 = (f32[4,6,128,64]{2,3,1,0:T(8,128)S(1)}, f32[4,6,128,64]{2,3,1,0:T(8,128)S(1)}, u32[]{:S(2)}, u32[]{:S(2)}) collective-permute-start(f32[4,6,128,64]{2,3,1,0:T(8,128)S(1)} %collective-permute-done.22), channel_id=1, source_target_pairs={{2,0},{4,2},{6,4},{8,6},{10,8},{12,10},{14,12},{16,14},{18,16},{20... | collective-permute-start | bytes 2359304 | tf_op jit(solution)/shard_map/ppermute | solution.py:18
  527.7 45.6 %copy-start.3 = (bf16[2,256,4,128]{3,2,1,0:T(4,128)(2,1)S(1)}, bf16[2,256,4,128]{3,2,1,0:T(4,128)(2,1)}, u32[]{:S(2)}) copy-start(bf16[2,256,4,128]{3,2,1,0:T(4,128)(2,1)} %copy-done.2) | copy-start | bytes 1572868
  527.7 44.0 %collective-permute-start.34 = (f32[4,6,128,64]{2,3,1,0:T(8,128)S(1)}, f32[4,6,128,64]{2,3,1,0:T(8,128)S(1)}, u32[]{:S(2)}, u32[]{:S(2)}) collective-permute-start(f32[4,6,128,64]{2,3,1,0:T(8,128)S(1)} %multiply_add_fusion.3), channel_id=1, source_target_pairs={{0,8},{2,10},{4,12},{6,14},{8,16},{10,18},{12,20},{14,22},{16,24},... | collective-permute-start | bytes 2359304 | tf_op jit(solution)/shard_map/ppermute | solution.py:18
  529.8 22.9 %collective-permute-start.18 = (f32[4,6]{1,0:T(4,128)S(1)}, f32[4,6]{1,0:T(4,128)S(1)}, u32[]{:S(2)}, u32[]{:S(2)}) collective-permute-start(f32[4,6]{1,0:T(4,128)S(1)} %copy-done.47), channel_id=1, source_target_pairs={{2,0},{4,2},{6,4},{8,6},{10,8},{12,10},{14,12},{16,14},{18,16},{20... | collective-permute-start | bytes 296 | tf_op jit(solution)/shard_map/ppermute | solution.py:18
  552.7 10.0 %collective-permute-start.19 = (f32[4,6]{1,0:T(4,128)S(1)}, f32[4,6]{1,0:T(4,128)S(1)}, u32[]{:S(2)}, u32[]{:S(2)}) collective-permute-start(f32[4,6]{1,0:T(4,128)S(1)} %collective-permute-done.18), channel_id=1, source_target_pairs={{2,0},{4,2},{6,4},{8,6},{10,8},{12,10},{14,12},{16,14},{18,16},{20... | collective-permute-start | bytes 296 | tf_op jit(solution)/shard_map/ppermute | solution.py:18
  557.6 7.2 collective-permute-start.29
  564.8 8.4 %collective-permute-start.30 = (f32[4,6]{1,0:T(4,128)S(1)}, f32[4,6]{1,0:T(4,128)S(1)}, u32[]{:S(2)}, u32[]{:S(2)}) collective-permute-start(f32[4,6]{1,0:T(4,128)S(1)} %get-tuple-element.17), channel_id=1, source_target_pairs={{0,8},{2,10},{4,12},{6,14},{8,16},{10,18},{12,20},{14,22},{16,24},... | collective-permute-start | bytes 296 | tf_op jit(solution)/shard_map/ppermute | solution.py:18
  566.9 17.9 %collective-permute-start.24 = (f32[4,6,128,64]{2,3,1,0:T(8,128)S(1)}, f32[4,6,128,64]{2,3,1,0:T(8,128)S(1)}, u32[]{:S(2)}, u32[]{:S(2)}) collective-permute-start(f32[4,6,128,64]{2,3,1,0:T(8,128)S(1)} %multiply_add_fusion.8), channel_id=1, source_target_pairs={{4,0},{6,2},{8,4},{10,6},{12,8},{14,10},{16,12},{18,14},{20,16},{2... | collective-permute-start | bytes 2359304 | tf_op jit(solution)/shard_map/ppermute | solution.py:18
  571.9 28.6 %collective-permute-start.35 = (f32[4,6,128,64]{2,3,1,0:T(8,128)S(1)}, f32[4,6,128,64]{2,3,1,0:T(8,128)S(1)}, u32[]{:S(2)}, u32[]{:S(2)}) collective-permute-start(f32[4,6,128,64]{2,3,1,0:T(8,128)S(1)} %multiply_add_fusion.2), channel_id=1, source_target_pairs={{0,16},{2,18},{4,20},{6,22},{8,24},{10,26},{12,28},{14,30},{1,17},... | collective-permute-start | bytes 2359304 | tf_op jit(solution)/shard_map/ppermute | solution.py:18
  573.3 27.3 %copy-start.13 = (f32[4,6,2,128,64]{3,4,1,0,2:T(8,128)S(1)}, f32[4,6,2,128,64]{3,4,1,0,2:T(8,128)}, u32[]{:S(2)}) copy-start(f32[4,6,2,128,64]{3,4,1,0,2:T(8,128)} %copy-done.12) | copy-start | bytes 4718596
  585.0 99.9 %collective-permute-start.25 = (f32[4,6,128,64]{2,3,1,0:T(8,128)S(1)}, f32[4,6,128,64]{2,3,1,0:T(8,128)}, u32[]{:S(2)}, u32[]{:S(2)}) collective-permute-start(f32[4,6,128,64]{2,3,1,0:T(8,128)S(1)} %multiply_add_fusion.7), channel_id=1, source_target_pairs={{8,0},{10,2},{12,4},{14,6},{16,8},{18,10},{20,12},{22,14},{24,16},... | collective-permute-start | bytes 2359304 | tf_op jit(solution)/shard_map/ppermute | solution.py:18
  626.6 64.0 %copy-start.1 = (bf16[2,256,4,128]{3,2,1,0:T(4,128)(2,1)S(1)}, bf16[2,256,4,128]{3,2,1,0:T(4,128)(2,1)}, u32[]{:S(2)}) copy-start(bf16[2,256,4,128]{3,2,1,0:T(4,128)(2,1)} %copy-done) | copy-start | bytes 1572868
  626.6 93.3 %all-to-all-start.3 = ((bf16[16,32,1536]{2,1,0:T(8,128)(2,1)}), bf16[16,32,1536]{2,1,0:T(8,128)(2,1)}, u32[]{:S(2)}, u32[]{:S(2)}) async-start(bf16[16,32,1536]{2,1,0:T(8,128)(2,1)} %broadcast_select_fusion.6), calls=%async_computation.3 | async-start | bytes 3145728 | tf_op jit(solution)/shard_map/all_to_all | solution.py:96
  633.8 51.1 %collective-permute-start.20 = (f32[4,6]{1,0:T(4,128)S(1)}, f32[4,6]{1,0:T(4,128)S(1)}, u32[]{:S(2)}, u32[]{:S(2)}) collective-permute-start(f32[4,6]{1,0:T(4,128)S(1)} %get-tuple-element.23), channel_id=1, source_target_pairs={{4,0},{6,2},{8,4},{10,6},{12,8},{14,10},{16,12},{18,14},{20,16},{2... | collective-permute-start | bytes 296 | tf_op jit(solution)/shard_map/ppermute | solution.py:18
  687.1 21.2 %collective-permute-start.26 = (f32[4,6,128,64]{2,3,1,0:T(8,128)}, f32[4,6,128,64]{2,3,1,0:T(8,128)S(1)}, u32[]{:S(2)}, u32[]{:S(2)}) collective-permute-start(f32[4,6,128,64]{2,3,1,0:T(8,128)} %multiply_add_fusion.6), channel_id=1, source_target_pairs={{16,0},{18,2},{20,4},{22,6},{24,8},{26,10},{28,12},{30,14},{17,1},... | collective-permute-start | bytes 2359304 | tf_op jit(solution)/shard_map/ppermute | solution.py:18
  688.4 5.6 collective-permute-start.21
  (37 other events, 99.8 us)
where the time goes:
time: 744 us; the launch traced here: 733 us
  waiting for transfers between devices  310 us (42%)
  starting transfers between devices  176 us (24%)
  local copies, waits for them, and re-layouts  108 us (15%)
  other arithmetic  92.8 us (12%)
  matrix products  41.3 us (6%)
    ppermute x36, waiting for transfers between devices, passed_along(): return lax.ppermute(block, axis, route)  250 us
    ppermute x36, starting transfers between devices, passed_along(): return lax.ppermute(block, axis, route)  140 us
    all_to_all x4, waiting for transfers between devices, reorder(): lax.all_to_all(outgoing, 'seq', split_axis=0, concat_axis=0, tiled=True)  60.2 us
    all_to_all x4, starting transfers between devices, reorder(): lax.all_to_all(outgoing, 'seq', split_axis=0, concat_axis=0, tiled=True)  36 us
    another operation x6, other arithmetic  29.2 us
    unnamed x130, local copies, waits for them, and re-layouts  20.4 us
    dot_general x4, matrix products, scan_block(): jnp.einsum('ghcjn,cjghp->ghcnp', scaled_keys, value_blocks, preferred_ele...  18.3 us
    dot_general x4, matrix products, scan_block(): jnp.einsum('ghcij,cjghp->cighp', weights, value_blocks, preferred_element...  15.1 us
  transfers between devices with their start and end apart: 40, of which 18 were waited for; matrix products, arithmetic and copies ran while one was open for 22% of the time, Pallas kernels for 0%

commit v1 on v0

v1 whole, which is shorter than its diff:
```python
import functools

import jax
import jax.numpy as jnp
from jax import lax
from jax.experimental import pallas as pl
from jax.experimental.pallas import tpu as pltpu
from jax.sharding import PartitionSpec as P

HEAD_DIM = 64
STATE = 128
SPAN = 256
FEATURES = 3072
PAD = 8
LANES = 128
EPSILON = 1e-05
F32 = jnp.float32
BF16 = jnp.bfloat16


def triangle(lower):
    rows = lax.broadcasted_iota(jnp.int32, (SPAN, SPAN), 0)
    cols = lax.broadcasted_iota(jnp.int32, (SPAN, SPAN), 1)
    return cols <= rows if lower else cols >= rows


def spread_pair(columns, pair):
    shape = (columns.shape[0], LANES)
    lane = lax.broadcasted_iota(jnp.int32, shape, 1)
    return jnp.where(
        lane < HEAD_DIM, columns[:, 2 * pair : 2 * pair + 1], columns[:, 2 * pair + 1 : 2 * pair + 2]
    )


def spread_heads(columns, pairs):
    return jnp.concatenate([spread_pair(columns, pair) for pair in range(pairs)], axis=1)


def running_columns(decay):
    ones = jnp.where(triangle(True), 1.0, 0.0).astype(BF16)
    return lax.dot_general(ones, decay, (((1,), (1,)), ((), ())), preferred_element_type=F32)


def running_rows(decay):
    ones = jnp.where(triangle(False), 1.0, 0.0).astype(BF16)
    return jnp.dot(decay, ones, preferred_element_type=F32)


def states_kernel(reverse, spans, v_ref, k_ref, decay_ref, before_ref, total_ref):
    pairs = v_ref.shape[1] // LANES
    order = range(spans)
    run = None
    for span in order[::-1] if reverse else order:
        rows = slice(span * SPAN, (span + 1) * SPAN)
        cum = running_columns(decay_ref[0, :, rows].astype(BF16))
        end = cum[SPAN - 1 : SPAN]
        weight = jnp.exp(cum) if reverse else jnp.exp(end - cum)
        scaled = (v_ref[rows, :].astype(F32) * spread_heads(weight, pairs)).astype(BF16)
        state = lax.dot_general(
            k_ref[rows, :], scaled, (((0,), (0,)), ((), ())), preferred_element_type=F32
        )
        if run is None:
            before_ref[span] = jnp.zeros_like(state)
            run = state
        else:
            before_ref[span] = run
            run = run * spread_heads(jnp.exp(end), pairs) + state
    total_ref[...] = run.astype(BF16)


def inner_kernel(reverse, spans, v_ref, k_ref, q_ref, decay_ref, out_ref):
    pairs = v_ref.shape[1] // LANES
    allowed = triangle(not reverse)
    lane = lax.broadcasted_iota(jnp.int32, (SPAN, LANES), 1)
    for span in range(spans):
        rows = slice(span * SPAN, (span + 1) * SPAN)
        decay = decay_ref[0, :, rows].astype(BF16)
        cum_col = running_columns(decay)
        cum_row = running_rows(decay)
        scores = lax.dot_general(
            q_ref[rows, :], k_ref[rows, :], (((1,), (1,)), ((), ())), preferred_element_type=F32
        )
        scores = jnp.where(allowed, scores, 0.0)
        for pair in range(pairs):
            values = v_ref[rows, pair * LANES : (pair + 1) * LANES]
            parts = []
            for head in (2 * pair, 2 * pair + 1):
                col, row = cum_col[:, head : head + 1], cum_row[head : head + 1, :]
                gap = row - col if reverse else col - row
                weights = (scores * jnp.exp(jnp.minimum(gap, 0.0))).astype(BF16)
                parts.append(jnp.dot(weights, values, preferred_element_type=F32))
            out_ref[rows, pair * LANES : (pair + 1) * LANES] = jnp.where(
                lane < HEAD_DIM, parts[0], parts[1]
            )


def finish_kernel(reverse, spans, inner_ref, q_ref, decay_ref, before_ref, incoming_ref, out_ref):
    pairs = inner_ref.shape[1] // LANES
    order = range(spans)
    incoming = incoming_ref[...].astype(F32)
    passed = None
    for span in order[::-1] if reverse else order:
        rows = slice(span * SPAN, (span + 1) * SPAN)
        cum = running_columns(decay_ref[0, :, rows].astype(BF16))
        end = cum[SPAN - 1 : SPAN]
        weight = jnp.exp(end - cum) if reverse else jnp.exp(cum)
        if passed is None:
            entering = incoming
            passed = end
        else:
            entering = before_ref[span] + incoming * spread_heads(jnp.exp(passed), pairs)
            passed = passed + end
        outer = jnp.dot(q_ref[rows, :], entering.astype(BF16), preferred_element_type=F32)
        out_ref[rows, :] = (inner_ref[rows, :] + outer * spread_heads(weight, pairs)).astype(BF16)


class Scan:
    def __init__(self, values, keys, queries, decay, width, reverse):
        self.decay, self.reverse, self.width = decay, reverse, width
        self.groups = decay.shape[0]
        self.tokens = decay.shape[2]
        self.spans = self.tokens // SPAN
        self.cols = width // self.groups
        self.values, self.keys, self.queries = values, keys, queries

    def cut(self, operand, size):
        array, first = operand
        base = first // size
        return array, pl.BlockSpec((self.tokens, size), lambda g: (0, base + g))

    def call(self, body, operands, outs, out_specs, flops):
        arrays, specs = zip(*operands)
        shapes = jax.tree.leaves(outs)
        moved = sum(s.size * s.dtype.itemsize for s in shapes) * 2
        return pl.pallas_call(
            functools.partial(body, self.reverse, self.spans),
            grid=(self.groups,),
            in_specs=list(specs),
            out_specs=out_specs,
            out_shape=outs,
            compiler_params=pltpu.CompilerParams(vmem_limit_bytes=48 * 2**20),
            cost_estimate=pl.CostEstimate(flops=flops, bytes_accessed=moved, transcendentals=0),
        )(*arrays)

    def decay_cut(self):
        return self.decay, pl.BlockSpec((1, PAD, self.tokens), lambda g: (g, 0, 0))

    def states(self):
        wide = pl.BlockSpec((STATE, self.cols), lambda g: (0, g))
        deep = pl.BlockSpec((self.spans, STATE, self.cols), lambda g: (0, 0, g))
        self.before, total = self.call(
            states_kernel,
            [self.cut(self.values, self.cols), self.cut(self.keys, STATE), self.decay_cut()],
            (
                jax.ShapeDtypeStruct((self.spans, STATE, self.width), F32),
                jax.ShapeDtypeStruct((STATE, self.width), BF16),
            ),
            (deep, wide),
            2 * self.tokens * STATE * self.width,
        )
        return total

    def inner(self):
        self.near = self.call(
            inner_kernel,
            [
                self.cut(self.values, self.cols),
                self.cut(self.keys, STATE),
                self.cut(self.queries, STATE),
                self.decay_cut(),
            ],
            jax.ShapeDtypeStruct((self.tokens, self.width), F32),
            pl.BlockSpec((self.tokens, self.cols), lambda g: (0, g)),
            8 * self.tokens * SPAN * self.width,
        )

    def finish(self, incoming):
        wide = pl.BlockSpec((STATE, self.cols), lambda g: (0, g))
        deep = pl.BlockSpec((self.spans, STATE, self.cols), lambda g: (0, 0, g))
        rows = pl.BlockSpec((self.tokens, self.cols), lambda g: (0, g))
        return self.call(
            finish_kernel,
            [
                (self.near, rows),
                self.cut(self.queries, STATE),
                self.decay_cut(),
                (self.before, deep),
                (incoming, wide),
            ],
            jax.ShapeDtypeStruct((self.tokens, self.width), BF16),
            rows,
            2 * self.tokens * STATE * self.width,
        )


def prefix_kernel(reverse, arrived_ref, factor_ref, out_ref):
    count = arrived_ref.shape[0]
    run = jnp.zeros(arrived_ref.shape[1:], F32)
    order = range(count)
    for index in order[::-1] if reverse else order:
        out_ref[index] = run.astype(BF16)
        run = run * factor_ref[index] + arrived_ref[index].astype(F32)


def carried(total, factors, reverse):
    count = lax.axis_size("seq")
    pieces = total.reshape(count, STATE // count, -1)
    arrived = lax.all_to_all(pieces, "seq", split_axis=0, concat_axis=0, tiled=True)
    composed = pl.pallas_call(
        functools.partial(prefix_kernel, reverse),
        out_shape=jax.ShapeDtypeStruct(arrived.shape, BF16),
    )(arrived, factors)
    back = lax.all_to_all(composed, "seq", split_axis=0, concat_axis=0, tiled=True)
    return back.reshape(total.shape)


def gather_kernel(counts, index_ref, *refs):
    sources, out_ref, sems = refs[: len(counts)], refs[-2], refs[-1]
    copies = []
    for unit in range(out_ref.shape[0]):
        first = 0
        for place, (source, width) in enumerate(zip(sources, counts)):
            copy = pltpu.make_async_copy(
                source.at[index_ref[unit]],
                out_ref.at[unit, :, pl.ds(first, width)],
                sems.at[unit, place],
            )
            copy.start()
            copies.append(copy)
            first += width
    for copy in copies:
        copy.wait()


def gathered(arrays, index):
    widths = tuple(array.shape[2] for array in arrays)
    units, rows = arrays[0].shape[:2]
    hbm = pl.BlockSpec(memory_space=pl.ANY)
    return pl.pallas_call(
        functools.partial(gather_kernel, widths),
        in_specs=[pl.BlockSpec(memory_space=pltpu.SMEM)] + [hbm] * len(arrays),
        out_specs=hbm,
        out_shape=jax.ShapeDtypeStruct((units, rows, sum(widths)), arrays[0].dtype),
        scratch_shapes=[pltpu.SemaphoreType.DMA((units, len(arrays)))],
    )(index, *arrays)


def inverse(order):
    count = order.shape[0]
    spots = jnp.arange(count, dtype=jnp.int32)
    return jnp.sum(jnp.where(order[None, :] == spots[:, None], spots[None, :], 0), axis=1)


def shards(
    ssm_input,
    input_map,
    output_map,
    decay_forward,
    decay_reverse,
    skip_gain,
    norm_gain,
    scan_order,
    raster_order,
    grad_normed,
):
    unit_count = scan_order.shape[0]
    tok_rows, width = ssm_input.shape
    unit_rows = tok_rows // unit_count
    maps = input_map.shape[1]
    groups = maps // STATE
    heads = decay_forward.shape[0]
    raster_dest = raster_order // unit_count
    scan_source = scan_order // unit_count
    send_scan = inverse(raster_dest)
    send_raster = inverse(scan_source)

    def units(array):
        return array.reshape(unit_count, unit_rows, -1)

    def moved(arrays, send_index, recv_index):
        outgoing = gathered([units(array) for array in arrays], send_index)
        arrived = lax.all_to_all(outgoing, "seq", split_axis=0, concat_axis=0, tiled=True)
        return gathered([arrived], recv_index).reshape(tok_rows, -1)

    def to_scan(*arrays):
        return moved(arrays, send_scan, scan_source)

    def to_raster(array):
        return moved([array], send_raster, raster_dest)

    def padded(decay):
        wide = decay.astype(F32).reshape(groups, heads // groups, tok_rows)
        return jnp.pad(wide, ((0, 0), (0, PAD - heads // groups), (0, 0)))

    sums = jnp.stack([decay_forward, decay_reverse]).astype(F32).sum(axis=2)
    all_sums = lax.all_gather(sums, "seq", axis=0)
    factors = jnp.repeat(jnp.exp(all_sums), HEAD_DIM, axis=2)
    forward_factors, reverse_factors = factors[:, 0:1], factors[:, 1:2]
    decay_f, decay_r = padded(decay_forward), padded(decay_reverse)

    joined = to_scan(ssm_input, input_map, output_map)
    keys_at, queries_at = width, width + maps

    ahead = Scan((ssm_input, 0), (input_map, 0), (output_map, 0), decay_f, width, False)
    ahead_in = carried(ahead.states(), forward_factors, False)
    ahead.inner()
    y_forward = ahead.finish(ahead_in)

    behind = Scan((joined, 0), (joined, keys_at), (joined, queries_at), decay_r, width, True)
    behind_in = carried(behind.states(), reverse_factors, True)
    behind.inner()
    y_reverse = to_raster(behind.finish(behind_in))

    skip_cols = jnp.repeat(skip_gain, HEAD_DIM)
    combined = (
        y_forward.astype(F32) + y_reverse.astype(F32) + skip_cols * ssm_input.astype(F32)
    )
    scaled_grad = norm_gain * grad_normed.astype(F32)
    both = jnp.stack(
        [jnp.sum(combined * combined, axis=1), jnp.sum(combined * scaled_grad, axis=1)]
    )
    squares, inner_sum = lax.psum(both, "head")
    inv_rms = lax.rsqrt(squares / FEATURES + EPSILON)
    normed_output = (combined * inv_rms[:, None] * norm_gain).astype(BF16)
    grad_combined = (
        inv_rms[:, None] * scaled_grad - combined * (inv_rms**3 * inner_sum / FEATURES)[:, None]
    ).astype(BF16)

    grad_scan = to_scan(grad_combined)
    ahead_grad = Scan((grad_combined, 0), (output_map, 0), (input_map, 0), decay_f, width, True)
    ahead_grad_in = carried(ahead_grad.states(), forward_factors, True)
    ahead_grad.inner()
    grad_forward = ahead_grad.finish(ahead_grad_in)

    behind_grad = Scan((grad_scan, 0), (joined, queries_at), (joined, keys_at), decay_r, width, False)
    behind_grad_in = carried(behind_grad.states(), reverse_factors, False)
    behind_grad.inner()
    grad_reverse = to_raster(behind_grad.finish(behind_grad_in))

    grad_input = (
        grad_forward.astype(F32)
        + grad_reverse.astype(F32)
        + skip_cols * grad_combined.astype(F32)
    )
    return (normed_output, grad_input.astype(BF16))


def solution(mesh):
    return jax.shard_map(
        shards,
        mesh=mesh,
        in_specs=(
            P("seq", "head"),
            P("seq", "head"),
            P("seq", "head"),
            P("head", "seq"),
            P("head", "seq"),
            P("head"),
            P("head"),
            P("seq"),
            P("seq"),
            P("seq", "head"),
        ),
        out_specs=(P("seq", "head"), P("seq", "head")),
        check_vma=False,
    )
```

time: 744 us -> 849 us (1.14); the launches traced: 733 us -> 847 us
  Pallas kernels: 0 us -> 529 us
  waiting for transfers between devices: 310 us -> 121 us
  starting transfers between devices: 176 us -> 72.4 us
  local copies, waits for them, and re-layouts: 108 us -> 31.8 us
  other arithmetic: 92.8 us -> 17.3 us
  blocking collectives: 2.45 us -> 74.9 us
  matrix products: 41.3 us -> 0 us
    pallas_call x0 -> x24, Pallas kernels: none -> 529 us  [the longest x8 461 us: gathered(): pl.pallas_call(functools.partial(gather_kernel, widths), in_specs=[pl.Blo...]
    ppermute x36 -> x0, waiting for transfers between devices: 250 us -> none  [passed_along(): return lax.ppermute(block, axis, route)]
    ppermute x36 -> x0, starting transfers between devices: 140 us -> none  [passed_along(): return lax.ppermute(block, axis, route)]
    all_to_all x4 -> x11, waiting for transfers between devices: 60.2 us -> 121 us  [the longest x3 91 us: moved(): lax.all_to_all(outgoing, 'seq', split_axis=0, concat_axis=0, tiled=True)]
    convert_element_type x13 -> x0, local copies, waits for them, and re-layouts: 42.2 us -> none  [the longest x2 13.9 us: shards(): grad_scan = scan_block(to_scan(grad_combined), out_map_scan, in_map_scan,...]
    dot_general x16 -> x0, matrix products: 41.3 us -> none  [the longest x4 18.3 us: scan_block(): jnp.einsum('ghcjn,cjghp->ghcnp', scaled_keys, value_blocks, preferred_ele...]
    all_to_all x0 -> x1, blocking collectives: none -> 41.2 us  [moved(): lax.all_to_all(outgoing, 'seq', split_axis=0, concat_axis=0, tiled=True)]
    all_to_all x4 -> x11, starting transfers between devices: 36 us -> 72.4 us  [the longest x4 30.2 us: carried(): lax.all_to_all(composed, 'seq', split_axis=0, concat_axis=0, tiled=True)]
  transfers between devices with their start and end apart: 40 -> 11, of which waited for: 18 -> 8; matrix products, arithmetic and copies ran while one was open for 22% -> 1% of each run, Pallas kernels for 0% -> 19%
where the time goes in v1:
time: 849 us; the launch traced here: 847 us
  Pallas kernels  529 us (62%)
  waiting for transfers between devices  121 us (14%)
  blocking collectives  74.9 us (9%)
  starting transfers between devices  72.4 us (9%)
  local copies, waits for them, and re-layouts  31.8 us (4%)
  other arithmetic  17.3 us (2%)
    pallas_call x8, Pallas kernels, gathered(): pl.pallas_call(functools.partial(gather_kernel, widths), in_specs=[pl.Blo...  461 us
    all_to_all x3, waiting for transfers between devices, moved(): lax.all_to_all(outgoing, 'seq', split_axis=0, concat_axis=0, tiled=True)  91 us
    pallas_call x12, Pallas kernels, call(): pl.pallas_call(functools.partial(body, self.reverse, self.spans), grid=(s...  60.7 us
    all_to_all x1, blocking collectives, moved(): lax.all_to_all(outgoing, 'seq', split_axis=0, concat_axis=0, tiled=True)  41.2 us
    all_gather x1, blocking collectives, shards(): all_sums = lax.all_gather(sums, 'seq', axis=0)  31.2 us
    all_to_all x4, starting transfers between devices, carried(): lax.all_to_all(composed, 'seq', split_axis=0, concat_axis=0, tiled=True)  30.2 us
    unnamed x80, local copies, waits for them, and re-layouts  26.9 us
    all_to_all x4, starting transfers between devices, carried(): lax.all_to_all(pieces, 'seq', split_axis=0, concat_axis=0, tiled=True)  21.1 us
  transfers between devices with their start and end apart: 11, of which 8 were waited for; matrix products, arithmetic and copies ran while one was open for 1% of the time, Pallas kernels for 19%

profile of v1, /device:TPU:12, one launch (start us, length us, event | category | flops | bytes accessed | tf_op | source)
XLA Modules:
  0.0 847.2 jit_solution(7718166087508163251)
XLA Ops:
  2.0 81.6 %shard_map.117 = bf16[16,32,2560]{2,1,0:T(8,128)(2,1)} custom-call(s32[16]{0:T(128)} %select_reduce_fusion.index_ref, bf16[16,32,1536]{2,1,0:T(8,128)(2,1)} %bitcast.49, bf16[16,32,512]{2,1,0:T(8,128)(2,1)} %bitcast.56, bf16[16,32,512]{2,1,0:T(8,128)(2,1)} %bitcast.55), custom_call_target="tpu_custom_call" | custom-call | tf_op jit(solution)/shard_map/pallas_call | solution.py:239
  83.6 7.2 all-to-all-start.2
  91.4 58.6 %all-to-all-done.2.refs_0_ = bf16[16,32,2560]{2,1,0:T(8,128)(2,1)S(1)} async-done(((bf16[16,32,2560]{2,1,0:T(8,128)(2,1)}), bf16[16,32,2560]{2,1,0:T(8,128)(2,1)S(1)}, u32[]{:S(2)}, u32[]{:S(2)}) %all-to-all-start.2) | async-done | bytes 2621472 | tf_op jit(solution)/shard_map/all_to_all | solution.py:282
  150.0 1.5 copy-done.30
  151.5 81.3 %shard_map.118 = bf16[16,32,2560]{2,1,0:T(8,128)(2,1)} custom-call(s32[16]{0:T(128)} %and_select_fusion.index_ref, bf16[16,32,2560]{2,1,0:T(8,128)(2,1)} %copy-done.30), custom_call_target="tpu_custom_call" | custom-call | tf_op jit(solution)/shard_map/pallas_call | solution.py:239
  232.8 1.7 copy-done
  234.6 5.5 shard_map.120
  241.2 5.2 all-to-all-start.3
  246.5 1.4 copy-done.2
  247.9 5.4 shard_map.114
  254.4 2.3 all-to-all-done.3.arrived_ref
  256.8 5.2 all-to-all-start
  262.8 31.2 %all-gather.1 = f32[16,2,24]{2,1,0:T(2,128)S(1)} all-gather(f32[1,2,24]{2,1,0:T(2,128)S(1)} %bitcast.67), channel_id=2, replica_groups=mesh['seq'=16,'head'=2] {'seq'}, dimensions={0}, use_global_device_ids=true | all-gather | bytes 3264 | tf_op jit(solution)/shard_map/all_gather | solution.py:296
  295.0 1.9 reshape.98
  296.8 1.9 fusion.7
  298.7 1.8 shard_map.121
  300.6 13.3 %all-to-all-start.4 = ((bf16[16,8,1536]{2,1,0:T(8,128)(2,1)}), bf16[16,8,1536]{2,1,0:T(8,128)(2,1)S(1)}, u32[]{:S(2)}, u32[]{:S(2)}) async-start(bf16[16,8,1536]{2,1,0:T(8,128)(2,1)} %shard_map.121), calls=%async_computation.4 | async-start | bytes 786432 | tf_op jit(solution)/shard_map/all_to_all | solution.py:213
  313.8 1.9 shard_map.115
  315.7 8.9 %all-to-all-done.4 = bf16[16,8,1536]{2,1,0:T(8,128)(2,1)S(1)} async-done(((bf16[16,8,1536]{2,1,0:T(8,128)(2,1)}), bf16[16,8,1536]{2,1,0:T(8,128)(2,1)S(1)}, u32[]{:S(2)}, u32[]{:S(2)}) %all-to-all-start.4) | async-done | bytes 393248 | tf_op jit(solution)/shard_map/all_to_all | solution.py:213
  324.6 5.9 all-to-all-start.1
  331.2 5.2 shard_map.119.inner_ref
  336.5 1.6 copy-done.10
  338.1 4.7 shard_map.122
  344.0 49.7 %shard_map.123 = bf16[16,32,1536]{2,1,0:T(8,128)(2,1)} custom-call(s32[16]{0:T(128)} %select_reduce_fusion.1.index_ref, bf16[16,32,1536]{2,1,0:T(8,128)(2,1)} %bitcast.54), custom_call_target="tpu_custom_call" | custom-call | tf_op jit(solution)/shard_map/pallas_call | solution.py:239
  393.7 6.9 all-to-all-start.5
  400.8 1.4 copy-done.3
  403.2 5.1 shard_map.113.inner_ref
  408.4 1.6 copy-done.19
  410.0 4.7 shard_map.116
  414.7 1.2 copy-done.9
  415.8 9.6 %all-to-all-done.5.refs_0_ = bf16[16,32,1536]{2,1,0:T(8,128)(2,1)} async-done(((bf16[16,32,1536]{2,1,0:T(8,128)(2,1)}), bf16[16,32,1536]{2,1,0:T(8,128)(2,1)}, u32[]{:S(2)}, u32[]{:S(2)}) %all-to-all-start.5) | async-done | bytes 1572896 | tf_op jit(solution)/shard_map/all_to_all | solution.py:282
  425.5 49.6 %shard_map.124 = bf16[16,32,1536]{2,1,0:T(8,128)(2,1)} custom-call(s32[16]{0:T(128)} %copy-done.36, bf16[16,32,1536]{2,1,0:T(8,128)(2,1)} %all-to-all-done.5.refs_0_), custom_call_target="tpu_custom_call" | custom-call | tf_op jit(solution)/shard_map/pallas_call | solution.py:239
  475.0 4.2 multiply_reduce_fusion.1
  479.2 2.5 psum.7
  481.7 6.0 subtract_convert_fusion
  487.7 49.6 %shard_map.129 = bf16[16,32,1536]{2,1,0:T(8,128)(2,1)} custom-call(s32[16]{0:T(128)} %select_reduce_fusion.index_ref, bf16[16,32,1536]{2,1,0:T(8,128)(2,1)} %bitcast.50), custom_call_target="tpu_custom_call" | custom-call | tf_op jit(solution)/shard_map/pallas_call | solution.py:239
  537.3 41.2 %all_to_all.60.refs_0_ = bf16[16,32,1536]{2,1,0:T(8,128)(2,1)} all-to-all(bf16[16,32,1536]{2,1,0:T(8,128)(2,1)} %shard_map.129), channel_id=1, replica_groups=mesh['seq'=16,'head'=2] {'seq'}, dimensions={0} | all-to-all | bytes 3145728 | tf_op jit(solution)/shard_map/all_to_all | solution.py:282
  578.6 49.6 %shard_map.130 = bf16[16,32,1536]{2,1,0:T(8,128)(2,1)} custom-call(s32[16]{0:T(128)} %and_select_fusion.index_ref, bf16[16,32,1536]{2,1,0:T(8,128)(2,1)} %all_to_all.60.refs_0_), custom_call_target="tpu_custom_call" | custom-call | tf_op jit(solution)/shard_map/pallas_call | solution.py:239
  628.1 1.4 copy-done.7
  629.5 4.8 shard_map.132
  634.4 1.2 copy-done.26
  636.3 5.3 all-to-all-start.9
  641.5 1.4 copy-done.4
  642.9 4.8 shard_map.126
  649.6 2.8 all-to-all-done.9.arrived_ref
  652.4 5.5 all-to-all-start.6
  657.9 1.9 shard_map.133
  659.7 8.1 all-to-all-done.6.arrived_ref
  667.8 5.5 all-to-all-start.10
  673.3 1.8 shard_map.127
  675.2 8.0 all-to-all-done.10
  683.1 5.5 all-to-all-start.7
  688.6 1.4 copy-done.8
  690.1 5.9 shard_map.131.inner_ref
  696.0 4.7 shard_map.134
  700.7 1.2 copy-done.12
  701.9 49.7 %shard_map.135 = bf16[16,32,1536]{2,1,0:T(8,128)(2,1)} custom-call(s32[16]{0:T(128)} %select_reduce_fusion.1.index_ref, bf16[16,32,1536]{2,1,0:T(8,128)(2,1)} %bitcast.53), custom_call_target="tpu_custom_call" | custom-call | tf_op jit(solution)/shard_map/pallas_call | solution.py:239
  751.6 7.0 all-to-all-start.11
  758.6 5.1 shard_map.125.inner_ref
  763.7 1.6 copy-done.18
  765.3 4.7 shard_map.128
  771.2 22.7 %all-to-all-done.11.refs_0_ = bf16[16,32,1536]{2,1,0:T(8,128)(2,1)} async-done(((bf16[16,32,1536]{2,1,0:T(8,128)(2,1)}), bf16[16,32,1536]{2,1,0:T(8,128)(2,1)}, u32[]{:S(2)}, u32[]{:S(2)}) %all-to-all-start.11) | async-done | bytes 1572896 | tf_op jit(solution)/shard_map/all_to_all | solution.py:282
  794.0 49.6 %shard_map.136 = bf16[16,32,1536]{2,1,0:T(8,128)(2,1)} custom-call(s32[16]{0:T(128)} %copy-done.36, bf16[16,32,1536]{2,1,0:T(8,128)(2,1)} %all-to-all-done.11.refs_0_), custom_call_target="tpu_custom_call" | custom-call | tf_op jit(solution)/shard_map/pallas_call | solution.py:239
  843.5 3.7 fusion.1
  (86 shorter events, 12.9 us)
Async XLA Ops:
  1.3 82.3 %copy-start.36 = (s32[16]{0:T(128)}, s32[16]{0:T(128)S(1)}, u32[]{:S(2)}) copy-start(s32[16]{0:T(128)S(1)} %and_select_fusion.1.index_ref) | copy-start | bytes 196
  83.6 7.2 copy-start.33
  83.6 7.3 copy-start.39
  83.6 66.4 %all-to-all-start.2 = ((bf16[16,32,2560]{2,1,0:T(8,128)(2,1)}), bf16[16,32,2560]{2,1,0:T(8,128)(2,1)S(1)}, u32[]{:S(2)}, u32[]{:S(2)}) async-start(bf16[16,32,2560]{2,1,0:T(8,128)(2,1)} %shard_map.117), calls=%async_computation.2 | async-start | bytes 5242880 | tf_op jit(solution)/shard_map/all_to_all | solution.py:282
  150.0 1.5 copy-start.30
  232.8 1.7 copy-start
  234.6 11.8 %copy-start.34 = (bf16[24,512]{1,0:T(8,128)(2,1)S(1)}, bf16[24,512]{1,0:T(8,128)(2,1)}, u32[]{:S(2)}) copy-start(bf16[24,512]{1,0:T(8,128)(2,1)} %param.13) | copy-start | bytes 73732
  234.6 11.9 %copy-start.15 = (bf16[512,512]{1,0:T(8,128)(2,1)S(1)}, bf16[512,512]{1,0:T(8,128)(2,1)}, u32[]{:S(2)}) copy-start(bf16[512,512]{1,0:T(8,128)(2,1)} %q_ref.7) | copy-start | bytes 1572868
  240.1 1.1 copy-start.22
  241.2 15.6 %all-to-all-start.3 = ((bf16[16,8,1536]{2,1,0:T(8,128)(2,1)}), bf16[16,8,1536]{2,1,0:T(8,128)(2,1)S(1)}, u32[]{:S(2)}, u32[]{:S(2)}) async-start(bf16[16,8,1536]{2,1,0:T(8,128)(2,1)} %bitcast.9), calls=%async_computation.3 | async-start | bytes 786432 | tf_op jit(solution)/shard_map/all_to_all | solution.py:208
  246.4 1.4 copy-start.2
  253.3 1.2 copy-start.20
  254.4 76.1 %copy-start.37 = (s32[16]{0:T(128)S(1)}, s32[16]{0:T(128)}, u32[]{:S(2)}) copy-start(s32[16]{0:T(128)} %and_select_fusion.index_ref) | copy-start | bytes 196
  254.4 76.8 %copy-start.1 = (bf16[16,32,2560]{2,1,0:T(8,128)(2,1)S(1)}, bf16[16,32,2560]{2,1,0:T(8,128)(2,1)}, u32[]{:S(2)}) copy-start(bf16[16,32,2560]{2,1,0:T(8,128)(2,1)} %shard_map.118) | copy-start | bytes 7864324
  256.8 41.9 %copy-start.31 = (bf16[16,8,1536]{2,1,0:T(8,128)(2,1)}, bf16[16,8,1536]{2,1,0:T(8,128)(2,1)S(1)}, u32[]{:S(2)}) copy-start(bf16[16,8,1536]{2,1,0:T(8,128)(2,1)S(1)} %all-to-all-done.3.arrived_ref) | copy-start | bytes 1179652
  256.8 43.8 %all-to-all-start = ((bf16[16,8,1536]{2,1,0:T(8,128)(2,1)}), bf16[16,8,1536]{2,1,0:T(8,128)(2,1)S(1)}, u32[]{:S(2)}, u32[]{:S(2)}) async-start(bf16[16,8,1536]{2,1,0:T(8,128)(2,1)} %bitcast), calls=%async_computation | async-start | bytes 786432 | tf_op jit(solution)/shard_map/all_to_all | solution.py:208
  300.6 13.3 %copy-start.32 = (bf16[16,8,1536]{2,1,0:T(8,128)(2,1)}, bf16[16,8,1536]{2,1,0:T(8,128)(2,1)S(1)}, u32[]{:S(2)}) copy-start(bf16[16,8,1536]{2,1,0:T(8,128)(2,1)S(1)} %all-to-all-done.arrived_ref) | copy-start | bytes 1179652
  300.6 24.0 %all-to-all-start.4 = ((bf16[16,8,1536]{2,1,0:T(8,128)(2,1)}), bf16[16,8,1536]{2,1,0:T(8,128)(2,1)S(1)}, u32[]{:S(2)}, u32[]{:S(2)}) async-start(bf16[16,8,1536]{2,1,0:T(8,128)(2,1)} %shard_map.121), calls=%async_computation.4 | async-start | bytes 786432 | tf_op jit(solution)/shard_map/all_to_all | solution.py:213
  324.6 69.1 %all-to-all-start.1 = ((bf16[16,8,1536]{2,1,0:T(8,128)(2,1)}), bf16[16,8,1536]{2,1,0:T(8,128)(2,1)}, u32[]{:S(2)}, u32[]{:S(2)}) async-start(bf16[16,8,1536]{2,1,0:T(8,128)(2,1)} %shard_map.115), calls=%async_computation.1 | async-start | bytes 786432 | tf_op jit(solution)/shard_map/all_to_all | solution.py:213
  331.2 6.9 copy-start.23
  336.5 1.6 copy-start.10
  342.8 1.1 copy-start.13
  344.0 56.6 %copy-start.38 = (f32[24]{0:T(128)S(1)}, f32[24]{0:T(128)}, u32[]{:S(2)}) copy-start(f32[24]{0:T(128)} %param.15) | copy-start | bytes 292
  344.0 56.8 %copy-start.14 = (bf16[512,512]{1,0:T(8,128)(2,1)S(1)}, bf16[512,512]{1,0:T(8,128)(2,1)}, u32[]{:S(2)}) copy-start(bf16[512,512]{1,0:T(8,128)(2,1)} %k_ref.7) | copy-start | bytes 1572868
  393.7 31.8 %all-to-all-start.5 = ((bf16[16,32,1536]{2,1,0:T(8,128)(2,1)}), bf16[16,32,1536]{2,1,0:T(8,128)(2,1)}, u32[]{:S(2)}, u32[]{:S(2)}) async-start(bf16[16,32,1536]{2,1,0:T(8,128)(2,1)} %shard_map.123), calls=%async_computation.5 | async-start | bytes 3145728 | tf_op jit(solution)/shard_map/all_to_all | solution.py:282
  400.8 1.4 copy-start.3
  402.2 1.0 copy-start.16
  403.2 6.7 copy-start.21
  408.3 1.6 copy-start.19
  414.6 1.2 copy-start.9
  415.8 59.2 %copy-start.35 = (f32[1536]{0:T(1024)S(1)}, f32[1536]{0:T(1024)}, u32[]{:S(2)}) copy-start(f32[1536]{0:T(1024)} %param.16) | copy-start | bytes 18436
  628.1 1.4 copy-start.7
  634.3 1.2 copy-start.26
  635.5 0.8 copy-start.29
  636.3 16.1 %all-to-all-start.9 = ((bf16[16,8,1536]{2,1,0:T(8,128)(2,1)}), bf16[16,8,1536]{2,1,0:T(8,128)(2,1)}, u32[]{:S(2)}, u32[]{:S(2)}) async-start(bf16[16,8,1536]{2,1,0:T(8,128)(2,1)} %bitcast.59), calls=%async_computation.9 | async-start | bytes 786432 | tf_op jit(solution)/shard_map/all_to_all | solution.py:208
  641.5 1.4 copy-start.4
  647.7 1.1 copy-start.24
  648.9 0.7 copy-start.28
  652.4 15.5 %all-to-all-start.6 = ((bf16[16,8,1536]{2,1,0:T(8,128)(2,1)}), bf16[16,8,1536]{2,1,0:T(8,128)(2,1)}, u32[]{:S(2)}, u32[]{:S(2)}) async-start(bf16[16,8,1536]{2,1,0:T(8,128)(2,1)} %bitcast.58), calls=%async_computation.6 | async-start | bytes 786432 | tf_op jit(solution)/shard_map/all_to_all | solution.py:208
  667.8 15.3 %all-to-all-start.10 = ((bf16[16,8,1536]{2,1,0:T(8,128)(2,1)}), bf16[16,8,1536]{2,1,0:T(8,128)(2,1)}, u32[]{:S(2)}, u32[]{:S(2)}) async-start(bf16[16,8,1536]{2,1,0:T(8,128)(2,1)} %shard_map.133), calls=%async_computation.10 | async-start | bytes 786432 | tf_op jit(solution)/shard_map/all_to_all | solution.py:213
  683.1 68.4 %all-to-all-start.7 = ((bf16[16,8,1536]{2,1,0:T(8,128)(2,1)}), bf16[16,8,1536]{2,1,0:T(8,128)(2,1)}, u32[]{:S(2)}, u32[]{:S(2)}) async-start(bf16[16,8,1536]{2,1,0:T(8,128)(2,1)} %shard_map.127), calls=%async_computation.7 | async-start | bytes 786432 | tf_op jit(solution)/shard_map/all_to_all | solution.py:213
  688.6 1.4 copy-start.8
  690.1 5.9 copy-start.27
  700.7 1.2 copy-start.12
  701.9 56.7 %copy-start.5 = (bf16[512,1536]{1,0:T(8,128)(2,1)S(1)}, bf16[512,1536]{1,0:T(8,128)(2,1)}, u32[]{:S(2)}) copy-start(bf16[512,1536]{1,0:T(8,128)(2,1)} %get-tuple-element.20.v_ref) | copy-start | bytes 4718596
  701.9 56.7 %copy-start.17 = (bf16[512,512]{1,0:T(8,128)(2,1)S(1)}, bf16[512,512]{1,0:T(8,128)(2,1)}, u32[]{:S(2)}) copy-start(bf16[512,512]{1,0:T(8,128)(2,1)} %q_ref.7) | copy-start | bytes 1572868
  751.6 42.4 %all-to-all-start.11 = ((bf16[16,32,1536]{2,1,0:T(8,128)(2,1)}), bf16[16,32,1536]{2,1,0:T(8,128)(2,1)}, u32[]{:S(2)}, u32[]{:S(2)}) async-start(bf16[16,32,1536]{2,1,0:T(8,128)(2,1)} %shard_map.135), calls=%async_computation.11 | async-start | bytes 3145728 | tf_op jit(solution)/shard_map/all_to_all | solution.py:282
  758.6 6.8 copy-start.25
  763.7 1.6 copy-start.18
  770.1 1.1 copy-start.11
  771.2 72.3 %copy-start.6 = (bf16[512,1536]{1,0:T(8,128)(2,1)S(1)}, bf16[512,1536]{1,0:T(8,128)(2,1)}, u32[]{:S(2)}) copy-start(bf16[512,1536]{1,0:T(8,128)(2,1)} %get-tuple-element.20.v_ref) | copy-start | bytes 4718596

commit v2 on v1

--- a/solution.py
+++ b/solution.py
@@ -215,33 +215,26 @@
 
 
 def gather_kernel(counts, index_ref, *refs):
-    sources, out_ref, sems = refs[: len(counts)], refs[-2], refs[-1]
-    copies = []
-    for unit in range(out_ref.shape[0]):
+    sources, out_ref = refs[: len(counts)], refs[-1]
+
+    @pl.loop(0, out_ref.shape[0])
+    def _(unit):
         first = 0
-        for place, (source, width) in enumerate(zip(sources, counts)):
-            copy = pltpu.make_async_copy(
-                source.at[index_ref[unit]],
-                out_ref.at[unit, :, pl.ds(first, width)],
-                sems.at[unit, place],
-            )
-            copy.start()
-            copies.append(copy)
+        for source, width in zip(sources, counts):
+            out_ref[unit, :, first : first + width] = source[index_ref[unit]]
             first += width
-    for copy in copies:
-        copy.wait()
 
 
 def gathered(arrays, index):
     widths = tuple(array.shape[2] for array in arrays)
     units, rows = arrays[0].shape[:2]
-    hbm = pl.BlockSpec(memory_space=pl.ANY)
+    whole = pl.BlockSpec(memory_space=pltpu.VMEM)
     return pl.pallas_call(
         functools.partial(gather_kernel, widths),
-        in_specs=[pl.BlockSpec(memory_space=pltpu.SMEM)] + [hbm] * len(arrays),
-        out_specs=hbm,
+        in_specs=[pl.BlockSpec(memory_space=pltpu.SMEM)] + [whole] * len(arrays),
+        out_specs=whole,
         out_shape=jax.ShapeDtypeStruct((units, rows, sum(widths)), arrays[0].dtype),
-        scratch_shapes=[pltpu.SemaphoreType.DMA((units, len(arrays)))],
+        compiler_params=pltpu.CompilerParams(vmem_limit_bytes=48 * 2**20),
     )(index, *arrays)
 
 
@@ -293,7 +286,8 @@
         return jnp.pad(wide, ((0, 0), (0, PAD - heads // groups), (0, 0)))
 
     sums = jnp.stack([decay_forward, decay_reverse]).astype(F32).sum(axis=2)
-    all_sums = lax.all_gather(sums, "seq", axis=0)
+    copies = jnp.broadcast_to(sums[None], (lax.axis_size("seq"), *sums.shape))
+    all_sums = lax.all_to_all(copies, "seq", split_axis=0, concat_axis=0, tiled=True)
     factors = jnp.repeat(jnp.exp(all_sums), HEAD_DIM, axis=2)
     forward_factors, reverse_factors = factors[:, 0:1], factors[:, 1:2]
     decay_f, decay_r = padded(decay_forward), padded(decay_reverse)

time: 849 us -> 379 us (0.45)
  Pallas kernels: 529 us -> 75 us
  blocking collectives: 74.9 us -> 43.3 us
  waiting for transfers between devices: 121 us -> 135 us
    pallas_call x8, Pallas kernels: 461 us -> 8 us  [gathered(): pl.pallas_call(functools.partial(gather_kernel, widths), in_specs=[pl.Blo...]
    all_gather x1 -> x0, blocking collectives: 31.2 us -> none  [shards(): all_sums = lax.all_gather(sums, 'seq', axis=0)]
    all_to_all x3, waiting for transfers between devices: 91 us -> 102 us  [moved(): lax.all_to_all(outgoing, 'seq', split_axis=0, concat_axis=0, tiled=True)]
    unnamed x80 -> x96, local copies, waits for them, and re-layouts: 26.9 us -> 36.2 us
    all_to_all x4, starting transfers between devices: 30.2 us -> 21.6 us  [carried(): lax.all_to_all(composed, 'seq', split_axis=0, concat_axis=0, tiled=True)]
  transfers between devices with their start and end apart: 11 -> 12, of which waited for: 8 -> 9; matrix products, arithmetic and copies ran while one was open for 1% -> 1% of each run, Pallas kernels for 19% -> 17%
where the time goes in v2:
time: 379 us; the launch traced here: 377 us
  waiting for transfers between devices  135 us (36%)
  Pallas kernels  75 us (20%)
  starting transfers between devices  71 us (19%)
  blocking collectives  43.3 us (11%)
  local copies, waits for them, and re-layouts  40 us (11%)
  other arithmetic  11.7 us (3%)
    all_to_all x3, waiting for transfers between devices, moved(): lax.all_to_all(outgoing, 'seq', split_axis=0, concat_axis=0, tiled=True)  102 us
    pallas_call x12, Pallas kernels, call(): pl.pallas_call(functools.partial(body, self.reverse, self.spans), grid=(s...  59.6 us
    all_to_all x1, blocking collectives, moved(): lax.all_to_all(outgoing, 'seq', split_axis=0, concat_axis=0, tiled=True)  40.9 us
    unnamed x96, local copies, waits for them, and re-layouts  36.2 us
    all_to_all x4, starting transfers between devices, carried(): lax.all_to_all(pieces, 'seq', split_axis=0, concat_axis=0, tiled=True)  22.8 us
    all_to_all x4, starting transfers between devices, carried(): lax.all_to_all(composed, 'seq', split_axis=0, concat_axis=0, tiled=True)  21.6 us
    all_to_all x3, starting transfers between devices, moved(): lax.all_to_all(outgoing, 'seq', split_axis=0, concat_axis=0, tiled=True)  21.4 us
    all_to_all x4, waiting for transfers between devices, carried(): lax.all_to_all(pieces, 'seq', split_axis=0, concat_axis=0, tiled=True)  17.1 us
  transfers between devices with their start and end apart: 12, of which 9 were waited for; matrix products, arithmetic and copies ran while one was open for 1% of the time, Pallas kernels for 17%

profile of v2, /device:TPU:12, one launch (start us, length us, event | category | flops | bytes accessed | tf_op | source)
XLA Modules:
  0.0 377.2 jit_solution(10356292981373971347)
XLA Ops:
  1.4 1.4 copy-done
  5.7 1.5 copy-done.16
  7.2 7.3 %all-to-all-start.3 = ((bf16[16,32,2560]{2,1,0:T(8,128)(2,1)}), bf16[16,32,2560]{2,1,0:T(8,128)(2,1)S(1)}, u32[]{:S(2)}, u32[]{:S(2)}) async-start(bf16[16,32,2560]{2,1,0:T(8,128)(2,1)} %copy-done.16), calls=%async_computation.3 | async-start | bytes 5242880 | tf_op jit(solution)/shard_map/all_to_all | solution.py:275
  14.6 59.0 %all-to-all-done.3.refs_0_ = bf16[16,32,2560]{2,1,0:T(8,128)(2,1)S(1)} async-done(((bf16[16,32,2560]{2,1,0:T(8,128)(2,1)}), bf16[16,32,2560]{2,1,0:T(8,128)(2,1)S(1)}, u32[]{:S(2)}, u32[]{:S(2)}) %all-to-all-start.3) | async-done | bytes 2621472 | tf_op jit(solution)/shard_map/all_to_all | solution.py:275
  73.7 1.5 copy-done.14
  75.7 5.2 %all-to-all-start.1 = ((f32[16,2,24]{2,1,0:T(2,128)}), f32[16,2,24]{2,1,0:T(2,128)S(1)}, u32[]{:S(2)}, u32[]{:S(2)}) async-start(f32[16,2,24]{2,1,0:T(2,128)} %broadcast_in_dim.24), calls=%async_computation.1 | async-start | bytes 32768 | tf_op jit(solution)/shard_map/all_to_all | solution.py:290
  80.9 1.7 copy-done.15
  83.5 4.9 %shard_map.120 = (f32[2,128,1536]{2,1,0:T(8,128)S(1)}, bf16[128,1536]{1,0:T(8,128)(2,1)S(1)}) custom-call(bf16[512,2560]{1,0:T(8,128)(2,1)S(1)} %bitcast.38, bf16[512,2560]{1,0:T(8,128)(2,1)S(1)} %bitcast.39, f32[4,8,512]{2,1,0:T(8,128)S(1)} %pad_convert_fusion.decay_ref), custom_call_target="tpu_custom_call" | custom-call | flops 201326592 | bytes 3932160 | tf_op jit(solution)/shard_map/pallas_call | solution.py:135
  88.4 1.1 copy-done.32
  90.3 6.9 %all-to-all-start.4 = ((bf16[16,8,1536]{2,1,0:T(8,128)(2,1)}), bf16[16,8,1536]{2,1,0:T(8,128)(2,1)}, u32[]{:S(2)}, u32[]{:S(2)}) async-start(bf16[16,8,1536]{2,1,0:T(8,128)(2,1)} %bitcast.58), calls=%async_computation.4 | async-start | bytes 786432 | tf_op jit(solution)/shard_map/all_to_all | solution.py:208
  97.3 1.4 copy-done.1
  98.7 4.8 %shard_map.114 = (f32[2,128,1536]{2,1,0:T(8,128)S(1)}, bf16[128,1536]{1,0:T(8,128)(2,1)S(1)}) custom-call(bf16[512,1536]{1,0:T(8,128)(2,1)S(1)} %copy-done.1, bf16[512,512]{1,0:T(8,128)(2,1)S(1)} %copy-done.24, f32[4,8,512]{2,1,0:T(8,128)S(1)} %pad_convert_fusion.1.decay_ref), custom_call_target="tpu_custom_call" | custom-call | flops 201326592 | bytes 3932160 | tf_op jit(solution)/shard_map/pallas_call | solution.py:135
  103.5 1.1 copy-done.30
  105.4 1.7 all-to-all-done.4.arrived_ref
  107.1 5.2 %all-to-all-start = ((bf16[16,8,1536]{2,1,0:T(8,128)(2,1)}), bf16[16,8,1536]{2,1,0:T(8,128)(2,1)S(1)}, u32[]{:S(2)}, u32[]{:S(2)}) async-start(bf16[16,8,1536]{2,1,0:T(8,128)(2,1)} %bitcast.57), calls=%async_computation | async-start | bytes 786432 | tf_op jit(solution)/shard_map/all_to_all | solution.py:208
  113.3 1.2 reshape.99
  115.3 1.8 shard_map.121
  117.1 5.2 %all-to-all-done.arrived_ref = bf16[16,8,1536]{2,1,0:T(8,128)(2,1)S(1)} async-done(((bf16[16,8,1536]{2,1,0:T(8,128)(2,1)}), bf16[16,8,1536]{2,1,0:T(8,128)(2,1)S(1)}, u32[]{:S(2)}, u32[]{:S(2)}) %all-to-all-start) | async-done | bytes 393248 | tf_op jit(solution)/shard_map/all_to_all | solution.py:208
  123.0 5.1 %all-to-all-start.5 = ((bf16[16,8,1536]{2,1,0:T(8,128)(2,1)}), bf16[16,8,1536]{2,1,0:T(8,128)(2,1)S(1)}, u32[]{:S(2)}, u32[]{:S(2)}) async-start(bf16[16,8,1536]{2,1,0:T(8,128)(2,1)} %shard_map.121), calls=%async_computation.5 | async-start | bytes 786432 | tf_op jit(solution)/shard_map/all_to_all | solution.py:213
  128.1 1.9 shard_map.115
  129.9 8.2 %all-to-all-done.5 = bf16[16,8,1536]{2,1,0:T(8,128)(2,1)S(1)} async-done(((bf16[16,8,1536]{2,1,0:T(8,128)(2,1)}), bf16[16,8,1536]{2,1,0:T(8,128)(2,1)S(1)}, u32[]{:S(2)}, u32[]{:S(2)}) %all-to-all-start.5) | async-done | bytes 393248 | tf_op jit(solution)/shard_map/all_to_all | solution.py:213
  138.2 5.5 %all-to-all-start.2 = ((bf16[16,8,1536]{2,1,0:T(8,128)(2,1)}), bf16[16,8,1536]{2,1,0:T(8,128)(2,1)}, u32[]{:S(2)}, u32[]{:S(2)}) async-start(bf16[16,8,1536]{2,1,0:T(8,128)(2,1)} %shard_map.115), calls=%async_computation.2 | async-start | bytes 786432 | tf_op jit(solution)/shard_map/all_to_all | solution.py:213
  143.8 5.3 %shard_map.119.inner_ref = f32[512,1536]{1,0:T(8,128)S(1)} custom-call(bf16[512,2560]{1,0:T(8,128)(2,1)S(1)} %bitcast.40, bf16[512,2560]{1,0:T(8,128)(2,1)S(1)} %bitcast.41, bf16[512,2560]{1,0:T(8,128)(2,1)S(1)} %bitcast.42, f32[4,8,512]{2,1,0:T(8,128)S(1)} %pad_convert_fusion.decay_ref), custom_call_target="tpu_custom_call" | custom-call | flops 1610612736 | bytes 6291456 | tf_op jit(solution)/shard_map/pallas_call | solution.py:135
  149.1 1.6 copy-done.13
  150.7 4.7 %shard_map.122 = bf16[512,1536]{1,0:T(8,128)(2,1)S(1)} custom-call(f32[512,1536]{1,0:T(8,128)} %copy-done.13, bf16[512,2560]{1,0:T(8,128)(2,1)S(1)} %bitcast.43, f32[4,8,512]{2,1,0:T(8,128)S(1)} %pad_convert_fusion.decay_ref, f32[2,128,1536]{2,1,0:T(8,128)S(1)} %copy-done.33, bf16[128,1536]{1,0:T(8,128)(2,1)S(1)} %bitcast.56), custom_call_target="tpu_custom_call" | custom-call | flops 201326592 | bytes 3145728 | tf_op jit(solution)/shard_map/pallas_call | solution.py:135
  156.2 1.1 copy-done.19
  157.4 7.0 %all-to-all-start.6 = ((bf16[16,32,1536]{2,1,0:T(8,128)(2,1)}), bf16[16,32,1536]{2,1,0:T(8,128)(2,1)}, u32[]{:S(2)}, u32[]{:S(2)}) async-start(bf16[16,32,1536]{2,1,0:T(8,128)(2,1)} %copy-done.19), calls=%async_computation.6 | async-start | bytes 3145728 | tf_op jit(solution)/shard_map/all_to_all | solution.py:275
  164.5 1.4 copy-done.2
  166.9 5.1 %shard_map.113.inner_ref = f32[512,1536]{1,0:T(8,128)S(1)} custom-call(bf16[512,1536]{1,0:T(8,128)(2,1)S(1)} %copy-done.2, bf16[512,512]{1,0:T(8,128)(2,1)S(1)} %copy-done.25, bf16[512,512]{1,0:T(8,128)(2,1)S(1)} %copy-done.22, f32[4,8,512]{2,1,0:T(8,128)S(1)} %pad_convert_fusion.1.decay_ref), custom_call_target="tpu_custom_call" | custom-call | flops 1610612736 | bytes 6291456 | tf_op jit(solution)/shard_map/pallas_call | solution.py:135
  172.1 1.6 copy-done.29
  173.7 4.7 %shard_map.116 = bf16[512,1536]{1,0:T(8,128)(2,1)S(1)} custom-call(f32[512,1536]{1,0:T(8,128)} %copy-done.29, bf16[512,512]{1,0:T(8,128)(2,1)S(1)} %copy-done.22, f32[4,8,512]{2,1,0:T(8,128)S(1)} %pad_convert_fusion.1.decay_ref, f32[2,128,1536]{2,1,0:T(8,128)S(1)} %copy-done.31, bf16[128,1536]{1,0:T(8,128)(2,1)} %bitcast.3.incoming_ref), custom_call_target="tpu_custom_call" | custom-call | flops 201326592 | bytes 3145728 | tf_op jit(solution)/shard_map/pallas_call | solution.py:135
  179.5 20.2 %all-to-all-done.6.refs_0_ = bf16[16,32,1536]{2,1,0:T(8,128)(2,1)} async-done(((bf16[16,32,1536]{2,1,0:T(8,128)(2,1)}), bf16[16,32,1536]{2,1,0:T(8,128)(2,1)}, u32[]{:S(2)}, u32[]{:S(2)}) %all-to-all-start.6) | async-done | bytes 1572896 | tf_op jit(solution)/shard_map/all_to_all | solution.py:275
  199.7 1.8 shard_map.124
  202.0 3.3 multiply_reduce_fusion.1
  205.4 2.5 psum.7
  207.9 5.5 %subtract_convert_fusion = (bf16[512,1536]{1,0:T(8,128)(2,1)S(1)}, bf16[512,1536]{1,0:T(8,128)(2,1)}) fusion(bf16[512,1536]{1,0:T(8,128)(2,1)} %param.19, f32[512]{0:T(512)S(1)} %fusion.4, f32[512]{0:T(512)S(1)} %bitcast.64, f32[1536]{0:T(1024)S(1)} %copy-done.45, bf16[512,1536]{1,0:T(8,128)(2,1)} %v_ref.3, f32[1536]{0:T(1024)S(1)} %mul.65, ...), kind=kLoop, calls=%fused_computation.5 | loop fusion | flops 11796480 | bytes 9453568 | tf_op jit(solution)/shard_map/convert_element_type | solution.py:321
  215.2 40.9 %all_to_all.65.refs_0_ = bf16[16,32,1536]{2,1,0:T(8,128)(2,1)S(1)} all-to-all(bf16[16,32,1536]{2,1,0:T(8,128)(2,1)S(1)} %shard_map.129), channel_id=1, replica_groups=mesh['seq'=16,'head'=2] {'seq'}, dimensions={0} | all-to-all | bytes 3145728 | tf_op jit(solution)/shard_map/all_to_all | solution.py:275
  256.8 4.8 %shard_map.132 = (f32[2,128,1536]{2,1,0:T(8,128)S(1)}, bf16[128,1536]{1,0:T(8,128)(2,1)S(1)}) custom-call(bf16[512,1536]{1,0:T(8,128)(2,1)S(1)} %bitcast.50, bf16[512,2560]{1,0:T(8,128)(2,1)S(1)} %bitcast.44, f32[4,8,512]{2,1,0:T(8,128)S(1)} %pad_convert_fusion.decay_ref), custom_call_target="tpu_custom_call" | custom-call | flops 201326592 | bytes 3932160 | tf_op jit(solution)/shard_map/pallas_call | solution.py:135
  261.6 1.2 copy-done.8
  262.8 1.2 copy-done.36
  264.7 5.2 %all-to-all-start.10 = ((bf16[16,8,1536]{2,1,0:T(8,128)(2,1)}), bf16[16,8,1536]{2,1,0:T(8,128)(2,1)}, u32[]{:S(2)}, u32[]{:S(2)}) async-start(bf16[16,8,1536]{2,1,0:T(8,128)(2,1)} %bitcast.60), calls=%async_computation.10 | async-start | bytes 786432 | tf_op jit(solution)/shard_map/all_to_all | solution.py:208
  270.0 1.4 copy-done.5
  271.4 4.8 %shard_map.126 = (f32[2,128,1536]{2,1,0:T(8,128)S(1)}, bf16[128,1536]{1,0:T(8,128)(2,1)S(1)}) custom-call(bf16[512,1536]{1,0:T(8,128)(2,1)S(1)} %copy-done.5, bf16[512,512]{1,0:T(8,128)(2,1)S(1)} %copy-done.22, f32[4,8,512]{2,1,0:T(8,128)S(1)} %pad_convert_fusion.1.decay_ref), custom_call_target="tpu_custom_call" | custom-call | flops 201326592 | bytes 3932160 | tf_op jit(solution)/shard_map/pallas_call | solution.py:135
  276.2 1.2 copy-done.34
  278.1 2.3 all-to-all-done.10.arrived_ref
  280.4 5.5 %all-to-all-start.7 = ((bf16[16,8,1536]{2,1,0:T(8,128)(2,1)}), bf16[16,8,1536]{2,1,0:T(8,128)(2,1)}, u32[]{:S(2)}, u32[]{:S(2)}) async-start(bf16[16,8,1536]{2,1,0:T(8,128)(2,1)} %bitcast.59), calls=%async_computation.7 | async-start | bytes 786432 | tf_op jit(solution)/shard_map/all_to_all | solution.py:208
  285.9 1.9 shard_map.133
  287.7 7.9 %all-to-all-done.7.arrived_ref = bf16[16,8,1536]{2,1,0:T(8,128)(2,1)} async-done(((bf16[16,8,1536]{2,1,0:T(8,128)(2,1)}), bf16[16,8,1536]{2,1,0:T(8,128)(2,1)}, u32[]{:S(2)}, u32[]{:S(2)}) %all-to-all-start.7) | async-done | bytes 393248 | tf_op jit(solution)/shard_map/all_to_all | solution.py:208
  295.7 5.5 %all-to-all-start.11 = ((bf16[16,8,1536]{2,1,0:T(8,128)(2,1)}), bf16[16,8,1536]{2,1,0:T(8,128)(2,1)}, u32[]{:S(2)}, u32[]{:S(2)}) async-start(bf16[16,8,1536]{2,1,0:T(8,128)(2,1)} %shard_map.133), calls=%async_computation.11 | async-start | bytes 786432 | tf_op jit(solution)/shard_map/all_to_all | solution.py:213
  301.2 1.9 shard_map.127
  303.0 8.0 %all-to-all-done.11 = bf16[16,8,1536]{2,1,0:T(8,128)(2,1)} async-done(((bf16[16,8,1536]{2,1,0:T(8,128)(2,1)}), bf16[16,8,1536]{2,1,0:T(8,128)(2,1)}, u32[]{:S(2)}, u32[]{:S(2)}) %all-to-all-start.11) | async-done | bytes 393248 | tf_op jit(solution)/shard_map/all_to_all | solution.py:213
  311.0 5.5 %all-to-all-start.8 = ((bf16[16,8,1536]{2,1,0:T(8,128)(2,1)}), bf16[16,8,1536]{2,1,0:T(8,128)(2,1)}, u32[]{:S(2)}, u32[]{:S(2)}) async-start(bf16[16,8,1536]{2,1,0:T(8,128)(2,1)} %shard_map.127), calls=%async_computation.8 | async-start | bytes 786432 | tf_op jit(solution)/shard_map/all_to_all | solution.py:213
  316.5 1.4 copy-done.9
  317.9 5.9 %shard_map.131.inner_ref = f32[512,1536]{1,0:T(8,128)} custom-call(bf16[512,1536]{1,0:T(8,128)(2,1)S(1)} %bitcast.51, bf16[512,2560]{1,0:T(8,128)(2,1)S(1)} %bitcast.45, bf16[512,2560]{1,0:T(8,128)(2,1)S(1)} %bitcast.46, f32[4,8,512]{2,1,0:T(8,128)S(1)} %pad_convert_fusion.decay_ref), custom_call_target="tpu_custom_call" | custom-call | flops 1610612736 | bytes 6291456 | tf_op jit(solution)/shard_map/pallas_call | solution.py:135
  323.8 4.7 %shard_map.134 = bf16[512,1536]{1,0:T(8,128)(2,1)S(1)} custom-call(f32[512,1536]{1,0:T(8,128)} %shard_map.131.inner_ref, bf16[512,2560]{1,0:T(8,128)(2,1)S(1)} %bitcast.47, f32[4,8,512]{2,1,0:T(8,128)S(1)} %pad_convert_fusion.decay_ref, f32[2,128,1536]{2,1,0:T(8,128)S(1)} %copy-done.37, bf16[128,1536]{1,0:T(8,128)(2,1)} %bitcast.21.incoming_ref), custom_call_target="tpu_custom_call" | custom-call | flops 201326592 | bytes 3145728 | tf_op jit(solution)/shard_map/pallas_call | solution.py:135
  329.3 1.2 copy-done.20
  330.4 7.1 %all-to-all-start.12 = ((bf16[16,32,1536]{2,1,0:T(8,128)(2,1)}), bf16[16,32,1536]{2,1,0:T(8,128)(2,1)}, u32[]{:S(2)}, u32[]{:S(2)}) async-start(bf16[16,32,1536]{2,1,0:T(8,128)(2,1)} %copy-done.20), calls=%async_computation.12 | async-start | bytes 3145728 | tf_op jit(solution)/shard_map/all_to_all | solution.py:275
  337.6 5.1 %shard_map.125.inner_ref = f32[512,1536]{1,0:T(8,128)S(1)} custom-call(bf16[512,1536]{1,0:T(8,128)(2,1)S(1)} %copy-done.6, bf16[512,512]{1,0:T(8,128)(2,1)S(1)} %copy-done.22, bf16[512,512]{1,0:T(8,128)(2,1)S(1)} %copy-done.26, f32[4,8,512]{2,1,0:T(8,128)S(1)} %pad_convert_fusion.1.decay_ref), custom_call_target="tpu_custom_call" | custom-call | flops 1610612736 | bytes 6291456 | tf_op jit(solution)/shard_map/pallas_call | solution.py:135
  342.7 1.6 copy-done.28
  344.3 4.7 %shard_map.128 = bf16[512,1536]{1,0:T(8,128)(2,1)S(1)} custom-call(f32[512,1536]{1,0:T(8,128)} %copy-done.28, bf16[512,512]{1,0:T(8,128)(2,1)S(1)} %copy-done.27, f32[4,8,512]{2,1,0:T(8,128)S(1)} %pad_convert_fusion.1.decay_ref, f32[2,128,1536]{2,1,0:T(8,128)S(1)} %copy-done.35, bf16[128,1536]{1,0:T(8,128)(2,1)} %bitcast.17.incoming_ref), custom_call_target="tpu_custom_call" | custom-call | flops 201326592 | bytes 3145728 | tf_op jit(solution)/shard_map/pallas_call | solution.py:135
  349.1 1.2 copy-done.17
  350.3 22.7 %all-to-all-done.12.refs_0_ = bf16[16,32,1536]{2,1,0:T(8,128)(2,1)} async-done(((bf16[16,32,1536]{2,1,0:T(8,128)(2,1)}), bf16[16,32,1536]{2,1,0:T(8,128)(2,1)}, u32[]{:S(2)}, u32[]{:S(2)}) %all-to-all-start.12) | async-done | bytes 1572896 | tf_op jit(solution)/shard_map/all_to_all | solution.py:275
  373.0 1.8 shard_map.136
  375.3 1.9 fusion.1
  (104 shorter events, 18.6 us)
Async XLA Ops:
  1.4 1.4 copy-start
  2.8 1.0 copy-start.21
  3.9 1.0 copy-start.23
  5.7 1.5 copy-start.16
  7.2 7.3 %copy-start.43 = (bf16[24,512]{1,0:T(8,128)(2,1)S(1)}, bf16[24,512]{1,0:T(8,128)(2,1)}, u32[]{:S(2)}) copy-start(bf16[24,512]{1,0:T(8,128)(2,1)} %param.14) | copy-start | bytes 73732
  7.2 7.3 %copy-start.44 = (bf16[24,512]{1,0:T(8,128)(2,1)S(1)}, bf16[24,512]{1,0:T(8,128)(2,1)}, u32[]{:S(2)}) copy-start(bf16[24,512]{1,0:T(8,128)(2,1)} %param.13) | copy-start | bytes 73732
  7.2 7.4 %copy-start.47 = (s32[16]{0:T(128)S(1)}, s32[16]{0:T(128)}, u32[]{:S(2)}) copy-start(s32[16]{0:T(128)} %param.17) | copy-start | bytes 196
  7.2 66.5 %all-to-all-start.3 = ((bf16[16,32,2560]{2,1,0:T(8,128)(2,1)}), bf16[16,32,2560]{2,1,0:T(8,128)(2,1)S(1)}, u32[]{:S(2)}, u32[]{:S(2)}) async-start(bf16[16,32,2560]{2,1,0:T(8,128)(2,1)} %copy-done.16), calls=%async_computation.3 | async-start | bytes 5242880 | tf_op jit(solution)/shard_map/all_to_all | solution.py:275
  73.7 1.5 copy-start.14
  75.7 14.6 %all-to-all-start.1 = ((f32[16,2,24]{2,1,0:T(2,128)}), f32[16,2,24]{2,1,0:T(2,128)S(1)}, u32[]{:S(2)}, u32[]{:S(2)}) async-start(f32[16,2,24]{2,1,0:T(2,128)} %broadcast_in_dim.24), calls=%async_computation.1 | async-start | bytes 32768 | tf_op jit(solution)/shard_map/all_to_all | solution.py:290
  80.9 1.7 copy-start.15
  83.4 13.8 %copy-start.24 = (bf16[512,512]{1,0:T(8,128)(2,1)S(1)}, bf16[512,512]{1,0:T(8,128)(2,1)}, u32[]{:S(2)}) copy-start(bf16[512,512]{1,0:T(8,128)(2,1)} %q_ref.7) | copy-start | bytes 1572868
  88.4 1.1 copy-start.32
  89.5 0.7 copy-start.39
  90.3 16.8 %all-to-all-start.4 = ((bf16[16,8,1536]{2,1,0:T(8,128)(2,1)}), bf16[16,8,1536]{2,1,0:T(8,128)(2,1)}, u32[]{:S(2)}, u32[]{:S(2)}) async-start(bf16[16,8,1536]{2,1,0:T(8,128)(2,1)} %bitcast.58), calls=%async_computation.4 | async-start | bytes 786432 | tf_op jit(solution)/shard_map/all_to_all | solution.py:208
  97.3 1.4 copy-start.1
  103.5 1.1 copy-start.30
  104.6 0.8 copy-start.38
  107.1 15.1 %all-to-all-start = ((bf16[16,8,1536]{2,1,0:T(8,128)(2,1)}), bf16[16,8,1536]{2,1,0:T(8,128)(2,1)S(1)}, u32[]{:S(2)}, u32[]{:S(2)}) async-start(bf16[16,8,1536]{2,1,0:T(8,128)(2,1)} %bitcast.57), calls=%async_computation | async-start | bytes 786432 | tf_op jit(solution)/shard_map/all_to_all | solution.py:208
  122.3 0.8 copy-start.42
  123.0 15.1 %all-to-all-start.5 = ((bf16[16,8,1536]{2,1,0:T(8,128)(2,1)}), bf16[16,8,1536]{2,1,0:T(8,128)(2,1)S(1)}, u32[]{:S(2)}, u32[]{:S(2)}) async-start(bf16[16,8,1536]{2,1,0:T(8,128)(2,1)} %shard_map.121), calls=%async_computation.5 | async-start | bytes 786432 | tf_op jit(solution)/shard_map/all_to_all | solution.py:213
  138.2 19.2 %all-to-all-start.2 = ((bf16[16,8,1536]{2,1,0:T(8,128)(2,1)}), bf16[16,8,1536]{2,1,0:T(8,128)(2,1)}, u32[]{:S(2)}, u32[]{:S(2)}) async-start(bf16[16,8,1536]{2,1,0:T(8,128)(2,1)} %shard_map.115), calls=%async_computation.2 | async-start | bytes 786432 | tf_op jit(solution)/shard_map/all_to_all | solution.py:213
  143.8 6.9 %copy-start.33 = (f32[2,128,1536]{2,1,0:T(8,128)S(1)}, f32[2,128,1536]{2,1,0:T(8,128)}, u32[]{:S(2)}) copy-start(f32[2,128,1536]{2,1,0:T(8,128)} %copy-done.32) | copy-start | bytes 4718596
  149.1 1.6 copy-start.13
  155.4 8.9 %copy-start.46 = (f32[24]{0:T(128)S(1)}, f32[24]{0:T(128)}, u32[]{:S(2)}) copy-start(f32[24]{0:T(128)} %param.15) | copy-start | bytes 292
  155.5 9.0 %copy-start.22 = (bf16[512,512]{1,0:T(8,128)(2,1)S(1)}, bf16[512,512]{1,0:T(8,128)(2,1)}, u32[]{:S(2)}) copy-start(bf16[512,512]{1,0:T(8,128)(2,1)} %k_ref.7) | copy-start | bytes 1572868
  156.2 1.1 copy-start.19
  157.4 42.3 %all-to-all-start.6 = ((bf16[16,32,1536]{2,1,0:T(8,128)(2,1)}), bf16[16,32,1536]{2,1,0:T(8,128)(2,1)}, u32[]{:S(2)}, u32[]{:S(2)}) async-start(bf16[16,32,1536]{2,1,0:T(8,128)(2,1)} %copy-done.19), calls=%async_computation.6 | async-start | bytes 3145728 | tf_op jit(solution)/shard_map/all_to_all | solution.py:275
  164.5 1.4 copy-start.2
  165.9 1.0 copy-start.25
  166.9 6.7 %copy-start.31 = (f32[2,128,1536]{2,1,0:T(8,128)S(1)}, f32[2,128,1536]{2,1,0:T(8,128)}, u32[]{:S(2)}) copy-start(f32[2,128,1536]{2,1,0:T(8,128)} %copy-done.30) | copy-start | bytes 4718596
  172.1 1.6 copy-start.29
  173.7 27.8 %copy-start.45 = (f32[1536]{0:T(1024)S(1)}, f32[1536]{0:T(1024)}, u32[]{:S(2)}) copy-start(f32[1536]{0:T(1024)} %param.16) | copy-start | bytes 18436
  178.4 1.1 copy-start.10
  199.7 1.9 copy-start.3
  199.7 2.4 copy-start.11
  202.0 3.3 copy-start.12
  214.1 1.1 copy-start.4
  261.6 1.2 copy-start.8
  262.8 1.2 copy-start.36
  264.0 0.7 copy-start.41
  264.7 15.6 %all-to-all-start.10 = ((bf16[16,8,1536]{2,1,0:T(8,128)(2,1)}), bf16[16,8,1536]{2,1,0:T(8,128)(2,1)}, u32[]{:S(2)}, u32[]{:S(2)}) async-start(bf16[16,8,1536]{2,1,0:T(8,128)(2,1)} %bitcast.60), calls=%async_computation.10 | async-start | bytes 786432 | tf_op jit(solution)/shard_map/all_to_all | solution.py:208
  270.0 1.4 copy-start.5
  276.2 1.2 copy-start.34
  277.3 0.8 copy-start.40
  280.4 15.3 %all-to-all-start.7 = ((bf16[16,8,1536]{2,1,0:T(8,128)(2,1)}), bf16[16,8,1536]{2,1,0:T(8,128)(2,1)}, u32[]{:S(2)}, u32[]{:S(2)}) async-start(bf16[16,8,1536]{2,1,0:T(8,128)(2,1)} %bitcast.59), calls=%async_computation.7 | async-start | bytes 786432 | tf_op jit(solution)/shard_map/all_to_all | solution.py:208
  295.7 15.3 %all-to-all-start.11 = ((bf16[16,8,1536]{2,1,0:T(8,128)(2,1)}), bf16[16,8,1536]{2,1,0:T(8,128)(2,1)}, u32[]{:S(2)}, u32[]{:S(2)}) async-start(bf16[16,8,1536]{2,1,0:T(8,128)(2,1)} %shard_map.133), calls=%async_computation.11 | async-start | bytes 786432 | tf_op jit(solution)/shard_map/all_to_all | solution.py:213
  311.0 19.4 %all-to-all-start.8 = ((bf16[16,8,1536]{2,1,0:T(8,128)(2,1)}), bf16[16,8,1536]{2,1,0:T(8,128)(2,1)}, u32[]{:S(2)}, u32[]{:S(2)}) async-start(bf16[16,8,1536]{2,1,0:T(8,128)(2,1)} %shard_map.127), calls=%async_computation.8 | async-start | bytes 786432 | tf_op jit(solution)/shard_map/all_to_all | solution.py:213
  316.5 1.4 copy-start.9
  317.9 5.9 %copy-start.37 = (f32[2,128,1536]{2,1,0:T(8,128)S(1)}, f32[2,128,1536]{2,1,0:T(8,128)}, u32[]{:S(2)}) copy-start(f32[2,128,1536]{2,1,0:T(8,128)} %copy-done.36) | copy-start | bytes 4718596
  328.5 9.0 %copy-start.26 = (bf16[512,512]{1,0:T(8,128)(2,1)S(1)}, bf16[512,512]{1,0:T(8,128)(2,1)}, u32[]{:S(2)}) copy-start(bf16[512,512]{1,0:T(8,128)(2,1)} %q_ref.7) | copy-start | bytes 1572868
  329.3 1.2 copy-start.20
  330.4 7.1 %copy-start.6 = (bf16[512,1536]{1,0:T(8,128)(2,1)S(1)}, bf16[512,1536]{1,0:T(8,128)(2,1)}, u32[]{:S(2)}) copy-start(bf16[512,1536]{1,0:T(8,128)(2,1)} %copy-done.4) | copy-start | bytes 4718596
  330.4 42.5 %all-to-all-start.12 = ((bf16[16,32,1536]{2,1,0:T(8,128)(2,1)}), bf16[16,32,1536]{2,1,0:T(8,128)(2,1)}, u32[]{:S(2)}, u32[]{:S(2)}) async-start(bf16[16,32,1536]{2,1,0:T(8,128)(2,1)} %copy-done.20), calls=%async_computation.12 | async-start | bytes 3145728 | tf_op jit(solution)/shard_map/all_to_all | solution.py:275
  337.6 6.8 %copy-start.27 = (bf16[512,512]{1,0:T(8,128)(2,1)S(1)}, bf16[512,512]{1,0:T(8,128)(2,1)}, u32[]{:S(2)}) copy-start(bf16[512,512]{1,0:T(8,128)(2,1)} %q_ref.7) | copy-start | bytes 1572868
  337.6 6.8 %copy-start.35 = (f32[2,128,1536]{2,1,0:T(8,128)S(1)}, f32[2,128,1536]{2,1,0:T(8,128)}, u32[]{:S(2)}) copy-start(f32[2,128,1536]{2,1,0:T(8,128)} %copy-done.34) | copy-start | bytes 4718596
  342.7 1.6 copy-start.28
  349.1 1.2 copy-start.17
  373.0 1.9 copy-start.7
  373.0 2.4 copy-start.18

commit v3 on v2

--- a/solution.py
+++ b/solution.py
@@ -174,8 +174,9 @@
             8 * self.tokens * SPAN * self.width,
         )
 
-    def finish(self, incoming):
-        wide = pl.BlockSpec((STATE, self.cols), lambda g: (0, g))
+    def finish(self, incoming, first):
+        base = first // self.cols
+        wide = pl.BlockSpec((STATE, self.cols), lambda g: (0, base + g))
         deep = pl.BlockSpec((self.spans, STATE, self.cols), lambda g: (0, 0, g))
         rows = pl.BlockSpec((self.tokens, self.cols), lambda g: (0, g))
         return self.call(
@@ -193,21 +194,25 @@
         )
 
 
-def prefix_kernel(reverse, arrived_ref, factor_ref, out_ref):
-    count = arrived_ref.shape[0]
-    run = jnp.zeros(arrived_ref.shape[1:], F32)
-    order = range(count)
-    for index in order[::-1] if reverse else order:
-        out_ref[index] = run.astype(BF16)
-        run = run * factor_ref[index] + arrived_ref[index].astype(F32)
-
-
-def carried(total, factors, reverse):
+def prefix_kernel(directions, arrived_ref, factor_ref, out_ref):
+    count, rows, width = arrived_ref.shape
+    width //= len(directions)
+    for place, reverse in enumerate(directions):
+        cols = slice(place * width, (place + 1) * width)
+        run = jnp.zeros((rows, width), F32)
+        order = range(count)
+        for index in order[::-1] if reverse else order:
+            out_ref[index, :, cols] = run.astype(BF16)
+            run = run * factor_ref[index, :, cols] + arrived_ref[index, :, cols].astype(F32)
+
+
+def carried(totals, factors, directions):
     count = lax.axis_size("seq")
+    total = jnp.concatenate(totals, axis=1)
     pieces = total.reshape(count, STATE // count, -1)
     arrived = lax.all_to_all(pieces, "seq", split_axis=0, concat_axis=0, tiled=True)
     composed = pl.pallas_call(
-        functools.partial(prefix_kernel, reverse),
+        functools.partial(prefix_kernel, directions),
         out_shape=jax.ShapeDtypeStruct(arrived.shape, BF16),
     )(arrived, factors)
     back = lax.all_to_all(composed, "seq", split_axis=0, concat_axis=0, tiled=True)
@@ -270,16 +275,12 @@
     def units(array):
         return array.reshape(unit_count, unit_rows, -1)
 
-    def moved(arrays, send_index, recv_index):
+    def sent(arrays, send_index):
         outgoing = gathered([units(array) for array in arrays], send_index)
-        arrived = lax.all_to_all(outgoing, "seq", split_axis=0, concat_axis=0, tiled=True)
+        return lax.all_to_all(outgoing, "seq", split_axis=0, concat_axis=0, tiled=True)
+
+    def placed(arrived, recv_index):
         return gathered([arrived], recv_index).reshape(tok_rows, -1)
-
-    def to_scan(*arrays):
-        return moved(arrays, send_scan, scan_source)
-
-    def to_raster(array):
-        return moved([array], send_raster, raster_dest)
 
     def padded(decay):
         wide = decay.astype(F32).reshape(groups, heads // groups, tok_rows)
@@ -289,21 +290,25 @@
     copies = jnp.broadcast_to(sums[None], (lax.axis_size("seq"), *sums.shape))
     all_sums = lax.all_to_all(copies, "seq", split_axis=0, concat_axis=0, tiled=True)
     factors = jnp.repeat(jnp.exp(all_sums), HEAD_DIM, axis=2)
-    forward_factors, reverse_factors = factors[:, 0:1], factors[:, 1:2]
+    factors = factors.reshape(factors.shape[0], 1, 2 * width)
     decay_f, decay_r = padded(decay_forward), padded(decay_reverse)
 
-    joined = to_scan(ssm_input, input_map, output_map)
     keys_at, queries_at = width, width + maps
 
+    arrived = sent([ssm_input, input_map, output_map], send_scan)
     ahead = Scan((ssm_input, 0), (input_map, 0), (output_map, 0), decay_f, width, False)
-    ahead_in = carried(ahead.states(), forward_factors, False)
+    ahead_total = ahead.states()
     ahead.inner()
-    y_forward = ahead.finish(ahead_in)
-
+    arrived, ahead_total, ahead.near, factors = lax.optimization_barrier(
+        (arrived, ahead_total, ahead.near, factors)
+    )
+    joined = placed(arrived, scan_source)
     behind = Scan((joined, 0), (joined, keys_at), (joined, queries_at), decay_r, width, True)
-    behind_in = carried(behind.states(), reverse_factors, True)
+    entering = carried((ahead_total, behind.states()), factors, (False, True))
     behind.inner()
-    y_reverse = to_raster(behind.finish(behind_in))
+    y_reverse_sent = sent([behind.finish(entering, width)], send_raster)
+    y_forward = ahead.finish(entering, 0)
+    y_reverse = placed(y_reverse_sent, raster_dest)
 
     skip_cols = jnp.repeat(skip_gain, HEAD_DIM)
     combined = (
@@ -320,16 +325,20 @@
         inv_rms[:, None] * scaled_grad - combined * (inv_rms**3 * inner_sum / FEATURES)[:, None]
     ).astype(BF16)
 
-    grad_scan = to_scan(grad_combined)
+    arrived = sent([grad_combined], send_scan)
     ahead_grad = Scan((grad_combined, 0), (output_map, 0), (input_map, 0), decay_f, width, True)
-    ahead_grad_in = carried(ahead_grad.states(), forward_factors, True)
+    ahead_total = ahead_grad.states()
     ahead_grad.inner()
-    grad_forward = ahead_grad.finish(ahead_grad_in)
-
+    arrived, ahead_total, ahead_grad.near = lax.optimization_barrier(
+        (arrived, ahead_total, ahead_grad.near)
+    )
+    grad_scan = placed(arrived, scan_source)
     behind_grad = Scan((grad_scan, 0), (joined, queries_at), (joined, keys_at), decay_r, width, False)
-    behind_grad_in = carried(behind_grad.states(), reverse_factors, False)
+    entering = carried((ahead_total, behind_grad.states()), factors, (True, False))
     behind_grad.inner()
-    grad_reverse = to_raster(behind_grad.finish(behind_grad_in))
+    grad_reverse_sent = sent([behind_grad.finish(entering, width)], send_raster)
+    grad_forward = ahead_grad.finish(entering, 0)
+    grad_reverse = placed(grad_reverse_sent, raster_dest)
 
     grad_input = (
         grad_forward.astype(F32)

time: 379 us -> 358 us (0.945)
  starting transfers between devices: 71 us -> 39.8 us
  waiting for transfers between devices: 135 us -> 152 us
  local copies, waits for them, and re-layouts: 40 us -> 25.8 us
  blocking collectives: 43.3 us -> 50.5 us
    all_to_all x7 -> x4, starting transfers between devices: 44.2 us -> 22.1 us  [sent(): lax.all_to_all(outgoing, 'seq', split_axis=0, concat_axis=0, tiled=True)]
    unnamed x96 -> x92, local copies, waits for them, and re-layouts: 36.2 us -> 23.9 us
    all_to_all x4 -> x2, starting transfers between devices: 21.6 us -> 10.5 us  [carried(): lax.all_to_all(composed, 'seq', split_axis=0, concat_axis=0, tiled=True)]
    all_to_all x7 -> x4, waiting for transfers between devices: 119 us -> 129 us  [sent(): lax.all_to_all(outgoing, 'seq', split_axis=0, concat_axis=0, tiled=True)]
    all_to_all x1 -> x2, blocking collectives: 40.9 us -> 48 us  [carried(): lax.all_to_all(pieces, 'seq', split_axis=0, concat_axis=0, tiled=True)]
    all_to_all x4 -> x2, waiting for transfers between devices: 16.2 us -> 22.9 us  [carried(): lax.all_to_all(composed, 'seq', split_axis=0, concat_axis=0, tiled=True)]
    pallas_call x8, Pallas kernels: 8 us -> 12.4 us  [gathered(): pl.pallas_call(functools.partial(gather_kernel, widths), in_specs=[pl.Blo...]
  transfers between devices with their start and end apart: 12 -> 7, of which waited for: 9 -> 6; matrix products, arithmetic and copies ran while one was open for 1% -> 1% of each run, Pallas kernels for 17% -> 12%
where the time goes in v3:
time: 358 us; the launch traced here: 356 us
  waiting for transfers between devices  152 us (42%)
  Pallas kernels  76.6 us (21%)
  blocking collectives  50.5 us (14%)
  starting transfers between devices  39.8 us (11%)
  local copies, waits for them, and re-layouts  25.8 us (7%)
  other arithmetic  10.2 us (3%)
    all_to_all x4, waiting for transfers between devices, sent(): lax.all_to_all(outgoing, 'seq', split_axis=0, concat_axis=0, tiled=True)  129 us
    pallas_call x12, Pallas kernels, call(): pl.pallas_call(functools.partial(body, self.reverse, self.spans), grid=(s...  59.7 us
    all_to_all x2, blocking collectives, carried(): lax.all_to_all(pieces, 'seq', split_axis=0, concat_axis=0, tiled=True)  48 us
    unnamed x92, local copies, waits for them, and re-layouts  23.9 us
    all_to_all x2, waiting for transfers between devices, carried(): lax.all_to_all(composed, 'seq', split_axis=0, concat_axis=0, tiled=True)  22.9 us
    all_to_all x4, starting transfers between devices, sent(): lax.all_to_all(outgoing, 'seq', split_axis=0, concat_axis=0, tiled=True)  22.1 us
    pallas_call x8, Pallas kernels, gathered(): pl.pallas_call(functools.partial(gather_kernel, widths), in_specs=[pl.Blo...  12.4 us
    all_to_all x2, starting transfers between devices, carried(): lax.all_to_all(composed, 'seq', split_axis=0, concat_axis=0, tiled=True)  10.5 us
  transfers between devices with their start and end apart: 7, of which 6 were waited for; matrix products, arithmetic and copies ran while one was open for 1% of the time, Pallas kernels for 12%

profile of v3, /device:TPU:12, one launch (start us, length us, event | category | flops | bytes accessed | tf_op | source)
XLA Modules:
  0.0 356.2 jit_solution(5146788559842136190)
XLA Ops:
  0.6 0.8 convert_reduce_fusion
  1.5 0.6 broadcast_in_dim.43
  2.1 7.2 %all-to-all-start.1 = ((f32[16,2,24]{2,1,0:T(2,128)}), f32[16,2,24]{2,1,0:T(2,128)S(1)}, u32[]{:S(2)}, u32[]{:S(2)}) async-start(f32[16,2,24]{2,1,0:T(2,128)} %broadcast_in_dim.43), calls=%async_computation.1 | async-start | bytes 32768 | tf_op jit(solution)/shard_map/all_to_all | solution.py:291
  9.3 0.7 and_select_fusion.1.index_ref
  10.0 1.4 copy-done.2
  11.5 1.0 copy-done.18
  12.5 1.0 copy-done.22
  13.5 0.8 shard_map.113
  14.3 1.5 copy-done.12
  15.9 7.2 %all-to-all-start = ((bf16[16,32,2560]{2,1,0:T(8,128)(2,1)}), bf16[16,32,2560]{2,1,0:T(8,128)(2,1)}, u32[]{:S(2)}, u32[]{:S(2)}) async-start(bf16[16,32,2560]{2,1,0:T(8,128)(2,1)} %copy-done.12), calls=%async_computation | async-start | bytes 5242880 | tf_op jit(solution)/shard_map/all_to_all | solution.py:280
  23.2 4.8 %shard_map.114 = (f32[2,128,1536]{2,1,0:T(8,128)S(1)}, bf16[128,1536]{1,0:T(8,128)(2,1)S(1)}) custom-call(bf16[512,1536]{1,0:T(8,128)(2,1)S(1)} %copy-done.3, bf16[512,512]{1,0:T(8,128)(2,1)S(1)} %copy-done.23, f32[4,8,512]{2,1,0:T(8,128)S(1)} %pad_convert_fusion.1.decay_ref), custom_call_target="tpu_custom_call" | custom-call | flops 201326592 | bytes 3932160 | tf_op jit(solution)/shard_map/pallas_call | solution.py:135
  28.1 1.1 copy-done.32
  29.2 5.1 %shard_map.115.inner_ref = f32[512,1536]{1,0:T(8,128)S(1)} custom-call(bf16[512,1536]{1,0:T(8,128)(2,1)S(1)} %copy-done.3, bf16[512,512]{1,0:T(8,128)(2,1)S(1)} %copy-done.23, bf16[512,512]{1,0:T(8,128)(2,1)S(1)} %copy-done.19, f32[4,8,512]{2,1,0:T(8,128)S(1)} %pad_convert_fusion.1.decay_ref), custom_call_target="tpu_custom_call" | custom-call | flops 1610612736 | bytes 6291456 | tf_op jit(solution)/shard_map/pallas_call | solution.py:135
  34.4 1.6 copy-done.26
  36.0 0.2 broadcast_in_dim.44
  36.2 0.9 reshape_reshape.3.factor_ref
  37.1 45.0 %all-to-all-done.refs_0_ = bf16[16,32,2560]{2,1,0:T(8,128)(2,1)} async-done(((bf16[16,32,2560]{2,1,0:T(8,128)(2,1)}), bf16[16,32,2560]{2,1,0:T(8,128)(2,1)}, u32[]{:S(2)}, u32[]{:S(2)}) %all-to-all-start) | async-done | bytes 2621472 | tf_op jit(solution)/shard_map/all_to_all | solution.py:280
  82.1 2.0 shard_map.116
  84.1 4.9 %shard_map.117 = (f32[2,128,1536]{2,1,0:T(8,128)S(1)}, bf16[128,1536]{1,0:T(8,128)(2,1)S(1)}) custom-call(bf16[512,2560]{1,0:T(8,128)(2,1)S(1)} %bitcast.36, bf16[512,2560]{1,0:T(8,128)(2,1)S(1)} %bitcast.37, f32[4,8,512]{2,1,0:T(8,128)S(1)} %pad_convert_fusion.decay_ref), custom_call_target="tpu_custom_call" | custom-call | flops 201326592 | bytes 3932160 | tf_op jit(solution)/shard_map/pallas_call | solution.py:135
  89.1 1.1 copy-done.30
  90.3 23.5 %all_to_all.45.arrived_ref = bf16[16,8,3072]{2,1,0:T(8,128)(2,1)} all-to-all(bf16[16,8,3072]{2,1,0:T(8,128)(2,1)S(1)} %maximum_bitcast_fusion), channel_id=1, replica_groups=mesh['seq'=16,'head'=2] {'seq'}, dimensions={0} | all-to-all | bytes 1572864 | tf_op jit(solution)/shard_map/all_to_all | solution.py:213
  113.8 2.2 shard_map.118
  116.0 5.3 %all-to-all-start.3 = ((bf16[16,8,3072]{2,1,0:T(8,128)(2,1)}), bf16[16,8,3072]{2,1,0:T(8,128)(2,1)S(1)}, u32[]{:S(2)}, u32[]{:S(2)}) async-start(bf16[16,8,3072]{2,1,0:T(8,128)(2,1)} %shard_map.118), calls=%async_computation.3 | async-start | bytes 1572864 | tf_op jit(solution)/shard_map/all_to_all | solution.py:218
  121.4 5.3 %shard_map.120.inner_ref = f32[512,1536]{1,0:T(8,128)S(1)} custom-call(bf16[512,2560]{1,0:T(8,128)(2,1)S(1)} %bitcast.38, bf16[512,2560]{1,0:T(8,128)(2,1)S(1)} %bitcast.39, bf16[512,2560]{1,0:T(8,128)(2,1)S(1)} %bitcast.40, f32[4,8,512]{2,1,0:T(8,128)S(1)} %pad_convert_fusion.decay_ref), custom_call_target="tpu_custom_call" | custom-call | flops 1610612736 | bytes 6291456 | tf_op jit(solution)/shard_map/pallas_call | solution.py:135
  126.7 1.7 copy-done.11
  128.3 11.4 %all-to-all-done.3 = bf16[16,8,3072]{2,1,0:T(8,128)(2,1)S(1)} async-done(((bf16[16,8,3072]{2,1,0:T(8,128)(2,1)}), bf16[16,8,3072]{2,1,0:T(8,128)(2,1)S(1)}, u32[]{:S(2)}, u32[]{:S(2)}) %all-to-all-start.3) | async-done | bytes 786464 | tf_op jit(solution)/shard_map/all_to_all | solution.py:218
  139.8 1.7 copy-done.31
  141.5 4.8 %shard_map.121 = bf16[512,1536]{1,0:T(8,128)(2,1)S(1)} custom-call(f32[512,1536]{1,0:T(8,128)} %copy-done.11, bf16[512,2560]{1,0:T(8,128)(2,1)} %bitcast.41, f32[4,8,512]{2,1,0:T(8,128)S(1)} %pad_convert_fusion.decay_ref, f32[2,128,1536]{2,1,0:T(8,128)S(1)} %copy-done.31, bf16[128,3072]{1,0:T(8,128)(2,1)S(1)} %bitcast.52), custom_call_target="tpu_custom_call" | custom-call | flops 201326592 | bytes 3145728 | tf_op jit(solution)/shard_map/pallas_call | solution.py:135
  146.3 0.7 shard_map.122
  147.0 1.1 copy-done.15
  148.2 5.2 %all-to-all-start.4 = ((bf16[16,32,1536]{2,1,0:T(8,128)(2,1)}), bf16[16,32,1536]{2,1,0:T(8,128)(2,1)}, u32[]{:S(2)}, u32[]{:S(2)}) async-start(bf16[16,32,1536]{2,1,0:T(8,128)(2,1)} %copy-done.15), calls=%async_computation.4 | async-start | bytes 3145728 | tf_op jit(solution)/shard_map/all_to_all | solution.py:280
  153.5 1.4 copy-done.33
  154.9 4.7 %shard_map.119 = bf16[512,1536]{1,0:T(8,128)(2,1)S(1)} custom-call(f32[512,1536]{1,0:T(8,128)} %copy-done.26, bf16[512,512]{1,0:T(8,128)(2,1)S(1)} %copy-done.20, f32[4,8,512]{2,1,0:T(8,128)S(1)} %pad_convert_fusion.1.decay_ref, f32[2,128,1536]{2,1,0:T(8,128)S(1)} %copy-done.33, bf16[128,3072]{1,0:T(8,128)(2,1)S(1)} %bitcast.53), custom_call_target="tpu_custom_call" | custom-call | flops 201326592 | bytes 3145728 | tf_op jit(solution)/shard_map/pallas_call | solution.py:135
  159.6 30.1 %all-to-all-done.4.refs_0_ = bf16[16,32,1536]{2,1,0:T(8,128)(2,1)} async-done(((bf16[16,32,1536]{2,1,0:T(8,128)(2,1)}), bf16[16,32,1536]{2,1,0:T(8,128)(2,1)}, u32[]{:S(2)}, u32[]{:S(2)}) %all-to-all-start.4) | async-done | bytes 1572896 | tf_op jit(solution)/shard_map/all_to_all | solution.py:280
  189.7 1.7 shard_map.123
  191.6 1.3 multiply_reduce_fusion.1
  193.0 2.5 psum.7
  195.5 5.0 %subtract_convert_fusion = (bf16[512,1536]{1,0:T(8,128)(2,1)S(1)}, bf16[512,1536]{1,0:T(8,128)(2,1)}) fusion(bf16[512,1536]{1,0:T(8,128)(2,1)} %param.19, f32[512]{0:T(512)S(1)} %fusion.4, f32[512]{0:T(512)S(1)} %bitcast.61, f32[1536]{0:T(1024)S(1)} %copy-done.43, bf16[512,1536]{1,0:T(8,128)(2,1)S(1)} %copy-done.4, f32[1536]{0:T(1024)S(1)} %mul.65, ...), kind=kLoop, calls=%fused_computation.5 | loop fusion | flops 11796480 | bytes 9453568 | tf_op jit(solution)/shard_map/convert_element_type | solution.py:326
  200.5 1.9 shard_map.124
  202.4 4.6 %all-to-all-start.5 = ((bf16[16,32,1536]{2,1,0:T(8,128)(2,1)}), bf16[16,32,1536]{2,1,0:T(8,128)(2,1)}, u32[]{:S(2)}, u32[]{:S(2)}) async-start(bf16[16,32,1536]{2,1,0:T(8,128)(2,1)} %shard_map.124), calls=%async_computation.5 | async-start | bytes 3145728 | tf_op jit(solution)/shard_map/all_to_all | solution.py:280
  207.0 4.8 %shard_map.125 = (f32[2,128,1536]{2,1,0:T(8,128)S(1)}, bf16[128,1536]{1,0:T(8,128)(2,1)S(1)}) custom-call(bf16[512,1536]{1,0:T(8,128)(2,1)S(1)} %get-tuple-element.34.v_ref, bf16[512,512]{1,0:T(8,128)(2,1)S(1)} %copy-done.21, f32[4,8,512]{2,1,0:T(8,128)S(1)} %pad_convert_fusion.1.decay_ref), custom_call_target="tpu_custom_call" | custom-call | flops 201326592 | bytes 3932160 | tf_op jit(solution)/shard_map/pallas_call | solution.py:135
  211.8 1.1 copy-done.34
  212.9 0.8 copy-done.36
  213.7 5.1 %shard_map.126.inner_ref = f32[512,1536]{1,0:T(8,128)S(1)} custom-call(bf16[512,1536]{1,0:T(8,128)(2,1)S(1)} %get-tuple-element.34.v_ref, bf16[512,512]{1,0:T(8,128)(2,1)S(1)} %copy-done.21, bf16[512,512]{1,0:T(8,128)(2,1)S(1)} %copy-done.24, f32[4,8,512]{2,1,0:T(8,128)S(1)} %pad_convert_fusion.1.decay_ref), custom_call_target="tpu_custom_call" | custom-call | flops 1610612736 | bytes 6291456 | tf_op jit(solution)/shard_map/pallas_call | solution.py:135
  218.8 1.6 copy-done.27
  220.5 23.8 %all-to-all-done.5.refs_0_ = bf16[16,32,1536]{2,1,0:T(8,128)(2,1)} async-done(((bf16[16,32,1536]{2,1,0:T(8,128)(2,1)}), bf16[16,32,1536]{2,1,0:T(8,128)(2,1)}, u32[]{:S(2)}, u32[]{:S(2)}) %all-to-all-start.5) | async-done | bytes 1572896 | tf_op jit(solution)/shard_map/all_to_all | solution.py:280
  244.3 1.6 shard_map.127
  245.9 4.8 %shard_map.128 = (f32[2,128,1536]{2,1,0:T(8,128)S(1)}, bf16[128,1536]{1,0:T(8,128)(2,1)S(1)}) custom-call(bf16[512,1536]{1,0:T(8,128)(2,1)S(1)} %bitcast.48, bf16[512,2560]{1,0:T(8,128)(2,1)S(1)} %bitcast.43, f32[4,8,512]{2,1,0:T(8,128)S(1)} %pad_convert_fusion.decay_ref), custom_call_target="tpu_custom_call" | custom-call | flops 201326592 | bytes 3932160 | tf_op jit(solution)/shard_map/pallas_call | solution.py:135
  250.7 1.2 copy-done.28
  252.0 24.5 %all_to_all.46.arrived_ref = bf16[16,8,3072]{2,1,0:T(8,128)(2,1)} all-to-all(bf16[16,8,3072]{2,1,0:T(8,128)(2,1)S(1)} %maximum_bitcast_fusion.1), channel_id=1, replica_groups=mesh['seq'=16,'head'=2] {'seq'}, dimensions={0} | all-to-all | bytes 1572864 | tf_op jit(solution)/shard_map/all_to_all | solution.py:213
  276.5 2.3 shard_map.129
  278.8 5.3 %all-to-all-start.7 = ((bf16[16,8,3072]{2,1,0:T(8,128)(2,1)}), bf16[16,8,3072]{2,1,0:T(8,128)(2,1)S(1)}, u32[]{:S(2)}, u32[]{:S(2)}) async-start(bf16[16,8,3072]{2,1,0:T(8,128)(2,1)} %shard_map.129), calls=%async_computation.7 | async-start | bytes 1572864 | tf_op jit(solution)/shard_map/all_to_all | solution.py:218
  284.1 1.4 copy-done.8
  285.5 6.0 %shard_map.131.inner_ref = f32[512,1536]{1,0:T(8,128)} custom-call(bf16[512,1536]{1,0:T(8,128)(2,1)S(1)} %bitcast.49, bf16[512,2560]{1,0:T(8,128)(2,1)S(1)} %bitcast.44, bf16[512,2560]{1,0:T(8,128)(2,1)S(1)} %bitcast.45, f32[4,8,512]{2,1,0:T(8,128)S(1)} %pad_convert_fusion.decay_ref), custom_call_target="tpu_custom_call" | custom-call | flops 1610612736 | bytes 6291456 | tf_op jit(solution)/shard_map/pallas_call | solution.py:135
  291.5 11.5 %all-to-all-done.7 = bf16[16,8,3072]{2,1,0:T(8,128)(2,1)S(1)} async-done(((bf16[16,8,3072]{2,1,0:T(8,128)(2,1)}), bf16[16,8,3072]{2,1,0:T(8,128)(2,1)S(1)}, u32[]{:S(2)}, u32[]{:S(2)}) %all-to-all-start.7) | async-done | bytes 786464 | tf_op jit(solution)/shard_map/all_to_all | solution.py:218
  302.9 1.4 copy-done.29
  304.3 4.7 %shard_map.132 = bf16[512,1536]{1,0:T(8,128)(2,1)S(1)} custom-call(f32[512,1536]{1,0:T(8,128)} %shard_map.131.inner_ref, bf16[512,2560]{1,0:T(8,128)(2,1)} %bitcast.42, f32[4,8,512]{2,1,0:T(8,128)S(1)} %pad_convert_fusion.decay_ref, f32[2,128,1536]{2,1,0:T(8,128)S(1)} %copy-done.29, bf16[128,3072]{1,0:T(8,128)(2,1)S(1)} %bitcast.50), custom_call_target="tpu_custom_call" | custom-call | flops 201326592 | bytes 3145728 | tf_op jit(solution)/shard_map/pallas_call | solution.py:135
  309.1 1.9 shard_map.133
  311.0 5.1 %all-to-all-start.8 = ((bf16[16,32,1536]{2,1,0:T(8,128)(2,1)}), bf16[16,32,1536]{2,1,0:T(8,128)(2,1)}, u32[]{:S(2)}, u32[]{:S(2)}) async-start(bf16[16,32,1536]{2,1,0:T(8,128)(2,1)} %shard_map.133), calls=%async_computation.8 | async-start | bytes 3145728 | tf_op jit(solution)/shard_map/all_to_all | solution.py:280
  316.0 4.7 %shard_map.130 = bf16[512,1536]{1,0:T(8,128)(2,1)S(1)} custom-call(f32[512,1536]{1,0:T(8,128)} %copy-done.27, bf16[512,512]{1,0:T(8,128)(2,1)S(1)} %copy-done.25, f32[4,8,512]{2,1,0:T(8,128)S(1)} %pad_convert_fusion.1.decay_ref, f32[2,128,1536]{2,1,0:T(8,128)S(1)} %copy-done.35, bf16[128,3072]{1,0:T(8,128)(2,1)S(1)} %bitcast.51), custom_call_target="tpu_custom_call" | custom-call | flops 201326592 | bytes 3145728 | tf_op jit(solution)/shard_map/pallas_call | solution.py:135
  320.8 1.2 copy-done.16
  322.0 30.5 %all-to-all-done.8.refs_0_ = bf16[16,32,1536]{2,1,0:T(8,128)(2,1)} async-done(((bf16[16,32,1536]{2,1,0:T(8,128)(2,1)}), bf16[16,32,1536]{2,1,0:T(8,128)(2,1)}, u32[]{:S(2)}, u32[]{:S(2)}) %all-to-all-start.8) | async-done | bytes 1572896 | tf_op jit(solution)/shard_map/all_to_all | solution.py:280
  352.4 1.7 shard_map.134
  354.3 1.9 fusion.1
  (90 shorter events, 1.0 us)
Async XLA Ops:
  2.1 13.8 %all-to-all-start.1 = ((f32[16,2,24]{2,1,0:T(2,128)}), f32[16,2,24]{2,1,0:T(2,128)S(1)}, u32[]{:S(2)}, u32[]{:S(2)}) async-start(f32[16,2,24]{2,1,0:T(2,128)} %broadcast_in_dim.43), calls=%async_computation.1 | async-start | bytes 32768 | tf_op jit(solution)/shard_map/all_to_all | solution.py:291
  10.0 1.4 copy-start.2
  11.5 1.0 copy-start.18
  12.5 1.0 copy-start.22
  14.3 1.6 copy-start.12
  15.9 7.2 %copy-start.41 = (bf16[24,512]{1,0:T(8,128)(2,1)S(1)}, bf16[24,512]{1,0:T(8,128)(2,1)}, u32[]{:S(2)}) copy-start(bf16[24,512]{1,0:T(8,128)(2,1)} %param.13) | copy-start | bytes 73732
  15.9 7.3 %copy-start.42 = (bf16[24,512]{1,0:T(8,128)(2,1)S(1)}, bf16[24,512]{1,0:T(8,128)(2,1)}, u32[]{:S(2)}) copy-start(bf16[24,512]{1,0:T(8,128)(2,1)} %param.14) | copy-start | bytes 73732
  15.9 7.3 %copy-start.3 = (bf16[512,1536]{1,0:T(8,128)(2,1)S(1)}, bf16[512,1536]{1,0:T(8,128)(2,1)}, u32[]{:S(2)}) copy-start(bf16[512,1536]{1,0:T(8,128)(2,1)} %v_ref.3) | copy-start | bytes 4718596
  15.9 7.3 %copy-start.23 = (bf16[512,512]{1,0:T(8,128)(2,1)S(1)}, bf16[512,512]{1,0:T(8,128)(2,1)}, u32[]{:S(2)}) copy-start(bf16[512,512]{1,0:T(8,128)(2,1)} %q_ref.7) | copy-start | bytes 1572868
  15.9 13.3 %copy-start.19 = (bf16[512,512]{1,0:T(8,128)(2,1)S(1)}, bf16[512,512]{1,0:T(8,128)(2,1)}, u32[]{:S(2)}) copy-start(bf16[512,512]{1,0:T(8,128)(2,1)} %k_ref.7) | copy-start | bytes 1572868
  15.9 66.2 %all-to-all-start = ((bf16[16,32,2560]{2,1,0:T(8,128)(2,1)}), bf16[16,32,2560]{2,1,0:T(8,128)(2,1)}, u32[]{:S(2)}, u32[]{:S(2)}) async-start(bf16[16,32,2560]{2,1,0:T(8,128)(2,1)} %copy-done.12), calls=%async_computation | async-start | bytes 5242880 | tf_op jit(solution)/shard_map/all_to_all | solution.py:280
  28.0 1.1 copy-start.32
  29.2 6.8 %copy-start.45 = (s32[16]{0:T(128)S(1)}, s32[16]{0:T(128)}, u32[]{:S(2)}) copy-start(s32[16]{0:T(128)} %param.17) | copy-start | bytes 196
  34.4 1.6 copy-start.26
  84.1 37.3 %copy-start = (bf16[16,32,2560]{2,1,0:T(8,128)(2,1)}, bf16[16,32,2560]{2,1,0:T(8,128)(2,1)S(1)}, u32[]{:S(2)}) copy-start(bf16[16,32,2560]{2,1,0:T(8,128)(2,1)S(1)} %shard_map.116) | copy-start | bytes 7864324
  89.0 1.1 copy-start.30
  116.0 23.8 %all-to-all-start.3 = ((bf16[16,8,3072]{2,1,0:T(8,128)(2,1)}), bf16[16,8,3072]{2,1,0:T(8,128)(2,1)S(1)}, u32[]{:S(2)}, u32[]{:S(2)}) async-start(bf16[16,8,3072]{2,1,0:T(8,128)(2,1)} %shard_map.118), calls=%async_computation.3 | async-start | bytes 1572864 | tf_op jit(solution)/shard_map/all_to_all | solution.py:218
  126.7 1.7 copy-start.11
  139.8 6.5 %copy-start.13 = (bf16[16,8,3072]{2,1,0:T(8,128)(2,1)}, bf16[16,8,3072]{2,1,0:T(8,128)(2,1)S(1)}, u32[]{:S(2)}) copy-start(bf16[16,8,3072]{2,1,0:T(8,128)(2,1)S(1)} %all-to-all-done.3) | copy-start | bytes 2359300
  139.8 1.7 copy-start.31
  146.2 7.1 %copy-start.44 = (f32[24]{0:T(128)S(1)}, f32[24]{0:T(128)}, u32[]{:S(2)}) copy-start(f32[24]{0:T(128)} %param.15) | copy-start | bytes 292
  146.3 7.2 %copy-start.14 = (bf16[16,8,3072]{2,1,0:T(8,128)(2,1)S(1)}, bf16[16,8,3072]{2,1,0:T(8,128)(2,1)}, u32[]{:S(2)}) copy-start(bf16[16,8,3072]{2,1,0:T(8,128)(2,1)} %copy-done.13) | copy-start | bytes 2359300
  147.0 1.1 copy-start.15
  148.2 5.4 %copy-start.20 = (bf16[512,512]{1,0:T(8,128)(2,1)S(1)}, bf16[512,512]{1,0:T(8,128)(2,1)}, u32[]{:S(2)}) copy-start(bf16[512,512]{1,0:T(8,128)(2,1)} %k_ref.7) | copy-start | bytes 1572868
  148.2 41.6 %all-to-all-start.4 = ((bf16[16,32,1536]{2,1,0:T(8,128)(2,1)}), bf16[16,32,1536]{2,1,0:T(8,128)(2,1)}, u32[]{:S(2)}, u32[]{:S(2)}) async-start(bf16[16,32,1536]{2,1,0:T(8,128)(2,1)} %copy-done.15), calls=%async_computation.4 | async-start | bytes 3145728 | tf_op jit(solution)/shard_map/all_to_all | solution.py:280
  153.5 42.0 %copy-start.39 = (f32[1536]{0:T(1024)}, f32[1536]{0:T(1024)S(1)}, u32[]{:S(2)}) copy-start(f32[1536]{0:T(1024)S(1)} %mul.65) | copy-start | bytes 18436
  153.5 1.4 copy-start.33
  154.9 36.5 %copy-start.43 = (f32[1536]{0:T(1024)S(1)}, f32[1536]{0:T(1024)}, u32[]{:S(2)}) copy-start(f32[1536]{0:T(1024)} %param.16) | copy-start | bytes 18436
  159.6 33.4 %copy-start.10 = (bf16[512,1536]{1,0:T(8,128)(2,1)}, bf16[512,1536]{1,0:T(8,128)(2,1)S(1)}, u32[]{:S(2)}) copy-start(bf16[512,1536]{1,0:T(8,128)(2,1)S(1)} %shard_map.119) | copy-start | bytes 4718596
  159.6 31.9 %copy-start.4 = (bf16[512,1536]{1,0:T(8,128)(2,1)S(1)}, bf16[512,1536]{1,0:T(8,128)(2,1)}, u32[]{:S(2)}) copy-start(bf16[512,1536]{1,0:T(8,128)(2,1)} %v_ref.3) | copy-start | bytes 4718596
  189.7 1.9 copy-start.38
  191.6 1.4 copy-start.9
  200.5 11.3 %copy-start.5 = (bf16[512,1536]{1,0:T(8,128)(2,1)}, bf16[512,1536]{1,0:T(8,128)(2,1)S(1)}, u32[]{:S(2)}) copy-start(bf16[512,1536]{1,0:T(8,128)(2,1)S(1)} %get-tuple-element.34.v_ref) | copy-start | bytes 4718596
  200.5 6.5 %copy-start.21 = (bf16[512,512]{1,0:T(8,128)(2,1)S(1)}, bf16[512,512]{1,0:T(8,128)(2,1)}, u32[]{:S(2)}) copy-start(bf16[512,512]{1,0:T(8,128)(2,1)} %k_ref.7) | copy-start | bytes 1572868
  202.4 11.3 %copy-start.24 = (bf16[512,512]{1,0:T(8,128)(2,1)S(1)}, bf16[512,512]{1,0:T(8,128)(2,1)}, u32[]{:S(2)}) copy-start(bf16[512,512]{1,0:T(8,128)(2,1)} %q_ref.7) | copy-start | bytes 1572868
  202.4 41.9 %all-to-all-start.5 = ((bf16[16,32,1536]{2,1,0:T(8,128)(2,1)}), bf16[16,32,1536]{2,1,0:T(8,128)(2,1)}, u32[]{:S(2)}, u32[]{:S(2)}) async-start(bf16[16,32,1536]{2,1,0:T(8,128)(2,1)} %shard_map.124), calls=%async_computation.5 | async-start | bytes 3145728 | tf_op jit(solution)/shard_map/all_to_all | solution.py:280
  211.8 1.1 copy-start.34
  212.9 0.8 copy-start.36
  218.8 1.6 copy-start.27
  220.5 25.4 %copy-start.1 = (bf16[16,32,2560]{2,1,0:T(8,128)(2,1)S(1)}, bf16[16,32,2560]{2,1,0:T(8,128)(2,1)}, u32[]{:S(2)}) copy-start(bf16[16,32,2560]{2,1,0:T(8,128)(2,1)} %copy-done) | copy-start | bytes 7864324
  245.9 6.1 %copy-start.7 = (bf16[16,32,1536]{2,1,0:T(8,128)(2,1)}, bf16[16,32,1536]{2,1,0:T(8,128)(2,1)S(1)}, u32[]{:S(2)}) copy-start(bf16[16,32,1536]{2,1,0:T(8,128)(2,1)S(1)} %shard_map.127) | copy-start | bytes 4718596
  245.9 6.0 %copy-start.37 = (bf16[128,1536]{1,0:T(8,128)(2,1)S(1)}, bf16[128,1536]{1,0:T(8,128)(2,1)}, u32[]{:S(2)}) copy-start(bf16[128,1536]{1,0:T(8,128)(2,1)} %copy-done.36) | copy-start | bytes 1179652
  250.7 1.2 copy-start.28
  278.8 24.1 %all-to-all-start.7 = ((bf16[16,8,3072]{2,1,0:T(8,128)(2,1)}), bf16[16,8,3072]{2,1,0:T(8,128)(2,1)S(1)}, u32[]{:S(2)}, u32[]{:S(2)}) async-start(bf16[16,8,3072]{2,1,0:T(8,128)(2,1)} %shard_map.129), calls=%async_computation.7 | async-start | bytes 1572864 | tf_op jit(solution)/shard_map/all_to_all | solution.py:218
  284.1 1.4 copy-start.8
  302.9 1.4 copy-start.29
  309.0 7.0 %copy-start.25 = (bf16[512,512]{1,0:T(8,128)(2,1)S(1)}, bf16[512,512]{1,0:T(8,128)(2,1)}, u32[]{:S(2)}) copy-start(bf16[512,512]{1,0:T(8,128)(2,1)} %q_ref.7) | copy-start | bytes 1572868
  309.0 7.0 %copy-start.35 = (f32[2,128,1536]{2,1,0:T(8,128)S(1)}, f32[2,128,1536]{2,1,0:T(8,128)}, u32[]{:S(2)}) copy-start(f32[2,128,1536]{2,1,0:T(8,128)} %copy-done.34) | copy-start | bytes 4718596
  311.0 41.5 %all-to-all-start.8 = ((bf16[16,32,1536]{2,1,0:T(8,128)(2,1)}), bf16[16,32,1536]{2,1,0:T(8,128)(2,1)}, u32[]{:S(2)}, u32[]{:S(2)}) async-start(bf16[16,32,1536]{2,1,0:T(8,128)(2,1)} %shard_map.133), calls=%async_computation.8 | async-start | bytes 3145728 | tf_op jit(solution)/shard_map/all_to_all | solution.py:280
  316.0 38.1 %copy-start.40 = (f32[1536]{0:T(1024)S(1)}, f32[1536]{0:T(1024)}, u32[]{:S(2)}) copy-start(f32[1536]{0:T(1024)} %copy-done.39) | copy-start | bytes 18436
  320.8 1.2 copy-start.16
  322.0 32.2 %copy-start.6 = (bf16[512,1536]{1,0:T(8,128)(2,1)S(1)}, bf16[512,1536]{1,0:T(8,128)(2,1)}, u32[]{:S(2)}) copy-start(bf16[512,1536]{1,0:T(8,128)(2,1)} %copy-done.5) | copy-start | bytes 4718596
  352.4 1.9 copy-start.17

commit v4 on v3

--- a/solution.py
+++ b/solution.py
@@ -94,7 +94,7 @@
             )
 
 
-def finish_kernel(reverse, spans, inner_ref, q_ref, decay_ref, before_ref, incoming_ref, out_ref):
+def finish_kernel(reverse, spans, inner_ref, q_ref, decay_ref, before_ref, incoming_ref, out_ref, slot_ref=None):
     pairs = inner_ref.shape[1] // LANES
     order = range(spans)
     incoming = incoming_ref[...].astype(F32)
@@ -111,7 +111,15 @@
             entering = before_ref[span] + incoming * spread_heads(jnp.exp(passed), pairs)
             passed = passed + end
         outer = jnp.dot(q_ref[rows, :], entering.astype(BF16), preferred_element_type=F32)
-        out_ref[rows, :] = (inner_ref[rows, :] + outer * spread_heads(weight, pairs)).astype(BF16)
+        total = inner_ref[rows, :] + outer * spread_heads(weight, pairs)
+        if slot_ref is None:
+            out_ref[rows, :] = total.astype(BF16)
+            continue
+        unit_rows = out_ref.shape[1]
+        per_span = SPAN // unit_rows
+        for unit in range(per_span):
+            piece = total[unit * unit_rows : (unit + 1) * unit_rows]
+            out_ref[slot_ref[span * per_span + unit]] = piece.astype(BF16)
 
 
 class Scan:
@@ -125,43 +133,62 @@
 
     def cut(self, operand, size):
         array, first = operand
-        base = first // size
-        return array, pl.BlockSpec((self.tokens, size), lambda g: (0, base + g))
-
-    def call(self, body, operands, outs, out_specs, flops):
-        arrays, specs = zip(*operands)
-        shapes = jax.tree.leaves(outs)
-        moved = sum(s.size * s.dtype.itemsize for s in shapes) * 2
+        lead = (slice(None),) * (array.ndim - 1)
+
+        def view(ref, group):
+            at = pl.multiple_of(first + group * size, LANES)
+            return ref.at[(*lead, pl.ds(at, size))]
+
+        return array, view
+
+    def decay_cut(self):
+        return self.decay, lambda ref, group: ref.at[pl.ds(group, 1)]
+
+    def call(self, body, operands, outs, flops, slots=None):
+        arrays = []
+        for array, _ in operands:
+            if not any(array is other for other in arrays):
+                arrays.append(array)
+        places = [next(i for i, other in enumerate(arrays) if other is a) for a, _ in operands]
+        out_views = [self.cut((out, 0), out.shape[-1] // self.groups)[1] for out in outs]
+
+        def kernel(*refs):
+            ins, results = refs[: len(arrays)], refs[len(refs) - len(outs) :]
+
+            @pl.loop(0, self.groups)
+            def _(group):
+                taken = [view(ins[place], group) for place, (_, view) in zip(places, operands)]
+                given = [view(ref, group) for ref, view in zip(results, out_views)]
+                extra = () if slots is None else (refs[len(arrays)],)
+                body(self.reverse, self.spans, *taken, *given, *extra)
+
+        whole = pl.BlockSpec(memory_space=pltpu.VMEM)
+        index = [] if slots is None else [slots]
         return pl.pallas_call(
-            functools.partial(body, self.reverse, self.spans),
-            grid=(self.groups,),
-            in_specs=list(specs),
-            out_specs=out_specs,
+            kernel,
+            in_specs=[whole] * len(arrays) + [pl.BlockSpec(memory_space=pltpu.SMEM)] * len(index),
+            out_specs=[whole] * len(outs),
             out_shape=outs,
             compiler_params=pltpu.CompilerParams(vmem_limit_bytes=48 * 2**20),
-            cost_estimate=pl.CostEstimate(flops=flops, bytes_accessed=moved, transcendentals=0),
-        )(*arrays)
-
-    def decay_cut(self):
-        return self.decay, pl.BlockSpec((1, PAD, self.tokens), lambda g: (g, 0, 0))
+            cost_estimate=pl.CostEstimate(
+                flops=flops, bytes_accessed=2**22, transcendentals=0
+            ),
+        )(*arrays, *index)
 
     def states(self):
-        wide = pl.BlockSpec((STATE, self.cols), lambda g: (0, g))
-        deep = pl.BlockSpec((self.spans, STATE, self.cols), lambda g: (0, 0, g))
         self.before, total = self.call(
             states_kernel,
             [self.cut(self.values, self.cols), self.cut(self.keys, STATE), self.decay_cut()],
-            (
+            [
                 jax.ShapeDtypeStruct((self.spans, STATE, self.width), F32),
                 jax.ShapeDtypeStruct((STATE, self.width), BF16),
-            ),
-            (deep, wide),
+            ],
             2 * self.tokens * STATE * self.width,
         )
         return total
 
     def inner(self):
-        self.near = self.call(
+        (self.near,) = self.call(
             inner_kernel,
             [
                 self.cut(self.values, self.cols),
@@ -169,29 +196,28 @@
                 self.cut(self.queries, STATE),
                 self.decay_cut(),
             ],
-            jax.ShapeDtypeStruct((self.tokens, self.width), F32),
-            pl.BlockSpec((self.tokens, self.cols), lambda g: (0, g)),
+            [jax.ShapeDtypeStruct((self.tokens, self.width), F32)],
             8 * self.tokens * SPAN * self.width,
         )
 
-    def finish(self, incoming, first):
-        base = first // self.cols
-        wide = pl.BlockSpec((STATE, self.cols), lambda g: (0, base + g))
-        deep = pl.BlockSpec((self.spans, STATE, self.cols), lambda g: (0, 0, g))
-        rows = pl.BlockSpec((self.tokens, self.cols), lambda g: (0, g))
-        return self.call(
+    def finish(self, incoming, first, slots=None):
+        shape = (self.tokens, self.width)
+        if slots is not None:
+            shape = (slots.shape[0], self.tokens // slots.shape[0], self.width)
+        (result,) = self.call(
             finish_kernel,
             [
-                (self.near, rows),
+                self.cut((self.near, 0), self.cols),
                 self.cut(self.queries, STATE),
                 self.decay_cut(),
-                (self.before, deep),
-                (incoming, wide),
+                self.cut((self.before, 0), self.cols),
+                self.cut((incoming, first), self.cols),
             ],
-            jax.ShapeDtypeStruct((self.tokens, self.width), BF16),
-            rows,
+            [jax.ShapeDtypeStruct(shape, BF16)],
             2 * self.tokens * STATE * self.width,
+            slots,
         )
+        return result
 
 
 def prefix_kernel(directions, arrived_ref, factor_ref, out_ref):
@@ -206,17 +232,33 @@
             run = run * factor_ref[index, :, cols] + arrived_ref[index, :, cols].astype(F32)
 
 
-def carried(totals, factors, directions):
+def carried(totals, factors, directions, sums=None):
     count = lax.axis_size("seq")
     total = jnp.concatenate(totals, axis=1)
     pieces = total.reshape(count, STATE // count, -1)
+    if sums is not None:
+        parts, rest = [], sums.reshape(-1)
+        for _ in range(3):
+            parts.append(lax.reduce_precision(rest, 8, 7))
+            rest = rest - parts[-1]
+        taken = sums.size
+        row = jnp.concatenate(parts).astype(BF16)
+        row = jnp.pad(row, (0, -row.size % LANES))
+        row = jnp.broadcast_to(row, (*pieces.shape[:2], row.size))
+        pieces = jnp.concatenate([pieces, row], axis=2)
     arrived = lax.all_to_all(pieces, "seq", split_axis=0, concat_axis=0, tiled=True)
+    if sums is not None:
+        width = total.shape[1]
+        rows = arrived[:, 0, width : width + 3 * taken].astype(F32).reshape(count, 3, taken)
+        factors = jnp.exp(jnp.sum(rows, axis=1))[:, :, None]
+        factors = jnp.broadcast_to(factors, (count, taken, HEAD_DIM)).reshape(count, 1, width)
+        arrived = arrived[:, :, :width]
     composed = pl.pallas_call(
         functools.partial(prefix_kernel, directions),
         out_shape=jax.ShapeDtypeStruct(arrived.shape, BF16),
     )(arrived, factors)
     back = lax.all_to_all(composed, "seq", split_axis=0, concat_axis=0, tiled=True)
-    return back.reshape(total.shape)
+    return back.reshape(total.shape), factors
 
 
 def gather_kernel(counts, index_ref, *refs):
@@ -270,14 +312,15 @@
     raster_dest = raster_order // unit_count
     scan_source = scan_order // unit_count
     send_scan = inverse(raster_dest)
-    send_raster = inverse(scan_source)
 
     def units(array):
         return array.reshape(unit_count, unit_rows, -1)
 
+    def swapped(outgoing):
+        return lax.all_to_all(outgoing, "seq", split_axis=0, concat_axis=0, tiled=True)
+
     def sent(arrays, send_index):
-        outgoing = gathered([units(array) for array in arrays], send_index)
-        return lax.all_to_all(outgoing, "seq", split_axis=0, concat_axis=0, tiled=True)
+        return swapped(gathered([units(array) for array in arrays], send_index))
 
     def placed(arrived, recv_index):
         return gathered([arrived], recv_index).reshape(tok_rows, -1)
@@ -287,10 +330,6 @@
         return jnp.pad(wide, ((0, 0), (0, PAD - heads // groups), (0, 0)))
 
     sums = jnp.stack([decay_forward, decay_reverse]).astype(F32).sum(axis=2)
-    copies = jnp.broadcast_to(sums[None], (lax.axis_size("seq"), *sums.shape))
-    all_sums = lax.all_to_all(copies, "seq", split_axis=0, concat_axis=0, tiled=True)
-    factors = jnp.repeat(jnp.exp(all_sums), HEAD_DIM, axis=2)
-    factors = factors.reshape(factors.shape[0], 1, 2 * width)
     decay_f, decay_r = padded(decay_forward), padded(decay_reverse)
 
     keys_at, queries_at = width, width + maps
@@ -299,14 +338,14 @@
     ahead = Scan((ssm_input, 0), (input_map, 0), (output_map, 0), decay_f, width, False)
     ahead_total = ahead.states()
     ahead.inner()
-    arrived, ahead_total, ahead.near, factors = lax.optimization_barrier(
-        (arrived, ahead_total, ahead.near, factors)
+    arrived, ahead_total, ahead.near, sums = lax.optimization_barrier(
+        (arrived, ahead_total, ahead.near, sums)
     )
     joined = placed(arrived, scan_source)
     behind = Scan((joined, 0), (joined, keys_at), (joined, queries_at), decay_r, width, True)
-    entering = carried((ahead_total, behind.states()), factors, (False, True))
+    entering, factors = carried((ahead_total, behind.states()), None, (False, True), sums)
     behind.inner()
-    y_reverse_sent = sent([behind.finish(entering, width)], send_raster)
+    y_reverse_sent = swapped(behind.finish(entering, width, scan_source))
     y_forward = ahead.finish(entering, 0)
     y_reverse = placed(y_reverse_sent, raster_dest)
 
@@ -334,9 +373,9 @@
     )
     grad_scan = placed(arrived, scan_source)
     behind_grad = Scan((grad_scan, 0), (joined, queries_at), (joined, keys_at), decay_r, width, False)
-    entering = carried((ahead_total, behind_grad.states()), factors, (True, False))
+    entering, _ = carried((ahead_total, behind_grad.states()), factors, (True, False))
     behind_grad.inner()
-    grad_reverse_sent = sent([behind_grad.finish(entering, width)], send_raster)
+    grad_reverse_sent = swapped(behind_grad.finish(entering, width, scan_source))
     grad_forward = ahead_grad.finish(entering, 0)
     grad_reverse = placed(grad_reverse_sent, raster_dest)
 

time: 358 us -> 356 us (level)
  starting transfers between devices: 39.8 us -> 32.9 us
    all_to_all x5 -> x4, starting transfers between devices: 29.2 us -> 22.5 us  [swapped(): lax.all_to_all(outgoing, 'seq', split_axis=0, concat_axis=0, tiled=True)]
    pallas_call x8 -> x6, Pallas kernels: 12.4 us -> 9.77 us  [gathered(): pl.pallas_call(functools.partial(gather_kernel, widths), in_specs=[pl.Blo...]
    all_to_all x5 -> x4, waiting for transfers between devices: 129 us -> 131 us  [swapped(): lax.all_to_all(outgoing, 'seq', split_axis=0, concat_axis=0, tiled=True)]
    unnamed x92 -> x88, local copies, waits for them, and re-layouts: 23.9 us -> 24.8 us
  transfers between devices with their start and end apart: 7 -> 6, of which waited for: 6 -> 6; matrix products, arithmetic and copies ran while one was open for 1% -> 0% of each run, Pallas kernels for 12% -> 11%
where the time goes in v4:
time: 356 us; the launch traced here: 354 us
  waiting for transfers between devices  155 us (44%)
  Pallas kernels  75.2 us (21%)
  blocking collectives  52.2 us (15%)
  starting transfers between devices  32.9 us (9%)
  local copies, waits for them, and re-layouts  28.3 us (8%)
  other arithmetic  9.92 us (3%)
    all_to_all x4, waiting for transfers between devices, swapped(): lax.all_to_all(outgoing, 'seq', split_axis=0, concat_axis=0, tiled=True)  131 us
    pallas_call x12, Pallas kernels, call(): pl.pallas_call(kernel, in_specs=[whole] * len(arrays) + [pl.BlockSpec(mem...  60.9 us
    all_to_all x2, blocking collectives, carried(): lax.all_to_all(pieces, 'seq', split_axis=0, concat_axis=0, tiled=True)  49.7 us
    unnamed x88, local copies, waits for them, and re-layouts  24.8 us
    all_to_all x2, waiting for transfers between devices, carried(): lax.all_to_all(composed, 'seq', split_axis=0, concat_axis=0, tiled=True)  23.6 us
    all_to_all x4, starting transfers between devices, swapped(): lax.all_to_all(outgoing, 'seq', split_axis=0, concat_axis=0, tiled=True)  22.5 us
    all_to_all x2, starting transfers between devices, carried(): lax.all_to_all(composed, 'seq', split_axis=0, concat_axis=0, tiled=True)  10.4 us
    pallas_call x6, Pallas kernels, gathered(): pl.pallas_call(functools.partial(gather_kernel, widths), in_specs=[pl.Blo...  9.77 us
  transfers between devices with their start and end apart: 6, of which 6 were waited for; matrix products, arithmetic and copies ran while one was open for 0% of the time, Pallas kernels for 11%

profile of v4, /device:TPU:12, one launch (start us, length us, event | category | flops | bytes accessed | tf_op | source)
XLA Modules:
  0.0 354.4 jit_solution(8201551693589381695)
XLA Ops:
  0.6 0.7 and_select_fusion.1.index_ref
  1.4 1.4 copy-done.2
  2.8 1.0 copy-done.16
  3.9 1.0 copy-done.20
  4.9 0.8 shard_map.113
  5.7 1.6 copy-done.11
  7.3 7.4 %all-to-all-start = ((bf16[16,32,2560]{2,1,0:T(8,128)(2,1)}), bf16[16,32,2560]{2,1,0:T(8,128)(2,1)}, u32[]{:S(2)}, u32[]{:S(2)}) async-start(bf16[16,32,2560]{2,1,0:T(8,128)(2,1)} %copy-done.11), calls=%async_computation | async-start | bytes 5242880 | tf_op jit(solution)/shard_map/all_to_all | solution.py:320
  14.9 4.4 %shard_map.114 = (f32[2,128,1536]{2,1,0:T(8,128)S(1)}, bf16[128,1536]{1,0:T(8,128)(2,1)S(1)}) custom-call(bf16[512,1536]{1,0:T(8,128)(2,1)S(1)} %copy-done.3, bf16[512,512]{1,0:T(8,128)(2,1)S(1)} %copy-done.21, f32[4,8,512]{2,1,0:T(8,128)S(1)} %pad_convert_fusion.1.refs_2_.refs_3_), custom_call_target="tpu_custom_call" | custom-call | flops 201326592 | bytes 4194304 | tf_op jit(solution)/shard_map/pallas_call | solution.py:167
  19.4 1.1 copy-done.31
  20.5 4.6 %shard_map.115.refs_0_ = f32[512,1536]{1,0:T(8,128)S(1)} custom-call(bf16[512,1536]{1,0:T(8,128)(2,1)S(1)} %copy-done.3, bf16[512,512]{1,0:T(8,128)(2,1)S(1)} %copy-done.21, bf16[512,512]{1,0:T(8,128)(2,1)S(1)} %copy-done.17, f32[4,8,512]{2,1,0:T(8,128)S(1)} %pad_convert_fusion.1.refs_2_.refs_3_), custom_call_target="tpu_custom_call" | custom-call | flops 1610612736 | bytes 4194304 | tf_op jit(solution)/shard_map/pallas_call | solution.py:167
  25.1 1.6 copy-done.25
  26.8 47.3 %all-to-all-done.refs_0_ = bf16[16,32,2560]{2,1,0:T(8,128)(2,1)} async-done(((bf16[16,32,2560]{2,1,0:T(8,128)(2,1)}), bf16[16,32,2560]{2,1,0:T(8,128)(2,1)}, u32[]{:S(2)}, u32[]{:S(2)}) %all-to-all-start) | async-done | bytes 2621472 | tf_op jit(solution)/shard_map/all_to_all | solution.py:320
  74.2 2.0 shard_map.116
  76.2 4.4 %shard_map.117 = (f32[2,128,1536]{2,1,0:T(8,128)S(1)}, bf16[128,1536]{1,0:T(8,128)(2,1)S(1)}) custom-call(bf16[512,2560]{1,0:T(8,128)(2,1)S(1)} %bitcast.32, f32[4,8,512]{2,1,0:T(8,128)S(1)} %pad_convert_fusion.refs_1_.refs_2_), custom_call_target="tpu_custom_call" | custom-call | flops 201326592 | bytes 4194304 | tf_op jit(solution)/shard_map/pallas_call | solution.py:167
  80.6 1.1 copy-done.27
  81.8 0.1 pad_maximum_fusion
  82.0 25.2 %all_to_all.40 = bf16[16,8,3328]{2,1,0:T(8,128)(2,1)S(1)} all-to-all(bf16[16,8,3328]{2,1,0:T(8,128)(2,1)S(1)} %pad_maximum_fusion), channel_id=1, replica_groups=mesh['seq'=16,'head'=2] {'seq'}, dimensions={0} | all-to-all | bytes 1703936 | tf_op jit(solution)/shard_map/all_to_all | solution.py:249
  107.2 0.9 copy-done.38
  108.3 0.2 broadcast_in_dim.21
  108.4 0.9 reshape.95.factor_ref
  109.3 2.1 slice.8.arrived_ref
  111.4 2.2 shard_map.118
  113.6 5.1 %all-to-all-start.2 = ((bf16[16,8,3072]{2,1,0:T(8,128)(2,1)}), bf16[16,8,3072]{2,1,0:T(8,128)(2,1)S(1)}, u32[]{:S(2)}, u32[]{:S(2)}) async-start(bf16[16,8,3072]{2,1,0:T(8,128)(2,1)} %shard_map.118), calls=%async_computation.2 | async-start | bytes 1572864 | tf_op jit(solution)/shard_map/all_to_all | solution.py:260
  118.8 4.5 %shard_map.120.refs_0_ = f32[512,1536]{1,0:T(8,128)S(1)} custom-call(bf16[512,2560]{1,0:T(8,128)(2,1)S(1)} %bitcast.33, f32[4,8,512]{2,1,0:T(8,128)S(1)} %pad_convert_fusion.refs_1_.refs_2_), custom_call_target="tpu_custom_call" | custom-call | flops 1610612736 | bytes 4194304 | tf_op jit(solution)/shard_map/pallas_call | solution.py:167
  123.3 1.7 copy-done.24
  125.0 12.4 %all-to-all-done.2 = bf16[16,8,3072]{2,1,0:T(8,128)(2,1)S(1)} async-done(((bf16[16,8,3072]{2,1,0:T(8,128)(2,1)}), bf16[16,8,3072]{2,1,0:T(8,128)(2,1)S(1)}, u32[]{:S(2)}, u32[]{:S(2)}) %all-to-all-start.2) | async-done | bytes 786464 | tf_op jit(solution)/shard_map/all_to_all | solution.py:260
  137.4 1.7 copy-done.28
  139.1 6.9 %shard_map.121 = bf16[16,32,1536]{2,1,0:T(8,128)(2,1)} custom-call(f32[512,1536]{1,0:T(8,128)} %copy-done.24, bf16[512,2560]{1,0:T(8,128)(2,1)} %bitcast.34, f32[4,8,512]{2,1,0:T(8,128)S(1)} %pad_convert_fusion.refs_1_.refs_2_, f32[2,128,1536]{2,1,0:T(8,128)S(1)} %copy-done.28, bf16[128,3072]{1,0:T(8,128)(2,1)S(1)} %bitcast.44, ...), custom_call_target="tpu_custom_call" | custom-call | flops 201326592 | bytes 4194304 | tf_op jit(solution)/shard_map/pallas_call | solution.py:167
  146.0 5.2 %all-to-all-start.3 = ((bf16[16,32,1536]{2,1,0:T(8,128)(2,1)}), bf16[16,32,1536]{2,1,0:T(8,128)(2,1)}, u32[]{:S(2)}, u32[]{:S(2)}) async-start(bf16[16,32,1536]{2,1,0:T(8,128)(2,1)} %shard_map.121), calls=%async_computation.3 | async-start | bytes 3145728 | tf_op jit(solution)/shard_map/all_to_all | solution.py:320
  151.4 1.1 copy-done.13
  152.6 1.4 copy-done.32
  154.0 4.8 %shard_map.119 = bf16[512,1536]{1,0:T(8,128)(2,1)S(1)} custom-call(f32[512,1536]{1,0:T(8,128)} %copy-done.25, bf16[512,512]{1,0:T(8,128)(2,1)S(1)} %copy-done.18, f32[4,8,512]{2,1,0:T(8,128)S(1)} %pad_convert_fusion.1.refs_2_.refs_3_, f32[2,128,1536]{2,1,0:T(8,128)S(1)} %copy-done.32, bf16[128,3072]{1,0:T(8,128)(2,1)S(1)} %bitcast.45), custom_call_target="tpu_custom_call" | custom-call | flops 201326592 | bytes 4194304 | tf_op jit(solution)/shard_map/pallas_call | solution.py:167
  158.8 28.9 %all-to-all-done.3.refs_0_ = bf16[16,32,1536]{2,1,0:T(8,128)(2,1)} async-done(((bf16[16,32,1536]{2,1,0:T(8,128)(2,1)}), bf16[16,32,1536]{2,1,0:T(8,128)(2,1)}, u32[]{:S(2)}, u32[]{:S(2)}) %all-to-all-start.3) | async-done | bytes 1572896 | tf_op jit(solution)/shard_map/all_to_all | solution.py:320
  187.6 1.7 shard_map.122
  189.4 0.1 copy-done.37
  189.5 1.5 multiply_reduce_fusion.1
  191.1 2.5 psum.7
  193.6 5.0 %subtract_convert_fusion = (bf16[512,1536]{1,0:T(8,128)(2,1)S(1)}, bf16[512,1536]{1,0:T(8,128)(2,1)}) fusion(bf16[512,1536]{1,0:T(8,128)(2,1)} %param.19, f32[512]{0:T(512)S(1)} %fusion.5, f32[512]{0:T(512)S(1)} %bitcast.51, f32[1536]{0:T(1024)S(1)} %copy-done.41, bf16[512,1536]{1,0:T(8,128)(2,1)S(1)} %copy-done.4, f32[1536]{0:T(1024)S(1)} %mul.65, ...), kind=kLoop, calls=%fused_computation.5 | loop fusion | flops 11796480 | bytes 9453568 | tf_op jit(solution)/shard_map/convert_element_type | solution.py:365
  198.6 1.9 shard_map.123
  200.5 4.6 %all-to-all-start.4 = ((bf16[16,32,1536]{2,1,0:T(8,128)(2,1)}), bf16[16,32,1536]{2,1,0:T(8,128)(2,1)}, u32[]{:S(2)}, u32[]{:S(2)}) async-start(bf16[16,32,1536]{2,1,0:T(8,128)(2,1)} %shard_map.123), calls=%async_computation.4 | async-start | bytes 3145728 | tf_op jit(solution)/shard_map/all_to_all | solution.py:320
  205.1 4.4 %shard_map.124 = (f32[2,128,1536]{2,1,0:T(8,128)S(1)}, bf16[128,1536]{1,0:T(8,128)(2,1)S(1)}) custom-call(bf16[512,1536]{1,0:T(8,128)(2,1)S(1)} %get-tuple-element.34.refs_0_, bf16[512,512]{1,0:T(8,128)(2,1)S(1)} %copy-done.19, f32[4,8,512]{2,1,0:T(8,128)S(1)} %pad_convert_fusion.1.refs_2_.refs_3_), custom_call_target="tpu_custom_call" | custom-call | flops 201326592 | bytes 4194304 | tf_op jit(solution)/shard_map/pallas_call | solution.py:167
  209.5 1.1 copy-done.33
  210.7 0.8 copy-done.35
  211.4 4.6 %shard_map.125.refs_0_ = f32[512,1536]{1,0:T(8,128)S(1)} custom-call(bf16[512,1536]{1,0:T(8,128)(2,1)S(1)} %get-tuple-element.34.refs_0_, bf16[512,512]{1,0:T(8,128)(2,1)S(1)} %copy-done.19, bf16[512,512]{1,0:T(8,128)(2,1)S(1)} %copy-done.22, f32[4,8,512]{2,1,0:T(8,128)S(1)} %pad_convert_fusion.1.refs_2_.refs_3_), custom_call_target="tpu_custom_call" | custom-call | flops 1610612736 | bytes 4194304 | tf_op jit(solution)/shard_map/pallas_call | solution.py:167
  216.0 1.6 copy-done.26
  217.7 24.7 %all-to-all-done.4.refs_0_ = bf16[16,32,1536]{2,1,0:T(8,128)(2,1)} async-done(((bf16[16,32,1536]{2,1,0:T(8,128)(2,1)}), bf16[16,32,1536]{2,1,0:T(8,128)(2,1)}, u32[]{:S(2)}, u32[]{:S(2)}) %all-to-all-start.4) | async-done | bytes 1572896 | tf_op jit(solution)/shard_map/all_to_all | solution.py:320
  242.4 1.6 shard_map.126
  244.0 4.4 %shard_map.127 = (f32[2,128,1536]{2,1,0:T(8,128)S(1)}, bf16[128,1536]{1,0:T(8,128)(2,1)S(1)}) custom-call(bf16[512,1536]{1,0:T(8,128)(2,1)S(1)} %bitcast.40, bf16[512,2560]{1,0:T(8,128)(2,1)S(1)} %bitcast.36, f32[4,8,512]{2,1,0:T(8,128)S(1)} %pad_convert_fusion.refs_1_.refs_2_), custom_call_target="tpu_custom_call" | custom-call | flops 201326592 | bytes 4194304 | tf_op jit(solution)/shard_map/pallas_call | solution.py:167
  248.5 1.2 copy-done.29
  249.7 24.5 %all_to_all.41.arrived_ref = bf16[16,8,3072]{2,1,0:T(8,128)(2,1)} all-to-all(bf16[16,8,3072]{2,1,0:T(8,128)(2,1)S(1)} %maximum_bitcast_fusion.1), channel_id=1, replica_groups=mesh['seq'=16,'head'=2] {'seq'}, dimensions={0} | all-to-all | bytes 1572864 | tf_op jit(solution)/shard_map/all_to_all | solution.py:249
  274.2 2.3 shard_map.128
  276.5 5.3 %all-to-all-start.6 = ((bf16[16,8,3072]{2,1,0:T(8,128)(2,1)}), bf16[16,8,3072]{2,1,0:T(8,128)(2,1)S(1)}, u32[]{:S(2)}, u32[]{:S(2)}) async-start(bf16[16,8,3072]{2,1,0:T(8,128)(2,1)} %shard_map.128), calls=%async_computation.6 | async-start | bytes 1572864 | tf_op jit(solution)/shard_map/all_to_all | solution.py:260
  281.8 1.4 copy-done.8
  283.2 6.3 %shard_map.130.refs_0_ = f32[512,1536]{1,0:T(8,128)} custom-call(bf16[512,1536]{1,0:T(8,128)(2,1)S(1)} %bitcast.41, bf16[512,2560]{1,0:T(8,128)(2,1)S(1)} %bitcast.37, f32[4,8,512]{2,1,0:T(8,128)S(1)} %pad_convert_fusion.refs_1_.refs_2_), custom_call_target="tpu_custom_call" | custom-call | flops 1610612736 | bytes 4194304 | tf_op jit(solution)/shard_map/pallas_call | solution.py:167
  289.4 11.2 %all-to-all-done.6 = bf16[16,8,3072]{2,1,0:T(8,128)(2,1)S(1)} async-done(((bf16[16,8,3072]{2,1,0:T(8,128)(2,1)}), bf16[16,8,3072]{2,1,0:T(8,128)(2,1)S(1)}, u32[]{:S(2)}, u32[]{:S(2)}) %all-to-all-start.6) | async-done | bytes 786464 | tf_op jit(solution)/shard_map/all_to_all | solution.py:260
  300.6 1.4 copy-done.30
  302.0 6.8 %shard_map.131 = bf16[16,32,1536]{2,1,0:T(8,128)(2,1)} custom-call(f32[512,1536]{1,0:T(8,128)} %shard_map.130.refs_0_, bf16[512,2560]{1,0:T(8,128)(2,1)} %bitcast.35, f32[4,8,512]{2,1,0:T(8,128)S(1)} %pad_convert_fusion.refs_1_.refs_2_, f32[2,128,1536]{2,1,0:T(8,128)S(1)} %copy-done.30, bf16[128,3072]{1,0:T(8,128)(2,1)S(1)} %bitcast.42, ...), custom_call_target="tpu_custom_call" | custom-call | flops 201326592 | bytes 4194304 | tf_op jit(solution)/shard_map/pallas_call | solution.py:167
  308.8 5.2 %all-to-all-start.7 = ((bf16[16,32,1536]{2,1,0:T(8,128)(2,1)}), bf16[16,32,1536]{2,1,0:T(8,128)(2,1)}, u32[]{:S(2)}, u32[]{:S(2)}) async-start(bf16[16,32,1536]{2,1,0:T(8,128)(2,1)} %shard_map.131), calls=%async_computation.7 | async-start | bytes 3145728 | tf_op jit(solution)/shard_map/all_to_all | solution.py:320
  314.0 4.9 %shard_map.129 = bf16[512,1536]{1,0:T(8,128)(2,1)S(1)} custom-call(f32[512,1536]{1,0:T(8,128)} %copy-done.26, bf16[512,512]{1,0:T(8,128)(2,1)S(1)} %copy-done.23, f32[4,8,512]{2,1,0:T(8,128)S(1)} %pad_convert_fusion.1.refs_2_.refs_3_, f32[2,128,1536]{2,1,0:T(8,128)S(1)} %copy-done.34, bf16[128,3072]{1,0:T(8,128)(2,1)S(1)} %bitcast.43), custom_call_target="tpu_custom_call" | custom-call | flops 201326592 | bytes 4194304 | tf_op jit(solution)/shard_map/pallas_call | solution.py:167
  318.9 1.2 copy-done.14
  320.1 30.3 %all-to-all-done.7.refs_0_ = bf16[16,32,1536]{2,1,0:T(8,128)(2,1)} async-done(((bf16[16,32,1536]{2,1,0:T(8,128)(2,1)}), bf16[16,32,1536]{2,1,0:T(8,128)(2,1)}, u32[]{:S(2)}, u32[]{:S(2)}) %all-to-all-start.7) | async-done | bytes 1572896 | tf_op jit(solution)/shard_map/all_to_all | solution.py:320
  350.4 1.7 shard_map.132
  352.2 0.1 copy-done.15
  352.3 2.1 fusion.1
  (89 shorter events, 1.1 us)
Async XLA Ops:
  1.4 1.4 copy-start.2
  2.8 1.0 copy-start.16
  3.9 1.0 copy-start.20
  5.7 1.6 copy-start.11
  7.3 7.5 %copy-start.40 = (bf16[24,512]{1,0:T(8,128)(2,1)S(1)}, bf16[24,512]{1,0:T(8,128)(2,1)}, u32[]{:S(2)}) copy-start(bf16[24,512]{1,0:T(8,128)(2,1)} %param.13) | copy-start | bytes 73732
  7.3 7.5 %copy-start.39 = (bf16[24,512]{1,0:T(8,128)(2,1)S(1)}, bf16[24,512]{1,0:T(8,128)(2,1)}, u32[]{:S(2)}) copy-start(bf16[24,512]{1,0:T(8,128)(2,1)} %param.14) | copy-start | bytes 73732
  7.3 7.6 %copy-start.3 = (bf16[512,1536]{1,0:T(8,128)(2,1)S(1)}, bf16[512,1536]{1,0:T(8,128)(2,1)}, u32[]{:S(2)}) copy-start(bf16[512,1536]{1,0:T(8,128)(2,1)} %refs_0_.3) | copy-start | bytes 4718596
  7.3 7.6 %copy-start.21 = (bf16[512,512]{1,0:T(8,128)(2,1)S(1)}, bf16[512,512]{1,0:T(8,128)(2,1)}, u32[]{:S(2)}) copy-start(bf16[512,512]{1,0:T(8,128)(2,1)} %refs_1_.11) | copy-start | bytes 1572868
  7.3 13.2 %copy-start.17 = (bf16[512,512]{1,0:T(8,128)(2,1)S(1)}, bf16[512,512]{1,0:T(8,128)(2,1)}, u32[]{:S(2)}) copy-start(bf16[512,512]{1,0:T(8,128)(2,1)} %refs_1_.10) | copy-start | bytes 1572868
  7.3 66.7 %all-to-all-start = ((bf16[16,32,2560]{2,1,0:T(8,128)(2,1)}), bf16[16,32,2560]{2,1,0:T(8,128)(2,1)}, u32[]{:S(2)}, u32[]{:S(2)}) async-start(bf16[16,32,2560]{2,1,0:T(8,128)(2,1)} %copy-done.11), calls=%async_computation | async-start | bytes 5242880 | tf_op jit(solution)/shard_map/all_to_all | solution.py:320
  19.4 1.1 copy-start.31
  20.5 6.2 %copy-start.43 = (s32[16]{0:T(128)S(1)}, s32[16]{0:T(128)}, u32[]{:S(2)}) copy-start(s32[16]{0:T(128)} %param.17) | copy-start | bytes 196
  25.1 1.6 copy-start.25
  76.2 42.6 %copy-start = (bf16[16,32,2560]{2,1,0:T(8,128)(2,1)}, bf16[16,32,2560]{2,1,0:T(8,128)(2,1)S(1)}, u32[]{:S(2)}) copy-start(bf16[16,32,2560]{2,1,0:T(8,128)(2,1)S(1)} %shard_map.116) | copy-start | bytes 7864324
  80.6 1.1 copy-start.27
  107.2 0.9 copy-start.38
  113.6 23.8 %all-to-all-start.2 = ((bf16[16,8,3072]{2,1,0:T(8,128)(2,1)}), bf16[16,8,3072]{2,1,0:T(8,128)(2,1)S(1)}, u32[]{:S(2)}, u32[]{:S(2)}) async-start(bf16[16,8,3072]{2,1,0:T(8,128)(2,1)} %shard_map.118), calls=%async_computation.2 | async-start | bytes 1572864 | tf_op jit(solution)/shard_map/all_to_all | solution.py:260
  123.3 1.7 copy-start.24
  137.4 8.6 %copy-start.12 = (bf16[16,8,3072]{2,1,0:T(8,128)(2,1)}, bf16[16,8,3072]{2,1,0:T(8,128)(2,1)S(1)}, u32[]{:S(2)}) copy-start(bf16[16,8,3072]{2,1,0:T(8,128)(2,1)S(1)} %all-to-all-done.2) | copy-start | bytes 2359300
  137.4 1.7 copy-start.28
  146.0 5.2 %copy-start.42 = (f32[24]{0:T(128)S(1)}, f32[24]{0:T(128)}, u32[]{:S(2)}) copy-start(f32[24]{0:T(128)} %param.15) | copy-start | bytes 292
  146.0 5.4 %copy-start.18 = (bf16[512,512]{1,0:T(8,128)(2,1)S(1)}, bf16[512,512]{1,0:T(8,128)(2,1)}, u32[]{:S(2)}) copy-start(bf16[512,512]{1,0:T(8,128)(2,1)} %refs_1_.10) | copy-start | bytes 1572868
  146.0 41.6 %all-to-all-start.3 = ((bf16[16,32,1536]{2,1,0:T(8,128)(2,1)}), bf16[16,32,1536]{2,1,0:T(8,128)(2,1)}, u32[]{:S(2)}, u32[]{:S(2)}) async-start(bf16[16,32,1536]{2,1,0:T(8,128)(2,1)} %shard_map.121), calls=%async_computation.3 | async-start | bytes 3145728 | tf_op jit(solution)/shard_map/all_to_all | solution.py:320
  151.4 1.1 copy-start.13
  152.5 1.4 copy-start.32
  154.0 35.4 %copy-start.41 = (f32[1536]{0:T(1024)S(1)}, f32[1536]{0:T(1024)}, u32[]{:S(2)}) copy-start(f32[1536]{0:T(1024)} %param.16) | copy-start | bytes 18436
  158.7 32.3 %copy-start.10 = (bf16[512,1536]{1,0:T(8,128)(2,1)}, bf16[512,1536]{1,0:T(8,128)(2,1)S(1)}, u32[]{:S(2)}) copy-start(bf16[512,1536]{1,0:T(8,128)(2,1)S(1)} %shard_map.119) | copy-start | bytes 4718596
  158.8 30.6 %copy-start.4 = (bf16[512,1536]{1,0:T(8,128)(2,1)S(1)}, bf16[512,1536]{1,0:T(8,128)(2,1)}, u32[]{:S(2)}) copy-start(bf16[512,1536]{1,0:T(8,128)(2,1)} %refs_0_.3) | copy-start | bytes 4718596
  187.6 1.9 copy-start.37
  189.5 1.5 copy-start.9
  198.5 11.0 %copy-start.5 = (bf16[512,1536]{1,0:T(8,128)(2,1)}, bf16[512,1536]{1,0:T(8,128)(2,1)S(1)}, u32[]{:S(2)}) copy-start(bf16[512,1536]{1,0:T(8,128)(2,1)S(1)} %get-tuple-element.34.refs_0_) | copy-start | bytes 4718596
  198.5 6.6 %copy-start.19 = (bf16[512,512]{1,0:T(8,128)(2,1)S(1)}, bf16[512,512]{1,0:T(8,128)(2,1)}, u32[]{:S(2)}) copy-start(bf16[512,512]{1,0:T(8,128)(2,1)} %refs_1_.10) | copy-start | bytes 1572868
  200.5 11.0 %copy-start.22 = (bf16[512,512]{1,0:T(8,128)(2,1)S(1)}, bf16[512,512]{1,0:T(8,128)(2,1)}, u32[]{:S(2)}) copy-start(bf16[512,512]{1,0:T(8,128)(2,1)} %refs_1_.11) | copy-start | bytes 1572868
  200.5 41.9 %all-to-all-start.4 = ((bf16[16,32,1536]{2,1,0:T(8,128)(2,1)}), bf16[16,32,1536]{2,1,0:T(8,128)(2,1)}, u32[]{:S(2)}, u32[]{:S(2)}) async-start(bf16[16,32,1536]{2,1,0:T(8,128)(2,1)} %shard_map.123), calls=%async_computation.4 | async-start | bytes 3145728 | tf_op jit(solution)/shard_map/all_to_all | solution.py:320
  209.5 1.1 copy-start.33
  210.7 0.8 copy-start.35
  216.0 1.6 copy-start.26
  217.6 26.4 %copy-start.1 = (bf16[16,32,2560]{2,1,0:T(8,128)(2,1)S(1)}, bf16[16,32,2560]{2,1,0:T(8,128)(2,1)}, u32[]{:S(2)}) copy-start(bf16[16,32,2560]{2,1,0:T(8,128)(2,1)} %copy-done) | copy-start | bytes 7864324
  244.0 5.7 %copy-start.7 = (bf16[16,32,1536]{2,1,0:T(8,128)(2,1)}, bf16[16,32,1536]{2,1,0:T(8,128)(2,1)S(1)}, u32[]{:S(2)}) copy-start(bf16[16,32,1536]{2,1,0:T(8,128)(2,1)S(1)} %shard_map.126) | copy-start | bytes 4718596
  244.0 5.6 %copy-start.36 = (bf16[128,1536]{1,0:T(8,128)(2,1)S(1)}, bf16[128,1536]{1,0:T(8,128)(2,1)}, u32[]{:S(2)}) copy-start(bf16[128,1536]{1,0:T(8,128)(2,1)} %copy-done.35) | copy-start | bytes 1179652
  248.4 1.2 copy-start.29
  276.5 24.1 %all-to-all-start.6 = ((bf16[16,8,3072]{2,1,0:T(8,128)(2,1)}), bf16[16,8,3072]{2,1,0:T(8,128)(2,1)S(1)}, u32[]{:S(2)}, u32[]{:S(2)}) async-start(bf16[16,8,3072]{2,1,0:T(8,128)(2,1)} %shard_map.128), calls=%async_computation.6 | async-start | bytes 1572864 | tf_op jit(solution)/shard_map/all_to_all | solution.py:260
  281.8 1.4 copy-start.8
  300.6 1.4 copy-start.30
  308.8 5.2 %copy-start.23 = (bf16[512,512]{1,0:T(8,128)(2,1)S(1)}, bf16[512,512]{1,0:T(8,128)(2,1)}, u32[]{:S(2)}) copy-start(bf16[512,512]{1,0:T(8,128)(2,1)} %refs_1_.11) | copy-start | bytes 1572868
  308.8 5.2 %copy-start.34 = (f32[2,128,1536]{2,1,0:T(8,128)S(1)}, f32[2,128,1536]{2,1,0:T(8,128)}, u32[]{:S(2)}) copy-start(f32[2,128,1536]{2,1,0:T(8,128)} %copy-done.33) | copy-start | bytes 4718596
  308.8 41.6 %all-to-all-start.7 = ((bf16[16,32,1536]{2,1,0:T(8,128)(2,1)}), bf16[16,32,1536]{2,1,0:T(8,128)(2,1)}, u32[]{:S(2)}, u32[]{:S(2)}) async-start(bf16[16,32,1536]{2,1,0:T(8,128)(2,1)} %shard_map.131), calls=%async_computation.7 | async-start | bytes 3145728 | tf_op jit(solution)/shard_map/all_to_all | solution.py:320
  318.9 1.2 copy-start.14
  320.1 32.1 %copy-start.6 = (bf16[512,1536]{1,0:T(8,128)(2,1)S(1)}, bf16[512,1536]{1,0:T(8,128)(2,1)}, u32[]{:S(2)}) copy-start(bf16[512,1536]{1,0:T(8,128)(2,1)} %copy-done.5) | copy-start | bytes 4718596
  350.4 1.9 copy-start.15
